TPU v7x, 32 devices: a whole 2x2x4 slice. The times are simulated.
32 devices in a mesh: dp: 16 (over z, y, core), tensor: 2 (over x).
Axes of the slice: x: 2, y: 2, z: 4, core: 2. Of those that a mesh axis runs over, the one named last changes fastest.
Arguments:
- stream: bfloat16 [32, 512, 1024], P('dp', 'tensor'), may hold values from -6 to 6
- lengths: int32 [32], replicated, may hold values from 64 to 512, as said below
- assignment: int32 [32], P('dp'), may hold values from 0 to 31, each once
- cotangent: bfloat16 [32, 512, 1024], P('dp', 'tensor'), may hold values from -6 to 6
- w_qkv: bfloat16 [1024, 3, 1024], P('dp', None, 'tensor'), may hold values from -0.1875 to 0.1875
- b_qv: bfloat16 [1024, 2], P(('tensor', 'dp')), may hold values from -3 to 3
- w_out: bfloat16 [1024, 1024], P(('tensor', 'dp')), may hold values from -1.5 to 1.5
- w_in: bfloat16 [1024, 4096], P('dp', 'tensor'), may hold values from -0.1875 to 0.1875
- b_in: bfloat16 [4096], P(('tensor', 'dp')), may hold values from -3 to 3
- w_back: bfloat16 [4096, 1024], P(('tensor', 'dp')), may hold values from -0.09375 to 0.09375
- gains: bfloat16 [1024, 2], P('dp'), may hold values from 0.099609375 to 1.8984375
- shifts: bfloat16 [1024, 4], P('dp'), may hold values from -3 to 3
Outputs:
- layer_out: bfloat16 [32, 512, 1024], P('dp', 'tensor')
- stream_grad: bfloat16 [32, 512, 1024], P('dp', 'tensor')
- grad_qkv: float32 [1024, 3, 1024], P('dp', None, 'tensor')
- grad_bqv: float32 [1024, 2], P(('tensor', 'dp'))
- grad_out: float32 [1024, 1024], P(('tensor', 'dp'))
- grad_in: float32 [1024, 4096], P('dp', 'tensor')
- grad_bin: float32 [4096], P(('tensor', 'dp'))
- grad_back: float32 [4096, 1024], P(('tensor', 'dp'))
- grad_gains: float32 [1024, 2], P('dp')
- grad_shifts: float32 [1024, 4], P('dp')
Inputs may be any that keep to these rules, and one draw needn't show every extreme that they name: `lengths`: at least one sequence has exactly 512 true tokens. `assignment`: each sequence is held by exactly one slot.
All inputs are finite; a program needn't handle non-finite values.
Results may differ from a plain program's by a relative error of at most 0.02.
Values may be sent and summed in bfloat16 or wider, within the bound.
No kernel may reach another device: no remote copies, remote signals or barrier semaphores. Data moves between devices by JAX's collectives and lax.ppermute only.
A program may use at most 192 MiB of HBM per device.

v0:
```python
import jax
import jax.numpy as jnp
from jax import lax
from jax.sharding import PartitionSpec as P

HD = 64


def norm_rows(summed, gain, offset):
    centred = summed - jnp.mean(summed, axis=-1, keepdims=True)
    variance = jnp.mean(centred * centred, axis=-1, keepdims=True)
    return centred * lax.rsqrt(variance + 1e-06) * gain + offset


def exact_gelu(values):
    return jax.nn.gelu(values, approximate=False)


def per_device(
    stream, lengths, assignment, cotangent, w_qkv, b_qv, w_out, w_in, b_in, w_back, gains, shifts
):
    count = jnp.sum(lengths).astype(jnp.float32)
    all_seqs = lengths.shape[0]
    matches = assignment[:, None] == jnp.arange(all_seqs, dtype=jnp.int32)[None, :]
    slot_len = jnp.sum(jnp.where(matches, lengths[None, :], 0), axis=1)
    (
        projection_weight,
        mixing_weight,
        up_weight,
        down_weight,
        bias_qv,
        bias_up,
        gain_all,
        shift_all,
    ) = (
        lax.all_gather(w_qkv, "dp", axis=0, tiled=True),
        lax.all_gather(w_out, "dp", axis=0, tiled=True),
        lax.all_gather(w_in, "dp", axis=0, tiled=True),
        lax.all_gather(w_back, "dp", axis=0, tiled=True),
        lax.all_gather(b_qv, "dp", axis=0, tiled=True),
        lax.all_gather(b_in, "dp", axis=0, tiled=True),
        lax.all_gather(gains, "dp", axis=0, tiled=True),
        lax.all_gather(shifts, "dp", axis=0, tiled=True),
    )
    seqs_dev, rows_dev, width = stream.shape
    full_rows = rows_dev * lax.axis_size("tensor")
    local_width = projection_weight.shape[2]
    shape_heads = (seqs_dev, full_rows, local_width // HD, HD)
    scale = HD ** (-0.5)
    gain_f = gain_all.astype(jnp.float32)
    shift_f = shift_all.astype(jnp.float32)
    bias_f = bias_qv.astype(jnp.float32)
    gathered_rows = lax.all_gather(stream, "tensor", axis=1, tiled=True)
    projected_rows = jnp.einsum(
        "bpo,orn->bprn", gathered_rows, projection_weight, preferred_element_type=jnp.float32
    )
    queries = (projected_rows[:, :, 0] + bias_f[:, 0]).astype(jnp.bfloat16).reshape(shape_heads)
    key_rows = projected_rows[:, :, 1].astype(jnp.bfloat16).reshape(shape_heads)
    value_rows = (projected_rows[:, :, 2] + bias_f[:, 1]).astype(jnp.bfloat16).reshape(shape_heads)
    allowed = jnp.arange(full_rows, dtype=jnp.int32)[None, :] < slot_len[:, None]
    products = jnp.einsum("sqhe,skhe->shqk", queries, key_rows, preferred_element_type=jnp.float32)
    scores = jnp.where(allowed[:, None, None, :], products * scale, -1e30)
    highest_score = jnp.max(scores, axis=-1, keepdims=True)
    expo = jnp.exp(scores - highest_score)
    weights = expo / jnp.sum(expo, axis=-1, keepdims=True)
    weights_low = weights.astype(jnp.bfloat16)
    context_rows = jnp.einsum(
        "shqk,skhe->sqhe", weights_low, value_rows, preferred_element_type=jnp.float32
    )
    context_rows = context_rows.reshape(seqs_dev, full_rows, local_width).astype(jnp.bfloat16)
    attention_terms = jnp.einsum(
        "kqz,zw->kqw", context_rows, mixing_weight, preferred_element_type=jnp.float32
    )
    attended = (
        lax.psum_scatter(
            attention_terms.astype(jnp.bfloat16), "tensor", scatter_dimension=1, tiled=True
        ).astype(jnp.float32)
        + shift_f[:, 1]
    )
    mixed, first_pull = jax.vjp(
        norm_rows, stream.astype(jnp.float32) + attended, gain_f[:, 0], shift_f[:, 0]
    )
    mixed_every_row = lax.all_gather(mixed.astype(jnp.bfloat16), "tensor", axis=1, tiled=True)
    inner = jnp.einsum(
        "vrw,wy->vry", mixed_every_row, up_weight, preferred_element_type=jnp.float32
    ) + bias_up.astype(jnp.float32)
    hidden, gelu_pull = jax.vjp(exact_gelu, inner)
    hidden_reduced = hidden.astype(jnp.bfloat16)
    perceptron_terms = jnp.einsum(
        "kqz,zw->kqw", hidden_reduced, down_weight, preferred_element_type=jnp.float32
    )
    branch = (
        lax.psum_scatter(
            perceptron_terms.astype(jnp.bfloat16), "tensor", scatter_dimension=1, tiled=True
        ).astype(jnp.float32)
        + shift_f[:, 3]
    )
    result, second_pull = jax.vjp(norm_rows, mixed + branch, gain_f[:, 1], shift_f[:, 2])
    position = lax.axis_index("tensor") * rows_dev + jnp.arange(rows_dev, dtype=jnp.int32)
    live = (position[None, :] < slot_len[:, None]).astype(jnp.float32)
    factor = jnp.float32(seqs_dev * lax.axis_size("dp") * full_rows) / count
    seed_grad = cotangent.astype(jnp.float32) * live[:, :, None] * factor
    grad_sum2, grad_gain2, grad_shift2 = second_pull(seed_grad)
    grad_branch = grad_sum2.astype(jnp.bfloat16)
    branch_bias_grad = jnp.sum(grad_branch.astype(jnp.float32), axis=(0, 1))
    branch_every_row = lax.all_gather(grad_branch, "tensor", axis=1, tiled=True)
    down_part = jnp.einsum(
        "irk,irt->kt", hidden_reduced, branch_every_row, preferred_element_type=jnp.float32
    )
    hidden_gradient = jnp.einsum(
        "atj,gj->atg", branch_every_row, down_weight, preferred_element_type=jnp.float32
    )
    inner_gradient = gelu_pull(hidden_gradient)[0].astype(jnp.bfloat16)
    up_bias_part = jnp.sum(inner_gradient.astype(jnp.float32), axis=(0, 1))
    up_portion = jnp.einsum(
        "pna,pnb->ab", mixed_every_row, inner_gradient, preferred_element_type=jnp.float32
    )
    mixed_partial_terms = jnp.einsum(
        "yjc,oc->yjo", inner_gradient, up_weight, preferred_element_type=jnp.float32
    )
    grad_mixed = grad_sum2 + lax.psum_scatter(
        mixed_partial_terms.astype(jnp.bfloat16), "tensor", scatter_dimension=1, tiled=True
    ).astype(jnp.float32)
    grad_sum1, grad_gain1, grad_shift1 = first_pull(grad_mixed)
    grad_attended = grad_sum1.astype(jnp.bfloat16)
    mix_bias_grad = jnp.sum(grad_attended.astype(jnp.float32), axis=(0, 1))
    attended_every_row = lax.all_gather(grad_attended, "tensor", axis=1, tiled=True)
    mixing_portion = jnp.einsum(
        "irk,irt->kt", context_rows, attended_every_row, preferred_element_type=jnp.float32
    )
    grad_context = jnp.einsum(
        "atj,gj->atg", attended_every_row, mixing_weight, preferred_element_type=jnp.float32
    )
    grad_context = grad_context.astype(jnp.bfloat16).reshape(shape_heads)
    grad_values = jnp.einsum(
        "shqk,sqhe->skhe", weights_low, grad_context, preferred_element_type=jnp.float32
    ).astype(jnp.bfloat16)
    grad_weights = jnp.einsum(
        "sqhe,skhe->shqk", grad_context, value_rows, preferred_element_type=jnp.float32
    )
    grad_scores = weights * (grad_weights - jnp.sum(weights * grad_weights, axis=-1, keepdims=True))
    grad_products = (grad_scores * scale).astype(jnp.bfloat16)
    grad_queries = jnp.einsum(
        "shqk,skhe->sqhe", grad_products, key_rows, preferred_element_type=jnp.float32
    ).astype(jnp.bfloat16)
    grad_keys = jnp.einsum(
        "shqk,sqhe->skhe", grad_products, queries, preferred_element_type=jnp.float32
    ).astype(jnp.bfloat16)
    flat_shape = (seqs_dev, full_rows, local_width)
    projection_gradient = jnp.stack(
        [
            grad_queries.reshape(flat_shape),
            grad_keys.reshape(flat_shape),
            grad_values.reshape(flat_shape),
        ],
        axis=2,
    )
    proj_bias_part = jnp.stack(
        [
            jnp.sum(grad_queries.astype(jnp.float32).reshape(flat_shape), axis=(0, 1)),
            jnp.sum(grad_values.astype(jnp.float32).reshape(flat_shape), axis=(0, 1)),
        ],
        axis=1,
    )
    projection_portion = jnp.einsum(
        "tqj,tquk->juk", gathered_rows, projection_gradient, preferred_element_type=jnp.float32
    )
    stream_terms = jnp.einsum(
        "wvjo,xjo->wvx", projection_gradient, projection_weight, preferred_element_type=jnp.float32
    )
    grad_stream = grad_sum1 + lax.psum_scatter(
        stream_terms.astype(jnp.bfloat16), "tensor", scatter_dimension=1, tiled=True
    ).astype(jnp.float32)
    gain_part = jnp.stack([grad_gain1, grad_gain2], axis=1)
    shift_part = jnp.stack([grad_shift1, mix_bias_grad, grad_shift2, branch_bias_grad], axis=1)
    proj_done, proj_bias_done, mix_done, up_done, up_bias_done, down_done, gain_done, shift_done = (
        lax.psum_scatter(
            projection_portion.astype(jnp.bfloat16), "dp", scatter_dimension=0, tiled=True
        ).astype(jnp.float32),
        lax.psum_scatter(
            proj_bias_part.astype(jnp.bfloat16), "dp", scatter_dimension=0, tiled=True
        ).astype(jnp.float32),
        lax.psum_scatter(
            mixing_portion.astype(jnp.bfloat16), "dp", scatter_dimension=0, tiled=True
        ).astype(jnp.float32),
        lax.psum_scatter(
            up_portion.astype(jnp.bfloat16), "dp", scatter_dimension=0, tiled=True
        ).astype(jnp.float32),
        lax.psum_scatter(
            up_bias_part.astype(jnp.bfloat16), "dp", scatter_dimension=0, tiled=True
        ).astype(jnp.float32),
        lax.psum_scatter(
            down_part.astype(jnp.bfloat16), "dp", scatter_dimension=0, tiled=True
        ).astype(jnp.float32),
        lax.psum_scatter(
            gain_part.astype(jnp.bfloat16), "dp", scatter_dimension=0, tiled=True
        ).astype(jnp.float32),
        lax.psum_scatter(
            shift_part.astype(jnp.bfloat16), "dp", scatter_dimension=0, tiled=True
        ).astype(jnp.float32),
    )
    gain_total, shift_total = lax.psum((gain_done, shift_done), "tensor")
    return (
        result.astype(jnp.bfloat16),
        grad_stream.astype(jnp.bfloat16),
        proj_done,
        proj_bias_done,
        mix_done,
        up_done,
        up_bias_done,
        down_done,
        gain_total,
        shift_total,
    )


def solution(mesh):
    in_specs = (
        P("dp", "tensor", None),
        P(),
        P("dp"),
        P("dp", "tensor", None),
        P("dp", None, "tensor"),
        P(("tensor", "dp"), None),
        P(("tensor", "dp"), None),
        P("dp", "tensor"),
        P(("tensor", "dp")),
        P(("tensor", "dp"), None),
        P("dp", None),
        P("dp", None),
    )
    out_specs = (
        P("dp", "tensor", None),
        P("dp", "tensor", None),
        P("dp", None, "tensor"),
        P(("tensor", "dp"), None),
        P(("tensor", "dp"), None),
        P("dp", "tensor"),
        P(("tensor", "dp")),
        P(("tensor", "dp"), None),
        P("dp", None),
        P("dp", None),
    )
    return jax.shard_map(
        per_device, mesh=mesh, in_specs=in_specs, out_specs=out_specs, check_vma=False
    )
```

profile of v0, /device:TPU:8, one launch (start us, length us, event | category | flops | bytes accessed | tf_op | source)
XLA Modules:
  0.0 1024.4 jit_solution(665660016362703300)
XLA Ops:
  9.4 18.9 %all-gather = bf16[16,32,2]{1,2,0:T(2,128)(2,1)S(1)} all-gather(bf16[1,32,2]{1,2,0:T(2,128)(2,1)} %bitcast.139), channel_id=1, replica_groups=mesh['dp'=16,'tensor'=2] {'dp'}, dimensions={0}, use_global_device_ids=true | all-gather | bytes 2176 | tf_op jit(solution)/shard_map/all_gather | solution.py:40
  29.5 14.3 %all-gather.13.cloned.1.call-done = bf16[2,512,1024]{2,1,0:T(8,128)(2,1)} async-done(((bf16[2,256,1024]{2,1,0:T(8,128)(2,1)}), bf16[2,512,1024]{2,1,0:T(8,128)(2,1)}) %all-gather.13.cloned.1.call-update) | async-done | bytes 2097168 | tf_op jit(solution)/shard_map/all_gather | solution.py:53
  43.9 47.8 %all-gather.15.cloned.1.call-done = bf16[1024,3,512]{2,0,1:T(8,128)(2,1)} async-done(((bf16[64,3,512]{2,0,1:T(8,128)(2,1)}), bf16[1024,3,512]{2,0,1:T(8,128)(2,1)}) %all-gather.15.cloned.1.call-update) | async-done | bytes 3145744 | tf_op jit(solution)/shard_map/all_gather | solution.py:36
  91.7 6.2 fusion.35
  99.8 12.6 %fusion.92 = (f32[2,8,512]{2,1,0:T(8,128)S(1)}, f32[2,8,512,512]{2,3,1,0:T(8,128)}) fusion(pred[2,512]{1,0:T(4,128)(4,1)S(1)} %iota_compare_fusion, bf16[2,512,8,64]{1,3,2,0:T(8,128)(2,1)S(1)} %bitcast.114, f32[2,512,8,64]{1,3,2,0:T(8,128)} %bitcast.110, f32[8,64]{1,0:T(8,128)S(1)} %add.143), kind=kOutput, calls=%fused_computation.142 | convolution fusion | flops 554697216 | bytes 19958784 | tf_op jit(solution)/shard_map/sub | solution.py:64
  112.5 7.5 fusion.62
  120.0 9.3 all-gather.17.cloned.1.call-done
  129.3 4.0 convolution_convert_fusion
  133.9 17.6 %all-gather.1 = bf16[16,64,4]{1,2,0:T(4,128)(2,1)S(1)} all-gather(bf16[1,64,4]{1,2,0:T(4,128)(2,1)S(1)} %bitcast.138), channel_id=1, replica_groups=mesh['dp'=16,'tensor'=2] {'dp'}, dimensions={0}, use_global_device_ids=true | all-gather | bytes 8704 | tf_op jit(solution)/shard_map/all_gather | solution.py:43
  151.6 17.5 %all-gather.2 = bf16[16,64,2]{1,2,0:T(2,128)(2,1)S(1)} all-gather(bf16[1,64,2]{1,2,0:T(2,128)(2,1)S(1)} %bitcast.140), channel_id=1, replica_groups=mesh['dp'=16,'tensor'=2] {'dp'}, dimensions={0}, use_global_device_ids=true | all-gather | bytes 4352 | tf_op jit(solution)/shard_map/all_gather | solution.py:42
  175.2 18.7 %all-gather.3 = bf16[16,1,128]{2,1,0:T(2,128)(2,1)S(1)} all-gather(bf16[1,1,128]{2,1,0:T(2,128)(2,1)S(1)} %bitcast.141), channel_id=1, replica_groups=mesh['dp'=16,'tensor'=2] {'dp'}, dimensions={0}, use_global_device_ids=true | all-gather | bytes 4352 | tf_op jit(solution)/shard_map/all_gather | solution.py:41
  194.0 24.0 %all-gather.21.cloned.1.call-done = bf16[1024,2048]{1,0:T(8,128)(2,1)} async-done(((bf16[64,2048]{1,0:T(8,128)(2,1)}), bf16[1024,2048]{1,0:T(8,128)(2,1)}) %all-gather.21.cloned.1.call-update) | async-done | bytes 4194320 | tf_op jit(solution)/shard_map/all_gather | solution.py:38
  218.0 33.7 %all-gather.19.cloned.1.call-done = bf16[2,512,1024]{2,1,0:T(8,128)(2,1)} async-done(((bf16[2,256,1024]{2,1,0:T(8,128)(2,1)}), bf16[2,512,1024]{2,1,0:T(8,128)(2,1)}) %all-gather.19.cloned.1.call-update) | async-done | bytes 2097168 | tf_op jit(solution)/shard_map/all_gather | solution.py:83
  251.7 10.1 fusion.42
  261.8 3.2 copy-done.6
  265.0 20.7 %multiply_convert_fusion.1 = (bf16[2,512,2048]{2,1,0:T(8,128)(2,1)}, f32[2,512,2048]{2,1,0:T(8,128)}) fusion(f32[2,512,2048]{2,1,0:T(8,128)S(1)} %get-tuple-element.95, f32[2048]{0:T(1024)S(1)} %bitcast.134, u8[512,2048]{1,0:T(8,128)(4,1)S(1)} %get-tuple-element.61, u8[512,2048]{1,0:T(8,128)(4,1)S(1)} %get-tuple-element.60), kind=kLoop, calls=%fused_computation.18 | loop fusion | flops 148897792 | bytes 23076864 | tf_op jit(solution)/shard_map/convert_element_type | solution.py:88
  285.8 18.9 %all-gather.23.cloned.1.call-done = bf16[2048,1024]{1,0:T(8,128)(2,1)} async-done(((bf16[128,1024]{1,0:T(8,128)(2,1)}), bf16[2048,1024]{1,0:T(8,128)(2,1)}) %all-gather.23.cloned.1.call-update) | async-done | bytes 4194320 | tf_op jit(solution)/shard_map/all_gather | solution.py:39
  304.7 9.3 fusion.48
  315.7 28.8 %reduce-scatter.19.cloned.1.call-done = bf16[2,256,1024]{2,1,0:T(8,128)(2,1)} async-done(((bf16[2,512,1024]{2,1,0:T(8,128)(2,1)}), bf16[2,256,1024]{2,1,0:T(8,128)(2,1)}) %reduce-scatter.19.cloned.1.call-update) | async-done | bytes 1048592 | tf_op jit(solution)/shard_map/reduce_scatter | solution.py:93
  344.5 2.2 fusion.87
  348.2 2.1 fusion.86
  352.9 33.2 %all-gather.25.cloned.1.call-done = bf16[2,512,1024]{2,1,0:T(8,128)(2,1)} async-done(((bf16[2,256,1024]{2,1,0:T(8,128)(2,1)}), bf16[2,512,1024]{2,1,0:T(8,128)(2,1)}) %all-gather.25.cloned.1.call-update) | async-done | bytes 2097168 | tf_op jit(solution)/shard_map/all_gather | solution.py:106
  386.1 13.4 %fusion.95 = (bf16[2048]{0:T(1024)(128)(2,1)S(1)}, bf16[2,512,2048]{2,1,0:T(8,128)(2,1)S(1)}) fusion(f32[2,512,2048]{2,1,0:T(8,128)} %get-tuple-element.83, bf16[2,512,1024]{2,1,0:T(8,128)(2,1)} %all-gather.25.cloned.1.call-done, bf16[2048,1024]{1,0:T(8,128)(2,1)} %all-gather.23.cloned.1.call-done, f32[2,512,2048]{2,1,0:T(8,128)} %copy-done.6, ...), kind=kOutput, calls=%fused_computation.143 | convolution fusion | flops 4328519680 | bytes 27275264 | tf_op jit(solution)/shard_map/atj,gj->atg/dot_general | solution.py:110
  401.5 5.8 fusion.45
  407.7 31.5 %reduce-scatter.21.cloned.1.call-done = bf16[2,256,1024]{2,1,0:T(8,128)(2,1)} async-done(((bf16[2,512,1024]{2,1,0:T(8,128)(2,1)}), bf16[2,256,1024]{2,1,0:T(8,128)(2,1)}) %reduce-scatter.21.cloned.1.call-update) | async-done | bytes 1048592 | tf_op jit(solution)/shard_map/reduce_scatter | solution.py:121
  439.2 3.4 multiply_reduce_fusion.2
  448.5 8.4 bitcast_convert_fusion.1
  458.5 8.4 bitcast_convert_fusion
  467.1 12.6 %all-gather.27.cloned.1.call-done = bf16[2,512,1024]{2,1,0:T(8,128)(2,1)} async-done(((bf16[2,256,1024]{2,1,0:T(8,128)(2,1)}), bf16[2,512,1024]{2,1,0:T(8,128)(2,1)}) %all-gather.27.cloned.1.call-update) | async-done | bytes 2097168 | tf_op jit(solution)/shard_map/all_gather | solution.py:127
  479.7 2.9 convolution_convert_fusion.1
  482.6 9.6 bitcast_reduce_fusion
  492.1 2.3 copy.91
  494.4 8.4 fusion.70
  502.8 23.2 %fusion.59 = bf16[2,8,64,512]{3,2,1,0:T(8,128)(2,1)S(1)} fusion(f32[2,8,512,512]{2,3,1,0:T(8,128)} %fusion.70, f32[2,8,512,512]{2,3,1,0:T(8,128)} %get-tuple-element.94, f32[2,8,512]{2,1,0:T(8,128)S(1)} %get-tuple-element.93, f32[2,512,8,64]{1,3,2,0:T(8,128)} %bitcast.111, f32[8,64]{1,0:T(8,128)S(1)} %add.143), kind=kOutput, calls=%fused_computation.91 | convolution fusion | flops 567812608 | bytes 36734976 | tf_op jit(solution)/shard_map/shqk,sqhe->skhe/dot_general | solution.py:146
  527.3 22.3 %bitcast_reduce_fusion.1 = (bf16[8,64]{1,0:T(8,128)(2,1)S(1)}, bf16[2,8,64,512]{3,2,1,0:T(8,128)(2,1)S(1)}) fusion(bf16[2,512,8,64]{1,3,2,0:T(8,128)(2,1)S(1)} %bitcast.115, f32[2,8,512,512]{2,3,1,0:T(8,128)} %fusion.70, f32[2,8,512,512]{2,3,1,0:T(8,128)} %get-tuple-element.94, f32[2,8,512]{2,1,0:T(8,128)S(1)} %get-tuple-element.93), kind=kOutput, calls=%fused_computation.96 | convolution fusion | flops 567287808 | bytes 35685376 | tf_op jit(solution)/shard_map/shqk,skhe->sqhe/dot_general | solution.py:143
  552.2 6.1 fusion.32
  558.3 5.8 copy.93
  564.2 4.3 bitcast_convert_fusion.4
  568.6 6.6 bitcast_convert_fusion.3
  577.2 25.3 %all-reduce.1 = bf16[2048]{0:T(1024)(128)(2,1)S(1)} all-reduce(bf16[2048]{0:T(1024)(128)(2,1)S(1)} %get-tuple-element.100), channel_id=10, replica_groups=mesh['dp'=16,'tensor'=2] {'dp'}, use_global_device_ids=true, to_apply=%region_24.25.clone | all-reduce | flops 2048 | bytes 8192
  604.6 5.5 all-reduce.2
  610.1 63.1 %reduce-scatter.27.cloned.1.call-done = bf16[64,2048]{1,0:T(8,128)(2,1)} async-done(((bf16[1024,2048]{1,0:T(8,128)(2,1)}), bf16[64,2048]{1,0:T(8,128)(2,1)}) %reduce-scatter.27.cloned.1.call-update) | async-done | bytes 262160 | tf_op jit(solution)/shard_map/reduce_scatter | solution.py:186
  675.1 73.5 %reduce-scatter.29.cloned.1.call-done = bf16[128,1024]{1,0:T(8,128)(2,1)} async-done(((bf16[2048,1024]{1,0:T(8,128)(2,1)}), bf16[128,1024]{1,0:T(8,128)(2,1)}) %reduce-scatter.29.cloned.1.call-update) | async-done | bytes 262160 | tf_op jit(solution)/shard_map/reduce_scatter | solution.py:192
  750.3 57.2 %reduce-scatter.31.cloned.1.call-done = bf16[32,2]{1,0:T(8,128)(2,1)} async-done(((bf16[512,2]{1,0:T(8,128)(2,1)}), bf16[32,2]{1,0:T(8,128)(2,1)}) %reduce-scatter.31.cloned.1.call-update) | async-done | bytes 144
  808.9 112.9 %all-reduce.5.cloned.1.call-done = bf16[1024,3,512]{2,1,0:T(4,128)(2,1)} async-done(((bf16[1024,3,512]{2,1,0:T(4,128)(2,1)}), bf16[1024,3,512]{2,1,0:T(4,128)(2,1)}) %all-reduce.5.cloned.1.call-update) | async-done | bytes 3145744
  923.6 58.1 %reduce-scatter.25.cloned.1.call-done = bf16[32,1024]{1,0:T(8,128)(2,1)} async-done(((bf16[512,1024]{1,0:T(8,128)(2,1)}), bf16[32,1024]{1,0:T(8,128)(2,1)}) %reduce-scatter.25.cloned.1.call-update) | async-done | bytes 65552 | tf_op jit(solution)/shard_map/reduce_scatter | solution.py:183
  983.3 31.8 %reduce-scatter.23.cloned.1.call-done = bf16[2,256,1024]{2,1,0:T(8,128)(2,1)} async-done(((bf16[2,512,1024]{2,1,0:T(8,128)(2,1)}), bf16[2,256,1024]{2,1,0:T(8,128)(2,1)}) %reduce-scatter.23.cloned.1.call-update) | async-done | bytes 1048592 | tf_op jit(solution)/shard_map/reduce_scatter | solution.py:171
  1015.1 2.5 add_convert_fusion.1
  (156 shorter events, 42.3 us)
Async XLA Ops:
  7.2 36.7 %all-gather.13.cloned.1.call-start = ((), (), s32[]{:S(2)}) async-start(), calls=%async_computation.10 | async-start | bytes 3145728 | tf_op jit(solution)/shard_map/all_gather | solution.py:53
  7.9 83.8 %all-gather.15.cloned.1.call-start = ((), (), s32[]{:S(2)}) async-start(), calls=%async_computation.11 | async-start | bytes 3342336 | tf_op jit(solution)/shard_map/all_gather | solution.py:36
  8.7 120.6 %all-gather.17.cloned.1.call-start = ((), (), s32[]{:S(2)}) async-start(), calls=%async_computation.12 | async-start | bytes 1114112 | tf_op jit(solution)/shard_map/all_gather | solution.py:37
  9.4 159.8 %reduce-scatter.17.cloned.1.call-start = ((), (), s32[]{:S(2)}) async-start(), calls=%async_computation.13 | async-start | bytes 3145728 | tf_op jit(solution)/shard_map/reduce_scatter | solution.py:75
  99.7 12.8 %copy-start.7 = (f32[2,512,1,512]{1,3,2,0:T(8,128)}, f32[2,512,1,512]{1,3,2,0:T(8,128)S(1)}, u32[]{:S(2)}) copy-start(f32[2,512,1,512]{1,3,2,0:T(8,128)S(1)} %get-tuple-element.85) | copy-start | bytes 6291460
  99.8 12.6 %copy-start.11 = (bf16[2,512,1,512]{1,3,2,0:T(8,128)(2,1)}, bf16[2,512,1,512]{1,3,2,0:T(8,128)(2,1)S(1)}, u32[]{:S(2)}) copy-start(bf16[2,512,1,512]{1,3,2,0:T(8,128)(2,1)S(1)} %slice.59) | copy-start | bytes 3145732
  120.0 31.5 %copy-start.24 = (bf16[2,8,64,512]{3,2,1,0:T(8,128)(2,1)}, bf16[2,8,64,512]{3,2,1,0:T(8,128)(2,1)S(1)}, u32[]{:S(2)}) copy-start(bf16[2,8,64,512]{3,2,1,0:T(8,128)(2,1)S(1)} %fusion.62) | copy-start | bytes 3145732
  120.0 13.9 %copy-start.16 = (bf16[64,4]{0,1:T(4,128)(2,1)S(1)}, bf16[64,4]{0,1:T(4,128)(2,1)}, u32[]{:S(2)}) copy-start(bf16[64,4]{0,1:T(4,128)(2,1)} %param.23) | copy-start | bytes 1540
  129.3 22.3 %copy-start.17 = (bf16[64,2]{0,1:T(2,128)(2,1)S(1)}, bf16[64,2]{0,1:T(2,128)(2,1)}, u32[]{:S(2)}) copy-start(bf16[64,2]{0,1:T(2,128)(2,1)} %param.22) | copy-start | bytes 772
  129.3 40.0 %copy-start = (bf16[2,256,1024]{2,1,0:T(8,128)(2,1)S(1)}, bf16[2,256,1024]{2,1,0:T(8,128)(2,1)}, u32[]{:S(2)}) copy-start(bf16[2,256,1024]{2,1,0:T(8,128)(2,1)} %param.12) | copy-start | bytes 3145732
  133.3 84.7 %all-gather.21.cloned.1.call-start = ((), (), s32[]{:S(2)}) async-start(), calls=%async_computation.15 | async-start | bytes 4456448 | tf_op jit(solution)/shard_map/all_gather | solution.py:38
  133.9 117.8 %all-gather.19.cloned.1.call-start = ((), (), s32[]{:S(2)}) async-start(), calls=%async_computation.14 | async-start | bytes 3145728 | tf_op jit(solution)/shard_map/all_gather | solution.py:83
  169.2 3.6 copy-start.1
  169.3 5.9 copy-start.18
  174.4 130.3 %all-gather.23.cloned.1.call-start = ((), (), s32[]{:S(2)}) async-start(), calls=%async_computation.16 | async-start | bytes 4456448 | tf_op jit(solution)/shard_map/all_gather | solution.py:39
  175.2 169.3 %reduce-scatter.19.cloned.1.call-start = ((), (), s32[]{:S(2)}) async-start(), calls=%async_computation.17 | async-start | bytes 3145728 | tf_op jit(solution)/shard_map/reduce_scatter | solution.py:93
  261.8 3.2 copy-start.6
  304.7 9.6 copy-start.23
  314.0 33.0 %copy-start.9 = (bf16[2,256,1024]{2,1,0:T(8,128)(2,1)S(1)}, bf16[2,256,1024]{2,1,0:T(8,128)(2,1)}, u32[]{:S(2)}) copy-start(bf16[2,256,1024]{2,1,0:T(8,128)(2,1)} %param.15) | copy-start | bytes 3145732
  314.1 72.1 %all-gather.25.cloned.1.call-start = ((), (), s32[]{:S(2)}) async-start(), calls=%async_computation.18 | async-start | bytes 3145728 | tf_op jit(solution)/shard_map/all_gather | solution.py:106
  350.2 1.4 copy-start.2
  352.8 86.4 %reduce-scatter.21.cloned.1.call-start = ((), (), s32[]{:S(2)}) async-start(), calls=%async_computation.19 | async-start | bytes 3145728 | tf_op jit(solution)/shard_map/reduce_scatter | solution.py:121
  386.1 15.3 %copy-start.19 = (bf16[1024,2048]{1,0:T(8,128)(2,1)S(1)}, bf16[1024,2048]{1,0:T(8,128)(2,1)}, u32[]{:S(2)}) copy-start(bf16[1024,2048]{1,0:T(8,128)(2,1)} %all-gather.21.cloned.1.call-done) | copy-start | bytes 12582916
  399.5 1.9 copy-start.26
  407.3 72.4 %all-gather.27.cloned.1.call-start = ((), (), s32[]{:S(2)}) async-start(), calls=%async_computation.20 | async-start | bytes 3145728 | tf_op jit(solution)/shard_map/all_gather | solution.py:127
  439.2 3.4 copy-start.3
  439.2 3.4 copy-start.10
  443.8 1.4 copy-start.4
  443.8 4.7 copy-start.20
  446.4 156.6 %reduce-scatter.33.cloned.1.call-start = ((), (), s32[]{:S(2)}) async-start(), calls=%async_computation.26 | async-start | bytes 278528
  447.5 156.4 %reduce-scatter.35.cloned.1.call-start = ((), (), s32[]{:S(2)}) async-start(), calls=%async_computation.27 | async-start | bytes 278528
  448.4 224.8 %reduce-scatter.27.cloned.1.call-start = ((), (), s32[]{:S(2)}) async-start(), calls=%async_computation.23 | async-start | bytes 4456448 | tf_op jit(solution)/shard_map/reduce_scatter | solution.py:186
  456.9 1.6 copy-start.21
  456.9 291.6 %reduce-scatter.29.cloned.1.call-start = ((), (), s32[]{:S(2)}) async-start(), calls=%async_computation.24 | async-start | bytes 4456448 | tf_op jit(solution)/shard_map/reduce_scatter | solution.py:192
  466.9 12.8 %copy-start.22 = (bf16[512,1024]{1,0:T(8,128)(2,1)S(1)}, bf16[512,1024]{1,0:T(8,128)(2,1)}, u32[]{:S(2)}) copy-start(bf16[512,1024]{1,0:T(8,128)(2,1)} %all-gather.17.cloned.1.call-done) | copy-start | bytes 3145732
  466.9 340.6 %reduce-scatter.31.cloned.1.call-start = ((), (), s32[]{:S(2)}) async-start(), calls=%async_computation.25 | async-start | bytes 139264
  482.6 11.8 %copy-start.8 = (f32[2,512,1,512]{1,3,2,0:T(8,128)S(1)}, f32[2,512,1,512]{1,3,2,0:T(8,128)}, u32[]{:S(2)}) copy-start(f32[2,512,1,512]{1,3,2,0:T(8,128)} %copy-done.7) | copy-start | bytes 6291460
  502.8 24.5 %copy-start.12 = (bf16[2,512,1,512]{1,3,2,0:T(8,128)(2,1)S(1)}, bf16[2,512,1,512]{1,3,2,0:T(8,128)(2,1)}, u32[]{:S(2)}) copy-start(bf16[2,512,1,512]{1,3,2,0:T(8,128)(2,1)} %copy-done.11) | copy-start | bytes 3145732
  552.0 369.8 %all-reduce.5.cloned.1.call-start = ((), (), s32[]{:S(2)}) async-start(), calls=%async_computation.28 | async-start | bytes 8388608
  564.1 4.5 copy-start.13
  564.1 4.5 copy-start.14
  564.1 4.5 copy-start.15
  564.1 417.7 %reduce-scatter.25.cloned.1.call-start = ((), (), s32[]{:S(2)}) async-start(), calls=%async_computation.22 | async-start | bytes 1114112 | tf_op jit(solution)/shard_map/reduce_scatter | solution.py:183
  568.5 6.8 copy-start.25
  568.5 446.6 %reduce-scatter.23.cloned.1.call-start = ((), (), s32[]{:S(2)}) async-start(), calls=%async_computation.21 | async-start | bytes 3145728 | tf_op jit(solution)/shard_map/reduce_scatter | solution.py:171
  575.2 439.9 %copy-start.5 = (f32[2,256,1024]{2,1,0:T(8,128)S(1)}, f32[2,256,1024]{2,1,0:T(8,128)}, u32[]{:S(2)}) copy-start(f32[2,256,1024]{2,1,0:T(8,128)} %copy-done.4) | copy-start | bytes 6291460
Sparse Core Ops, SparseCore 0:
  9.6 34.2 all-gather.12
  46.0 45.6 all-gather.14
  93.9 35.3 all-gather.16
  133.4 31.6 reduce-scatter.16
  167.4 50.5 all-gather.20
  220.1 31.5 all-gather.18
  254.1 50.5 all-gather.22
  314.2 30.2 reduce-scatter.18
  353.0 33.1 all-gather.24
  407.4 31.8 reduce-scatter.20
  446.5 33.1 all-gather.26
  484.0 55.2 reduce-scatter.32
  543.8 54.3 reduce-scatter.34
  602.4 70.8 reduce-scatter.26
  677.0 71.5 reduce-scatter.28
  752.8 54.6 reduce-scatter.30
  811.5 110.2 all-reduce.4
  925.3 56.4 reduce-scatter.24
  984.1 30.9 reduce-scatter.22
where the time goes:
time: 1030 us; the launch traced here: 1020 us
  waiting for transfers between devices  654 us (63%)
  matrix products  169 us (16%)
  blocking collectives  103 us (10%)
  other arithmetic  50 us (5%)
  local copies, waits for them, and re-layouts  29.1 us (3%)
  between operations  16.7 us (2%)
    unnamed x23, waiting for transfers between devices  174 us
    reduce_scatter x1, waiting for transfers between devices, per_device(): lax.psum_scatter(down_part.astype(jnp.bfloat16), 'dp', scatter_dimension=...  73.5 us
    reduce_scatter x1, waiting for transfers between devices, per_device(): lax.psum_scatter(up_portion.astype(jnp.bfloat16), 'dp', scatter_dimension...  63.1 us
    reduce_scatter x1, waiting for transfers between devices, per_device(): lax.psum_scatter(mixing_portion.astype(jnp.bfloat16), 'dp', scatter_dimen...  58.1 us
    all_gather x1, waiting for transfers between devices, per_device(): lax.all_gather(w_qkv, 'dp', axis=0, tiled=True)  47.8 us
    all_gather x1, waiting for transfers between devices, per_device(): lax.all_gather(mixed.astype(jnp.bfloat16), 'tensor', axis=1, tiled=True)  33.7 us
    all_gather x1, waiting for transfers between devices, per_device(): branch_every_row = lax.all_gather(grad_branch, 'tensor', axis=1, tiled=True)  33.2 us
    reduce_scatter x1, waiting for transfers between devices, per_device(): lax.psum_scatter(stream_terms.astype(jnp.bfloat16), 'tensor', scatter_dim...  31.8 us
  transfers between devices with their start and end apart: 19, of which 16 were waited for; matrix products, arithmetic and copies ran while one was open for 19% of the time, Pallas kernels for 0%

commit v1 on v0

--- a/solution.py
+++ b/solution.py
@@ -1,9 +1,16 @@
+import functools
+
 import jax
 import jax.numpy as jnp
 from jax import lax
+from jax.experimental import pallas as pl
+from jax.experimental.pallas import tpu as pltpu
 from jax.sharding import PartitionSpec as P
 
 HD = 64
+BF = jnp.bfloat16
+F32 = jnp.float32
+VMEM = 56 * 1024 * 1024
 
 
 def norm_rows(summed, gain, offset):
@@ -214,6 +221,827 @@
     )
 
 
+def kernel(body, name, grid, in_specs, out_specs, out_shape, args, *, scratch=(), prefetch=0, deps=()):
+    inputs = prefetch + len(in_specs)
+
+    def without_deps(*refs):
+        body(*refs[:inputs], *refs[inputs + len(deps) :])
+
+    return pl.pallas_call(
+        without_deps,
+        grid_spec=pltpu.PrefetchScalarGridSpec(
+            num_scalar_prefetch=prefetch,
+            grid=grid,
+            in_specs=list(in_specs) + [pl.BlockSpec(memory_space=pl.ANY)] * len(deps),
+            out_specs=out_specs,
+            scratch_shapes=scratch,
+        ),
+        out_shape=out_shape,
+        compiler_params=pltpu.CompilerParams(vmem_limit_bytes=VMEM),
+        name=name,
+    )(*args, *deps)
+
+
+def gelu_terms(v):
+    density = jnp.exp(v * v * -0.5)
+    t = 1.0 / (1.0 + (0.3275911 * 0.7071067811865476) * jnp.abs(v))
+    poly = t * (
+        0.254829592
+        + t * (-0.284496736 + t * (1.421413741 + t * (-1.453152027 + t * 1.061405429)))
+    )
+    tail = 0.5 * poly * density
+    return jnp.where(v >= 0, 1.0 - tail, tail), density * 0.3989422804014327
+
+
+def dot(a, b, dims=((1,), (0,))):
+    return lax.dot_general(a, b, (dims, ((), ())), preferred_element_type=F32)
+
+
+def project_body(a_ref, w00, w10, w01, w11, b_ref, o_ref, *, half):
+    j = pl.program_id(0)
+    k = w00.shape[0]
+
+    def go(w0, w1):
+        acc = dot(a_ref[:, :k], w0[...]) + dot(a_ref[:, k:], w1[...]) + b_ref[...]
+        o_ref[...] = acc.astype(o_ref.dtype)
+
+    @pl.when(j < half)
+    def _():
+        go(w00, w10)
+
+    @pl.when(j >= half)
+    def _():
+        go(w01, w11)
+
+
+def split_specs(rows, block, half):
+    low = pl.BlockSpec((rows, block), lambda j, *_: (0, jnp.minimum(j, half - 1)))
+    high = pl.BlockSpec((rows, block), lambda j, *_: (0, jnp.maximum(j - half, 0)))
+    return [low, low, high, high]
+
+
+def project(a, w, bias, block, deps=()):
+    rows, width = a.shape
+    cols = w[0][0].shape[1]
+    half = cols // block
+    return kernel(
+        functools.partial(project_body, half=half),
+        "project",
+        (2 * half,),
+        [pl.BlockSpec((rows, width), lambda j: (0, 0))]
+        + split_specs(width // 2, block, half)
+        + [pl.BlockSpec((1, block), lambda j: (0, j))],
+        pl.BlockSpec((rows, block), lambda j: (0, j)),
+        jax.ShapeDtypeStruct((rows, 2 * cols), BF),
+        (a, w[0][0], w[1][0], w[0][1], w[1][1], bias,),
+        deps=deps,
+    )
+
+
+def up_body(place, a_ref, w00, w10, w01, w11, b_ref, h_ref, g_ref, acc, *, half):
+    j = pl.program_id(0)
+    k = w00.shape[0]
+
+    def go(w0, w1):
+        new = dot(a_ref[:, :k], w0[...]) + dot(a_ref[:, k:], w1[...])
+        v = acc[...]
+        cdf, density = gelu_terms(v)
+        h_ref[...] = (v * cdf).astype(BF)
+        g_ref[...] = (cdf + v * density).astype(BF)
+        acc[...] = new + b_ref[...]
+
+    @pl.when(j < half)
+    def _():
+        go(w00, w10)
+
+    @pl.when(j >= half)
+    def _():
+        go(w01, w11)
+
+
+def up_gelu(a, w, bias, place, block, deps=()):
+    rows, width = a.shape
+    cols = w[0][0].shape[1]
+    half = cols // block
+    end = 2 * half - 1
+    out = jax.ShapeDtypeStruct((rows, 2 * cols), BF)
+
+    def where(j, place):
+        j = jnp.maximum(j - 1, 0)
+        return (0, (j + place[0] * half) % (2 * half))
+
+    spot = pl.BlockSpec((rows, block), where)
+    low = pl.BlockSpec((width // 2, block), lambda j, place: (0, jnp.minimum(j, half - 1)))
+    high = pl.BlockSpec((width // 2, block), lambda j, place: (0, jnp.clip(j - half, 0, half - 1)))
+    return kernel(
+        functools.partial(up_body, half=half),
+        "up_gelu",
+        (2 * half + 1,),
+        [pl.BlockSpec((rows, width), lambda j, place: (0, 0))]
+            + [low, low, high, high]
+            + [pl.BlockSpec((1, block), lambda j, place: (0, jnp.minimum(j, end)))],
+        [spot, spot],
+        [out, out],
+        (place, a, w[0][0], w[1][0], w[0][1], w[1][1], bias,),
+        scratch=[pltpu.VMEM((rows, block), F32)],
+        prefetch=1,
+        deps=deps,
+    )
+
+
+def down_grad_body(place, a_ref, w_ref, g_ref, d_ref, s_ref):
+    d = dot(a_ref[...], w_ref[...], ((1,), (1,)))
+    d = (d * g_ref[...].astype(F32)).astype(BF)
+    d_ref[...] = d
+    s_ref[...] = jnp.sum(d.astype(F32), axis=0, keepdims=True)
+
+
+def down_grad(a, w, g, place, block, part, deps=()):
+    rows, width = a.shape
+    cols = g.shape[1] // 2
+    steps = cols // block
+
+    def at(j, place):
+        return (j + (place[0] ^ part) * steps)
+
+    return kernel(
+        down_grad_body,
+        "down_grad",
+        (steps,),
+        [
+                pl.BlockSpec((rows, width), lambda j, place: (0, 0)),
+                pl.BlockSpec((block, width), lambda j, place: (at(j, place), 0)),
+                pl.BlockSpec((rows, block), lambda j, place: (0, at(j, place))),
+            ],
+        [
+                pl.BlockSpec((rows, block), lambda j, place: (0, j)),
+                pl.BlockSpec((1, block), lambda j, place: (0, j)),
+            ],
+        [
+            jax.ShapeDtypeStruct((rows, cols), BF),
+            jax.ShapeDtypeStruct((1, cols), F32),
+        ],
+        (place, a, w, g,),
+        prefetch=1,
+        deps=deps,
+    )
+
+
+def head_weights(info, q, k, rows):
+    own = rows // 2
+    at = lax.broadcasted_iota(jnp.int32, (1, rows), 1)
+    first = info[1] * own
+    pos = jnp.where(at < own, at + first, at - first)
+    s = dot(q, k, ((1,), (1,)))
+    s = jnp.where(pos < info[0], s * HD ** (-0.5), -1e30)
+    e = jnp.exp(s - jnp.max(s, axis=1, keepdims=True))
+    return e * (1.0 / jnp.sum(e, axis=1, keepdims=True))
+
+
+def attend_body(info, p_ref, c_ref):
+    rows, lanes = c_ref.shape
+    for h in range(lanes // HD):
+        part = [p_ref[:, j * lanes + h * HD : j * lanes + (h + 1) * HD] for j in range(3)]
+        w = head_weights(info, part[0], part[1], rows).astype(BF)
+        c_ref[:, h * HD : (h + 1) * HD] = dot(w, part[2]).astype(BF)
+
+
+def attend_grad_body(info, p_ref, t_ref, d_ref, s_ref):
+    rows, lanes = t_ref.shape
+    tn = ((0,), (0,))
+    for h in range(lanes // HD):
+        q, k, v = [p_ref[:, j * lanes + h * HD : j * lanes + (h + 1) * HD] for j in range(3)]
+        t = t_ref[:, h * HD : (h + 1) * HD]
+        w = head_weights(info, q, k, rows)
+        dw = dot(t, v, ((1,), (1,)))
+        ds = w * (dw - jnp.sum(w * dw, axis=1, keepdims=True)) * HD ** (-0.5)
+        ds = ds.astype(BF)
+        outs = (dot(ds, k), dot(ds, q, tn), dot(w.astype(BF), t, tn))
+        for j in range(3):
+            at = slice(j * lanes + h * HD, j * lanes + (h + 1) * HD)
+            low = outs[j].astype(BF)
+            d_ref[:, at] = low
+            s_ref[:, at] = jnp.sum(low.astype(F32), axis=0, keepdims=True)
+
+
+def attend(info, proj, lanes, part, deps=()):
+    rows, cols = proj.shape
+    steps = cols // (6 * lanes)
+    return kernel(
+        attend_body,
+        "attend",
+        (steps,),
+        [pl.BlockSpec((rows, 3 * lanes), lambda j, info: (0, j + part * steps))],
+        pl.BlockSpec((rows, lanes), lambda j, info: (0, j)),
+        jax.ShapeDtypeStruct((rows, cols // 6), BF),
+        (info, proj,),
+        prefetch=1,
+        deps=deps,
+    )
+
+
+def attend_grad(info, proj, top, lanes, part, deps=()):
+    rows, cols = proj.shape
+    steps = cols // (6 * lanes)
+    return kernel(
+        attend_grad_body,
+        "attend_grad",
+        (steps,),
+        [
+                pl.BlockSpec((rows, 3 * lanes), lambda j, info: (0, j + part * steps)),
+                pl.BlockSpec((rows, lanes), lambda j, info: (0, j + part * steps)),
+            ],
+        [
+                pl.BlockSpec((rows, 3 * lanes), lambda j, info: (0, j)),
+                pl.BlockSpec((1, 3 * lanes), lambda j, info: (0, j)),
+            ],
+        [
+            jax.ShapeDtypeStruct((rows, cols // 2), BF),
+            jax.ShapeDtypeStruct((1, cols // 2), F32),
+        ],
+        (info, proj, top,),
+        prefetch=1,
+        deps=deps,
+    )
+
+
+def whole_of(v):
+    return pl.BlockSpec(v.shape, lambda *_: (0,) * v.ndim)
+
+
+def tile_of(v, tile):
+    return pl.BlockSpec((tile, v.shape[1]), lambda j: (j, 0))
+
+
+def norm_of(z):
+    centred = z - jnp.mean(z, axis=1, keepdims=True)
+    r = lax.rsqrt(jnp.mean(centred * centred, axis=1, keepdims=True) + 1e-06)
+    return centred * r, r
+
+
+def norm_grad(t, zhat, r, gain):
+    gt = t * gain
+    mean = jnp.mean(gt, axis=1, keepdims=True)
+    return r * (gt - mean - zhat * jnp.mean(gt * zhat, axis=1, keepdims=True))
+
+
+def gather_sums(s_ref, *values):
+    sums = [jnp.sum(v, axis=0, keepdims=True) for v in values]
+    sums += [jnp.zeros_like(sums[0])] * (8 - len(sums))
+    sums = jnp.concatenate(sums, axis=0)
+
+    @pl.when(pl.program_id(0) == 0)
+    def _():
+        s_ref[...] = sums
+
+    @pl.when(pl.program_id(0) != 0)
+    def _():
+        s_ref[...] += sums
+
+
+def mix_body(c0, c1, s_ref, w0, w1, pc, pi, v_ref, zh_ref, r_ref, m_ref, mr_ref, x_ref):
+    h = w0.shape[0]
+    ctx = dot(c0[...], pc[:h, :]) + dot(c1[...], pc[h:, :])
+    ctx = ctx.astype(BF)
+    x_ref[...] = ctx
+    att = dot(ctx[:, :h], w0[...]) + dot(ctx[:, h:], w1[...]) + v_ref[3:4, :]
+    zhat, r = norm_of(s_ref[...].astype(F32) + att)
+    zh_ref[...] = zhat
+    r_ref[...] = jnp.broadcast_to(r, r_ref.shape)
+    mixed = zhat * v_ref[0:1, :] + v_ref[2:3, :]
+    m_ref[...] = mixed
+    mr_ref[...] = dot(mixed.astype(BF), pi[...]).astype(BF)
+
+
+def mix(c0, c1, stream, w0, w1, perm_ctx, perm_in, vecs, tile, deps=()):
+    rows, width = stream.shape
+    full = jax.ShapeDtypeStruct((rows, width), F32)
+    low = jax.ShapeDtypeStruct((rows, width), BF)
+    outs = [full, jax.ShapeDtypeStruct((rows, 128), F32), full, low, low]
+    return kernel(
+        mix_body,
+        "mix",
+        (rows // tile,),
+        [tile_of(v, tile) for v in (c0, c1, stream)]
+        + [whole_of(v) for v in (w0, w1, perm_ctx, perm_in, vecs)],
+        [tile_of(v, tile) for v in outs],
+        outs,
+        (c0, c1, stream, w0, w1, perm_ctx, perm_in, vecs,),
+        deps=deps,
+    )
+
+
+def turn_body(h_ref, w_ref, m_ref, c_ref, l_ref, v_ref, o_ref, g_ref, gb_ref, s_ref):
+    branch = dot(h_ref[...], w_ref[...]) + v_ref[5:6, :]
+    zhat, r = norm_of(m_ref[...] + branch)
+    gain = v_ref[1:2, :]
+    o_ref[...] = (zhat * gain + v_ref[4:5, :]).astype(BF)
+    seed = c_ref[...].astype(F32) * l_ref[:, 0:1]
+    g = norm_grad(seed, zhat, r, gain)
+    g_ref[...] = g
+    low = g.astype(BF)
+    gb_ref[...] = low
+    gather_sums(s_ref, seed * zhat, seed, low.astype(F32))
+
+
+def turn(h, w, mixed, cot, live, vecs, tile, deps=()):
+    rows, width = mixed.shape
+    full = jax.ShapeDtypeStruct((rows, width), F32)
+    low = jax.ShapeDtypeStruct((rows, width), BF)
+    sums = jax.ShapeDtypeStruct((8, width), F32)
+    return kernel(
+        turn_body,
+        "turn",
+        (rows // tile,),
+        [tile_of(h, tile), whole_of(w)]
+        + [tile_of(v, tile) for v in (mixed, cot, live)]
+        + [whole_of(vecs)],
+        [tile_of(v, tile) for v in (low, full, low)] + [whole_of(sums)],
+        [low, full, low, sums],
+        (h, w, mixed, cot, live, vecs,),
+        deps=deps,
+    )
+
+
+def unmix_body(
+    d0, d1, w00, w10, w01, w11, pi, g2, zh, r_ref, wo0, wo1, pc, v_ref, g1_ref, ga_ref, gc_ref, s_ref
+):
+    nt = ((1,), (1,))
+    parts = [
+        dot(d0[...], u[...], nt) + dot(d1[...], v[...], nt) for u, v in ((w00, w01), (w10, w11))
+    ]
+    back = jnp.concatenate(parts, axis=1).astype(BF)
+    grad = g2[...] + dot(back, pi[...], nt)
+    zhat = zh[...]
+    g1 = norm_grad(grad, zhat, r_ref[:, 0:1], v_ref[0:1, :])
+    g1_ref[...] = g1
+    low = g1.astype(BF)
+    ga_ref[...] = low
+    ctx = jnp.concatenate([dot(low, wo0[...], nt), dot(low, wo1[...], nt)], axis=1)
+    gc_ref[...] = dot(ctx.astype(BF), pc[...], nt).astype(BF)
+    gather_sums(s_ref, grad * zhat, grad, low.astype(F32))
+
+
+def unmix(d0, d1, w, perm_in, g2, zhat, r, wo0, wo1, perm_ctx, vecs, tile, deps=()):
+    rows, width = g2.shape
+    full = jax.ShapeDtypeStruct((rows, width), F32)
+    low = jax.ShapeDtypeStruct((rows, width), BF)
+    sums = jax.ShapeDtypeStruct((8, width), F32)
+    ws = (w[0][0], w[1][0], w[0][1], w[1][1])
+    return kernel(
+        unmix_body,
+        "unmix",
+        (rows // tile,),
+        [tile_of(d0, tile), tile_of(d1, tile)]
+        + [whole_of(v) for v in ws + (perm_in,)]
+        + [tile_of(v, tile) for v in (g2, zhat, r)]
+        + [whole_of(v) for v in (wo0, wo1, perm_ctx, vecs)],
+        [tile_of(v, tile) for v in (full, low, low)] + [whole_of(sums)],
+        [full, low, low, sums],
+        (d0, d1, *ws, perm_in, g2, zhat, r, wo0, wo1, perm_ctx, vecs,),
+        deps=deps,
+    )
+
+
+def stream_body(d0, d1, w00, w10, w01, w11, pi, g1, o_ref):
+    nt = ((1,), (1,))
+    parts = [
+        dot(d0[...], u[...], nt) + dot(d1[...], v[...], nt) for u, v in ((w00, w01), (w10, w11))
+    ]
+    back = jnp.concatenate(parts, axis=1).astype(BF)
+    o_ref[...] = (g1[...] + dot(back, pi[...], nt)).astype(BF)
+
+
+def stream_grad(d0, d1, w, perm_in, g1, tile, deps=()):
+    out = jax.ShapeDtypeStruct(g1.shape, BF)
+    ws = (w[0][0], w[1][0], w[0][1], w[1][1])
+    return kernel(
+        stream_body,
+        "stream_grad",
+        (g1.shape[0] // tile,),
+        [tile_of(d0, tile), tile_of(d1, tile)]
+        + [whole_of(v) for v in ws + (perm_in,)]
+        + [tile_of(g1, tile)],
+        tile_of(out, tile),
+        out,
+        (d0, d1, *ws, perm_in, g1,),
+        deps=deps,
+    )
+
+
+TN = ((0,), (0,))
+
+
+def rows_body(l_ref, r_ref, *refs, added, per):
+    grad = dot(l_ref[...], r_ref[...], TN)
+    if not added:
+        refs[0][...] = grad.astype(BF)
+        return
+    grad = (grad + refs[0][...].astype(F32)).astype(BF)
+    j = pl.program_id(0)
+    for i in range(4):
+
+        @pl.when(j // per == i)
+        def _():
+            refs[1 + i][...] = grad
+
+
+def weight_rows(left, right, got=None, deps=()):
+    tokens, k = left.shape
+    n = right.shape[1]
+    per = 2 if k // 8 % 128 == 0 else 1
+    block = k // (4 * per)
+    row = pl.BlockSpec((block, n), lambda j: (j, 0))
+    outs, out_specs, more = [jax.ShapeDtypeStruct((k, n), BF)], [row], []
+    if got is not None:
+        outs = [jax.ShapeDtypeStruct((k // 4, n), BF)] * 4
+        out_specs = [
+            pl.BlockSpec((block, n), lambda j, i=i: (jnp.clip(j - per * i, 0, per - 1), 0))
+            for i in range(4)
+        ]
+        more = [got]
+    return kernel(
+        functools.partial(rows_body, added=got is not None, per=per),
+        "weight_rows",
+        (4 * per,),
+        [pl.BlockSpec((tokens, block), lambda j: (0, j)), whole_of(right)]
+        + [row] * len(more),
+        out_specs,
+        outs,
+        (left, right, *more,),
+        deps=deps,
+    )
+
+
+def cols_body(l_ref, r0, r1, *refs, half, added):
+    j = pl.program_id(0)
+    turned = refs[-1]
+
+    @pl.when(j == 0)
+    def _():
+        turned[...] = l_ref[...].T
+
+    def go(r, high):
+        grad = dot(turned[...], r[...])
+        if not added:
+            refs[0][...] = grad.astype(BF)
+            return
+        got, keep_a, send_a, keep_b, send_b = refs[:5]
+        q = grad.shape[0] // 4
+        grad = (grad + got[...].astype(F32)).astype(BF)
+        keep_a[...] = grad[:q]
+        send_a[...] = grad[q : 2 * q]
+        if high:
+            send_b[...] = grad[2 * q :]
+        else:
+            keep_b[...] = grad[2 * q :]
+
+    @pl.when(j < half)
+    def _():
+        go(r0, False)
+
+    @pl.when(j >= half)
+    def _():
+        go(r1, True)
+
+
+def weight_cols(left, r0, r1, got=None, deps=()):
+    tokens, k = left.shape
+    n = r0.shape[1]
+    block = 512
+    half = n // block
+    low = pl.BlockSpec((tokens, block), lambda j: (0, jnp.minimum(j, half - 1)))
+    high = pl.BlockSpec((tokens, block), lambda j: (0, jnp.maximum(j - half, 0)))
+    full = pl.BlockSpec((k, block), lambda j: (0, j))
+    outs, out_specs, more = [jax.ShapeDtypeStruct((k, 2 * n), BF)], [full], []
+    if got is not None:
+        a = jax.ShapeDtypeStruct((k // 4, 2 * n), BF)
+        b = jax.ShapeDtypeStruct((k // 2, n), BF)
+        outs = [a, a, b, b]
+        sa = pl.BlockSpec((k // 4, block), lambda j: (0, j))
+        out_specs = [
+            sa,
+            sa,
+            pl.BlockSpec((k // 2, block), lambda j: (0, jnp.minimum(j, half - 1))),
+            pl.BlockSpec((k // 2, block), lambda j: (0, jnp.maximum(j - half, 0))),
+        ]
+        more = [got]
+    return kernel(
+        functools.partial(cols_body, half=half, added=got is not None),
+        "weight_cols",
+        (2 * half,),
+        [whole_of(left), low, high] + [full] * len(more),
+        out_specs,
+        outs,
+        (left, r0, r1, *more,),
+        scratch=[pltpu.VMEM((k, tokens), BF)],
+        deps=deps,
+    )
+
+
+class Order:
+    def __init__(self):
+        self.token = jnp.zeros((8, 128), F32)
+
+    def at(self, *values):
+        values, self.token = lax.optimization_barrier((values, self.token))
+        return values if len(values) > 1 else values[0]
+
+
+def rows_cat(*parts):
+    return jnp.concatenate(parts, axis=0)
+
+
+def one_sequence(
+    stream, lengths, assignment, cotangent, w_qkv, b_qv, w_out, w_in, b_in, w_back, gains, shifts
+):
+    _, own, width = stream.shape
+    rows = 2 * own
+    dp = lax.axis_size("dp")
+    x = lax.axis_index("tensor")
+    spot = lax.axis_index("dp")
+    zi, yi, ci = spot // 4, (spot // 2) % 2, spot % 2
+    lanes = 128
+
+    order = Order()
+    at = order.at
+    routes = {
+        "x": ("tensor", [(0, 1), (1, 0)]),
+        "y": ("dp", [(i, i ^ 2) for i in range(dp)]),
+        "c": ("dp", [(i, i ^ 1) for i in range(dp)]),
+    }
+    for k in range(1, 4):
+        routes[k] = ("dp", [(i, (i + 4 * k) % dp) for i in range(dp)])
+        routes[-k] = ("dp", [(i, (i - 4 * k) % dp) for i in range(dp)])
+
+    def send(way, value):
+        return lax.ppermute(at(value), *routes[way])
+
+    def along_z(value):
+        value = at(value)
+        return [lax.ppermute(value, *routes[k]) for k in range(1, 4)]
+
+    def other(v):
+        return lax.dynamic_index_in_dim(v, 1 - x, 0, keepdims=False)
+
+    def mine(v):
+        return lax.dynamic_index_in_dim(v, x, 0, keepdims=False)
+
+    n = jnp.arange(dp, dtype=jnp.int32)
+    slot = (zi - n // 4) % 4
+    first_half = slot < 2
+    y_rel = (n // 2) % 2 ^ yi
+    c_rel = n % 2 ^ ci
+    k2 = slot % 2
+    col_place = (slot // 2) * 4 + y_rel * 2 + k2
+
+    def row_place(x_rel):
+        return jnp.where(first_half, y_rel * 4 + x_rel * 2 + k2, 8 + x_rel * 4 + y_rel * 2 + k2)
+
+    def one_hot(dest, size):
+        return (dest[:, None] == jnp.arange(size, dtype=jnp.int32)[None, :]).astype(BF)
+
+    def spread(block_dest, block):
+        count = block_dest.shape[0]
+        dest = block_dest[:, None] * block + jnp.arange(block, dtype=jnp.int32)[None, :]
+        return one_hot(dest.reshape(-1), count * block)
+
+    perm_in = spread(c_rel * (dp // 2) + col_place, width // dp)
+    perm_ctx = spread(
+        jnp.concatenate([c_rel * dp + row_place(0), c_rel * dp + row_place(1)]), width // (2 * dp)
+    )
+    place = x[None].astype(jnp.int32)
+
+    def lane_rows(v):
+        v = v.astype(BF)
+        return jnp.pad(v, ((0, 0), (0, lanes - v.shape[1])))
+
+    small = jnp.concatenate(
+        [
+            b_in.reshape(1, lanes),
+            lane_rows(gains.T),
+            lane_rows(shifts.T),
+            lane_rows(b_qv.T),
+            jnp.zeros((7, lanes), BF),
+        ],
+        axis=0,
+    )
+
+    def add(u, v):
+        return u.astype(F32) + v.astype(F32)
+
+    groups = width // 2 // lanes
+    hw = width // 2
+    qs = w_qkv.reshape(-1, 3, groups, lanes).transpose(0, 2, 1, 3).reshape(-1, 3 * hw)
+
+    count = jnp.sum(lengths).astype(F32)
+    all_seqs = lengths.shape[0]
+    matches = mine(assignment) == jnp.arange(all_seqs, dtype=jnp.int32)
+    slot_len = jnp.sum(jnp.where(matches, lengths, 0))
+    info = jnp.stack([slot_len, x]).astype(jnp.int32)
+    row = jnp.arange(rows, dtype=jnp.int32)
+    position = jnp.where(row < own, row + x * own, row - x * own)
+    factor = F32(all_seqs * rows) / count
+    live = jnp.where(position < slot_len, factor, 0.0)
+    info, live, perm_in, perm_ctx, place, rel_at = (
+        info,
+        live,
+        perm_in,
+        perm_ctx,
+        place,
+        one_hot(c_rel * 8 + y_rel * 4 + slot, dp),
+    )
+
+    dw = width // dp
+    bw = width // (2 * dp)
+
+    def unpack(sm):
+        sm = sm.transpose(0, 1, 3, 2, 4, 5).reshape(dp, 2, 16, lanes)
+        sm = jnp.einsum("nr,rxql->nxql", rel_at, sm, preferred_element_type=F32)
+        vecs = sm[:, 0, 1:9, :dw].transpose(1, 0, 2).reshape(8, width)
+        bias_up = sm[:, :, 0].transpose(1, 0, 2).reshape(1, -1)
+        bias = sm[:, :, 7:9, :bw].transpose(2, 1, 0, 3).reshape(2, 2, groups, 1, lanes)
+        bias = jnp.concatenate([bias[0], jnp.zeros_like(bias[0]), bias[1]], axis=2)
+        return vecs, bias_up, bias.reshape(1, -1)
+
+    q1, q2, q3 = along_z(qs)
+    theirs = send("x", other(stream))
+    t1, t2, t3 = along_z(small)
+    q1, q2, q3 = at(q1, q2, q3)
+    qa, qb = rows_cat(qs, q1), rows_cat(q2, q3)
+    qax, qby = send("x", qa), send("y", qb)
+    o1, o2, o3 = along_z(w_out)
+    t1, t2, t3 = at(t1, t2, t3)
+    sm = jnp.stack([small, t1, t2, t3])
+    tx = send("x", sm)
+    theirs = at(theirs)
+    own_seq = rows_cat(mine(stream), theirs)
+    stream_rel = dot(own_seq, perm_in).astype(BF)
+    i1, i2, i3 = along_z(w_in)
+    wb = lax.all_gather(at(w_back), ("tensor", "dp"), axis=0, tiled=True)
+    qax, qby = at(qax, qby)
+    qay, qaxy, qbx, qbxy = send("y", qa), send("y", qax), send("x", qb), send("x", qby)
+    tx = at(tx)
+    sm = jnp.stack([sm, tx])
+    ty = send("y", sm)
+    o1, o2, o3 = at(o1, o2, o3)
+    oa, ob = rows_cat(w_out, o1), rows_cat(o2, o3)
+    ty = at(ty)
+    sm = jnp.stack([sm, ty])
+    tc = send("c", sm)
+    qay, qbx = at(qay, qbx)
+    q00 = rows_cat(qa, qay, qb, qby)
+    q10 = send("c", q00)
+    qaxy, qbxy = at(qaxy, qbxy)
+    q01 = rows_cat(qax, qaxy, qbx, qbxy)
+    q11 = send("c", q01)
+    oax, oby = send("x", oa), send("y", ob)
+    tc = at(tc)
+    vecs, bias_up, bias_proj = unpack(jnp.stack([sm, tc]))
+    i1, i2, i3 = at(i1, i2, i3)
+    ia, ib = rows_cat(w_in, i1), rows_cat(i2, i3)
+    iax, iby = send("x", ia), send("y", ib)
+    q10, q11, bias_proj, vecs, bias_up = at(q10, q11, bias_proj, vecs, bias_up)
+    wq = [[q00, q01], [q10, q11]]
+    proj = at(project(at(stream_rel), wq, bias_proj, 3 * lanes))
+    oax, oby, iax, iby = at(oax, oby, iax, iby)
+    oay, oaxy, obx, obxy = send("y", oa), send("y", oax), send("x", ob), send("x", oby)
+    iay, ibx = send("y", ia), send("x", ib)
+    ctx0 = at(attend(info, at(proj), lanes, 0))
+    oay, oaxy, obx, obxy, iay, ibx = at(oay, oaxy, obx, obxy, iay, ibx)
+    wo0 = rows_cat(oa, oax, oay, oaxy, ob, oby, obx, obxy)
+    wo1 = send("c", wo0)
+    iaxy, ibxy = send("y", iax), send("x", iby)
+    ctx1 = at(attend(info, at(proj), lanes, 1))
+    wo1, iaxy, ibxy = at(wo1, iaxy, ibxy)
+    i00, i01 = rows_cat(ia, iay, ib, iby), rows_cat(iax, iaxy, ibx, ibxy)
+    i10, i11 = send("c", i00), send("c", i01)
+    tile = own // 2
+    zhat1, r1, mixed, mixed_rel, ctx_rel = mix(
+        at(ctx0), ctx1, own_seq, wo0, wo1, perm_ctx, perm_in, vecs, tile
+    )
+    i10, i11, mixed_rel = at(i10, i11, mixed_rel)
+    cot_theirs = send("x", other(cotangent))
+    wi = [[i00, i01], [i10, i11]]
+    block = 2 * lanes
+    hidden, slope = up_gelu(at(mixed_rel), wi, bias_up, place, block)
+    hidden, cot_theirs, wb = at(hidden, cot_theirs, wb)
+    cot = rows_cat(mine(cotangent), cot_theirs)
+    live = jnp.broadcast_to(live[:, None], (rows, lanes))
+    result, grad_sum2, grad_branch, sums2 = turn(hidden, wb, mixed, cot, live, vecs, tile)
+
+    def whole(both, got):
+        return jnp.where(x == 0, jnp.stack([both, got]), jnp.stack([got, both]))
+
+    def finish(a, b, n):
+        parts = a[n:].astype(BF), b[:n].astype(BF), b[n:].astype(BF)
+        got = [lax.ppermute(v, *routes[-1 - i]) for i, v in enumerate(parts)]
+        return lambda: add(a[:n], got[0]) + add(got[1], got[2])
+
+    def join(a_near, a_far, b_near, b_far, a, b):
+        a1, b1 = add(a_far, a[1]).astype(BF), add(b_far, b[1]).astype(BF)
+        got = send("x", a1), send("y", b1)
+        return got, add(a_near, a[0]), add(b_near, b[0]), a1
+
+    def half_rows(v):
+        e = v.shape[0] // 2
+        return v[:e], v[e:]
+
+    def half_cols(v):
+        e = v.shape[1] // 2
+        return v[:, :e], v[:, e:]
+
+    def join_rows(keep_a, keep_b, a, b):
+        return join(*half_rows(keep_a), *half_rows(keep_b), half_rows(a), half_rows(b))
+
+    def join_cols(keep_a, keep_b, a, b):
+        return join(*half_cols(keep_a), *half_rows(keep_b), half_cols(a), half_rows(b))
+
+    def joined(got, a, b, _, n):
+        got = at(*got)
+        return add(a, got[0]), add(b, got[1]), n
+
+    grad_branch, hidden = at(grad_branch, hidden)
+    back = dot(hidden, grad_branch, TN).astype(BF)
+    back_done = lax.psum_scatter(at(back), ("tensor", "dp"), scatter_dimension=0, tiled=True)
+    lo_theirs = send("x", result[own:])
+    di0, us0 = down_grad(at(grad_branch), wb, slope, place, block, 0)
+    di1, us1 = down_grad(at(grad_branch), wb, slope, place, block, 1)
+    di0, di1 = at(di0, di1)
+    m0, m1 = half_cols(mixed_rel)
+    i_core = jnp.concatenate([dot(m1, r, TN).astype(BF) for r in (di0, di1)], axis=1)
+    i_got = send("c", i_core)
+    grad_sum1, grad_att, grad_ctx, sums1 = unmix(
+        at(di0), di1, wi, perm_in, grad_sum2, zhat1, r1, wo0, wo1, perm_ctx, vecs, own, deps=[i_core]
+    )
+    grad_att, i_got = at(grad_att, i_got)
+    ik_a, is_a, ik_b, is_b = weight_cols(m0, di0, di1, i_got, deps=[grad_att])
+    ia_got, ib_got = send("y", is_a), send("x", is_b)
+    c0, c1 = half_cols(ctx_rel)
+    o_core = dot(c1, grad_att, TN).astype(BF)
+    o_got = send("c", o_core)
+    dp0, ps0 = attend_grad(info, proj, at(grad_ctx), lanes, 0, deps=[is_a, o_core])
+    dp0, o_got = at(dp0, o_got)
+    ok_a, os_a, ok_b, os_b = weight_rows(c0, grad_att, o_got, deps=[dp0])
+    oa_got, ob_got = send("y", os_a), send("x", os_b)
+    dp1, ps1 = attend_grad(info, proj, at(grad_ctx), lanes, 1, deps=[os_a])
+    dp1 = at(dp1)
+    s0, s1 = half_cols(stream_rel)
+    q_core = jnp.concatenate([dot(s1, r, TN).astype(BF) for r in (dp0, dp1)], axis=1)
+    q_got = send("c", q_core)
+    ia_got, ib_got, oa_got, ob_got = at(ia_got, ib_got, oa_got, ob_got)
+    i_join = join_cols(ik_a, ik_b, ia_got, ib_got)
+    o_join = join_rows(ok_a, ok_b, oa_got, ob_got)
+    qk_a, qs_a, qk_b, qs_b = weight_cols(s0, dp0, dp1, at(q_got), deps=[i_join[3], o_join[3]])
+    qa_got, qb_got = send("y", qs_a), send("x", qs_b)
+    grad_stream = stream_grad(dp0, dp1, wq, perm_in, grad_sum1, own, deps=[qs_a])
+    grad_stream, qa_got, qb_got = at(grad_stream, qa_got, qb_got)
+    q_join = join_cols(qk_a, qk_b, qa_got, qb_got)
+    in_done = finish(*joined(*i_join, w_in.shape[0]))
+    out_done = finish(*joined(*o_join, w_out.shape[0]))
+    gs_theirs = send("x", grad_stream[own:])
+    qkv_done = finish(*joined(*q_join, qs.shape[0]))
+
+    proj_sum = jnp.concatenate([ps0, ps1], axis=1).reshape(2, groups, 3, lanes)
+    bias_grad = [proj_sum[:, :, j].reshape(2, dp, bw).transpose(1, 0, 2) for j in (0, 2)]
+    up_sum = jnp.concatenate([us0, us1], axis=1)
+
+    def widen(v):
+        return jnp.pad(v, ((0, 0), (0, 0), (0, lanes - v.shape[2])))
+
+    def both_halves(v):
+        return jnp.broadcast_to(widen(v.reshape(dp, 1, dw)), (dp, 2, lanes))
+
+    tiny = [up_sum.reshape(2, dp, lanes).transpose(1, 0, 2)]
+    tiny += [both_halves(v) for v in (sums1[0], sums2[0], sums1[1], sums1[2], sums2[1], sums2[2])]
+    tiny += [widen(v) for v in bias_grad]
+    tiny += [jnp.zeros_like(tiny[0])] * 7
+    tiny = jnp.stack(tiny, axis=2)
+    tiny = jnp.einsum(
+        "nr,nxql->rxql", rel_at.astype(F32), tiny, precision=lax.Precision.HIGHEST
+    ).reshape(2, 2, 4, 2, 16, lanes)
+
+    tiny = tiny[0] + send("c", tiny[1].astype(BF)).astype(F32)
+    tiny = tiny[0] + send("y", tiny[1].astype(BF)).astype(F32)
+    tiny = tiny[:, 0] + send("x", tiny[:, 1].astype(BF)).astype(F32)
+    t = finish(tiny[:2], tiny[2:], 1)()[0]
+    layer_out = whole(result[:own], lo_theirs)
+    grad_stream = whole(grad_stream[:own], gs_theirs)
+
+    return (
+        layer_out,
+        grad_stream,
+        qkv_done().reshape(-1, groups, 3, lanes).transpose(0, 2, 1, 3).reshape(w_qkv.shape),
+        t[7:9, :bw].T,
+        out_done(),
+        in_done(),
+        t[0],
+        back_done.astype(F32),
+        t[1:3, :dw].T,
+        t[3:7, :dw].T,
+    )
+
+
 def solution(mesh):
     in_specs = (
         P("dp", "tensor", None),
@@ -241,6 +1069,8 @@
         P("dp", None),
         P("dp", None),
     )
+    here = dict(mesh.shape)
+    paired = here["tensor"] == 2 and here["dp"] == 16
     return jax.shard_map(
-        per_device, mesh=mesh, in_specs=in_specs, out_specs=out_specs, check_vma=False
-    )
+        one_sequence if paired else per_device, mesh=mesh, in_specs=in_specs, out_specs=out_specs, check_vma=False
+    )

time: 1030 us -> 519 us (0.50)
  waiting for transfers between devices: 654 us -> 155 us
  Pallas kernels: 0 us -> 164 us
  matrix products: 169 us -> 20 us
  blocking collectives: 103 us -> 0 us
  starting transfers between devices: 1.77 us -> 87.7 us
  other arithmetic: 50 us -> 24 us
  local copies, waits for them, and re-layouts: 29.1 us -> 45.6 us
    reduce_scatter x7 -> x1, waiting for transfers between devices: 287 us -> 0.01 us  [one_sequence(): lax.psum_scatter(at(back), ('tensor', 'dp'), scatter_dimension=0, tiled=T...]
    all_gather x8 -> x1, waiting for transfers between devices: 194 us -> 0.02 us  [one_sequence(): wb = lax.all_gather(at(w_back), ('tensor', 'dp'), axis=0, tiled=True)]
    unnamed x23 -> x2, waiting for transfers between devices: 174 us -> 0.03 us
    pallas_call x0 -> x15, Pallas kernels: none -> 164 us  [kernel(): pl.pallas_call(without_deps, grid_spec=pltpu.PrefetchScalarGridSpec(num_s...]
    ppermute x0 -> x72, waiting for transfers between devices: none -> 155 us  [the longest x48 105 us: send(): return lax.ppermute(at(value), *routes[way])]
    dot_general x17 -> x9, matrix products: 156 us -> 20 us  [the longest x7 18.8 us: dot(): return lax.dot_general(a, b, (dims, ((), ())), preferred_element_type=F32)]
    ppermute x0 -> x72, starting transfers between devices: none -> 87.6 us  [the longest x48 41.3 us: send(): return lax.ppermute(at(value), *routes[way])]
    all_gather x4 -> x0, blocking collectives: 72.7 us -> none  [the longest x1 18.9 us: per_device(): lax.all_gather(b_qv, 'dp', axis=0, tiled=True)]
  transfers between devices with their start and end apart: 19 -> 74, of which waited for: 16 -> 26; matrix products, arithmetic and copies ran while one was open for 19% -> 12% of each run, Pallas kernels for 0% -> 26%
where the time goes in v1:
time: 519 us; the launch traced here: 512 us
  Pallas kernels  164 us (32%)
  waiting for transfers between devices  155 us (30%)
  starting transfers between devices  87.7 us (17%)
  local copies, waits for them, and re-layouts  45.6 us (9%)
  other arithmetic  24 us (5%)
  matrix products  20 us (4%)
  between operations  16.3 us (3%)
    pallas_call x15, Pallas kernels, kernel(): pl.pallas_call(without_deps, grid_spec=pltpu.PrefetchScalarGridSpec(num_s...  164 us
    ppermute x48, waiting for transfers between devices, send(): return lax.ppermute(at(value), *routes[way])  105 us
    ppermute x48, starting transfers between devices, send(): return lax.ppermute(at(value), *routes[way])  41.3 us
    ppermute x12, waiting for transfers between devices, finish(): got = [lax.ppermute(v, *routes[-1 - i]) for i, v in enumerate(parts)]  30.5 us
    ppermute x12, starting transfers between devices, finish(): got = [lax.ppermute(v, *routes[-1 - i]) for i, v in enumerate(parts)]  25.8 us
    ppermute x12, starting transfers between devices, along_z(): return [lax.ppermute(value, *routes[k]) for k in range(1, 4)]  20.5 us
    ppermute x12, waiting for transfers between devices, along_z(): return [lax.ppermute(value, *routes[k]) for k in range(1, 4)]  19.6 us
    dot_general x7, matrix products, dot(): return lax.dot_general(a, b, (dims, ((), ())), preferred_element_type=F32)  18.8 us
  transfers between devices with their start and end apart: 74, of which 26 were waited for; matrix products, arithmetic and copies ran while one was open for 12% of the time, Pallas kernels for 26%

profile of v1, /device:TPU:8, one launch (start us, length us, event | category | flops | bytes accessed | tf_op | source)
XLA Modules:
  0.0 512.3 jit_solution(8324879209860542666)
XLA Ops:
  8.6 2.1 dynamic-slice_bitcast_fusion.2
  14.4 3.5 collective-permute-start.5
  18.6 2.8 collective-permute-done.4
  21.4 3.9 collective-permute-start.3
  25.3 5.6 %collective-permute-done.5 = bf16[64,1536]{1,0:T(8,128)(2,1)S(1)} collective-permute-done((bf16[64,1536]{1,0:T(8,128)(2,1)S(1)}, bf16[64,1536]{1,0:T(8,128)(2,1)S(1)}, u32[]{:S(2)}, u32[]{:S(2)}) %collective-permute-start.5) | collective-permute-done | bytes 196640 | tf_op jit(solution)/shard_map/ppermute | solution.py:782
  35.5 8.6 %collective-permute-done = bf16[256,1024]{1,0:T(8,128)(2,1)} collective-permute-done((bf16[256,1024]{1,0:T(8,128)(2,1)}, bf16[256,1024]{1,0:T(8,128)(2,1)}, u32[]{:S(2)}, u32[]{:S(2)}) %collective-permute-start) | collective-permute-done | bytes 524320 | tf_op jit(solution)/shard_map/ppermute | solution.py:778
  50.5 3.4 collective-permute-start.15
  54.4 3.5 fusion.4.refs_0_
  60.0 4.1 collective-permute-start.8
  65.8 9.6 %collective-permute-done.16 = bf16[32,1024]{1,0:T(8,128)(2,1)S(1)} collective-permute-done((bf16[32,1024]{1,0:T(8,128)(2,1)S(1)}, bf16[32,1024]{1,0:T(8,128)(2,1)S(1)}, u32[]{:S(2)}, u32[]{:S(2)}) %collective-permute-start.16) | collective-permute-done | bytes 65568 | tf_op jit(solution)/shard_map/ppermute | solution.py:782
  78.0 5.4 %collective-permute-done.20 = bf16[128,1536]{1,0:T(8,128)(2,1)S(1)} collective-permute-done((bf16[128,1536]{1,0:T(8,128)(2,1)}, bf16[128,1536]{1,0:T(8,128)(2,1)S(1)}, u32[]{:S(2)}, u32[]{:S(2)}) %collective-permute-start.20) | collective-permute-done | bytes 393248 | tf_op jit(solution)/shard_map/ppermute | solution.py:778
  84.7 7.3 %collective-permute-done.18 = bf16[128,1536]{1,0:T(8,128)(2,1)S(1)} collective-permute-done((bf16[128,1536]{1,0:T(8,128)(2,1)S(1)}, bf16[128,1536]{1,0:T(8,128)(2,1)S(1)}, u32[]{:S(2)}, u32[]{:S(2)}) %collective-permute-start.18) | collective-permute-done | bytes 393248 | tf_op jit(solution)/shard_map/ppermute | solution.py:778
  92.0 3.7 collective-permute-done.19
  111.3 10.5 %project.1.refs_1_ = bf16[512,3072]{1,0:T(8,128)(2,1)} custom-call(bf16[512,1024]{1,0:T(8,128)(2,1)} %fusion.4.refs_0_, bf16[512,1536]{1,0:T(8,128)(2,1)} %copy-done.4, bf16[512,1536]{1,0:T(8,128)(2,1)} %collective-permute-done.26.refs_2_.refs_3_, bf16[512,1536]{1,0:T(8,128)(2,1)} %copy-done.3, bf16[512,1536]{1,0:T(8,128)(2,1)} %collective-permute-done.27.refs_4_.refs_5_, ...), custom_call_target="tpu_custom_call" | custom-call | tf_op jit(solution)/shard_map/project/pallas_call | solution.py:230
  121.7 6.2 %collective-permute-done.23 = bf16[64,1024]{1,0:T(8,128)(2,1)S(1)} collective-permute-done((bf16[64,1024]{1,0:T(8,128)(2,1)}, bf16[64,1024]{1,0:T(8,128)(2,1)S(1)}, u32[]{:S(2)}, u32[]{:S(2)}) %collective-permute-start.23) | collective-permute-done | bytes 131104 | tf_op jit(solution)/shard_map/ppermute | solution.py:778
  127.9 2.4 collective-permute-start.32
  136.2 11.2 %collective-permute-done.28 = bf16[64,1024]{1,0:T(8,128)(2,1)S(1)} collective-permute-done((bf16[64,1024]{1,0:T(8,128)(2,1)}, bf16[64,1024]{1,0:T(8,128)(2,1)S(1)}, u32[]{:S(2)}, u32[]{:S(2)}) %collective-permute-start.28) | collective-permute-done | bytes 131104 | tf_op jit(solution)/shard_map/ppermute | solution.py:778
  149.4 9.4 %attend.2.refs_0_ = bf16[512,512]{1,0:T(8,128)(2,1)} custom-call(s32[2]{0:T(128)} %pad_add_fusion.refs_0_, bf16[512,3072]{1,0:T(8,128)(2,1)} %project.1.refs_1_), custom_call_target="tpu_custom_call" | custom-call | tf_op jit(solution)/shard_map/attend/pallas_call | solution.py:230
  166.1 9.4 %attend.3.refs_1_ = bf16[512,512]{1,0:T(8,128)(2,1)} custom-call(s32[2]{0:T(128)} %pad_add_fusion.refs_0_, bf16[512,3072]{1,0:T(8,128)(2,1)} %project.1.refs_1_), custom_call_target="tpu_custom_call" | custom-call | tf_op jit(solution)/shard_map/attend/pallas_call | solution.py:230
  184.6 2.1 pad_maximum_fusion.2.refs_2_
  186.7 9.8 %mix.1 = (f32[512,1024]{1,0:T(8,128)}, f32[512,128]{1,0:T(8,128)}, f32[512,1024]{1,0:T(8,128)}, bf16[512,1024]{1,0:T(8,128)(2,1)}, bf16[512,1024]{1,0:T(8,128)(2,1)}) custom-call(bf16[512,512]{1,0:T(8,128)(2,1)} %attend.2.refs_0_, bf16[512,512]{1,0:T(8,128)(2,1)} %attend.3.refs_1_, bf16[512,1024]{1,0:T(8,128)(2,1)} %pad_maximum_fusion.2.refs_2_, ...), custom_call_target="tpu_custom_call" | custom-call | tf_op jit(solution)/shard_map/mix/pallas_call | solution.py:230
  198.7 19.2 %up_gelu.1 = (bf16[512,4096]{1,0:T(8,128)(2,1)}, bf16[512,4096]{1,0:T(8,128)(2,1)}) custom-call(s32[1]{0:T(128)} %bitcast.refs_0_, bf16[512,1024]{1,0:T(8,128)(2,1)} %get-tuple-element.386.refs_1_, bf16[512,2048]{1,0:T(8,128)(2,1)} %constant_dynamic-update-slice_fusion.22.refs_2_, bf16[512,2048]{1,0:T(8,128)(2,1)} %collective-permute-done.37.refs_3_, ...), custom_call_target="tpu_custom_call" | custom-call | tf_op jit(solution)/shard_map/up_gelu/pallas_call | solution.py:230
  219.8 12.4 %turn.1 = (bf16[512,1024]{1,0:T(8,128)(2,1)}, f32[512,1024]{1,0:T(8,128)}, bf16[512,1024]{1,0:T(8,128)(2,1)}, f32[8,1024]{1,0:T(8,128)}) custom-call(bf16[512,4096]{1,0:T(8,128)(2,1)} %get-tuple-element.401.refs_0_, bf16[4096,1024]{1,0:T(8,128)(2,1)} %all-gather.2.cloned.1.call-done.refs_1_.refs_2_, f32[512,1024]{1,0:T(8,128)} %get-tuple-element.396.refs_2_, ...), custom_call_target="tpu_custom_call" | custom-call | tf_op jit(solution)/shard_map/turn/pallas_call | solution.py:230
  232.2 2.3 slice_bitcast_fusion.1
  234.6 7.0 %convolution_convert_fusion = bf16[4096,1024]{1,0:T(8,128)(2,1)} fusion(bf16[512,4096]{1,0:T(8,128)(2,1)S(1)} %copy-done.8, bf16[512,1024]{1,0:T(8,128)(2,1)S(1)} %copy-done.9), kind=kOutput, calls=%fused_computation | convolution fusion | flops 4299161600 | bytes 13631488 | tf_op jit(solution)/shard_map/dot_general | solution.py:257
  241.6 8.6 %down_grad.2 = (bf16[512,2048]{1,0:T(8,128)(2,1)}, f32[1,2048]{1,0:T(1,128)}) custom-call(s32[1]{0:T(128)} %bitcast.refs_0_, bf16[512,1024]{1,0:T(8,128)(2,1)} %get-tuple-element.411.refs_1_, bf16[4096,1024]{1,0:T(8,128)(2,1)} %all-gather.2.cloned.1.call-done.refs_1_.refs_2_, bf16[512,4096]{1,0:T(8,128)(2,1)} %get-tuple-element.408.refs_3_), custom_call_target="tpu_custom_call" | custom-call | tf_op jit(solution)/shard_map/down_grad/pallas_call | solution.py:230
  250.2 8.7 %down_grad.3 = (bf16[512,2048]{1,0:T(8,128)(2,1)}, f32[1,2048]{1,0:T(1,128)}) custom-call(s32[1]{0:T(128)} %bitcast.refs_0_, bf16[512,1024]{1,0:T(8,128)(2,1)} %get-tuple-element.411.refs_1_, bf16[4096,1024]{1,0:T(8,128)(2,1)} %all-gather.2.cloned.1.call-done.refs_1_.refs_2_, bf16[512,4096]{1,0:T(8,128)(2,1)} %get-tuple-element.408.refs_3_), custom_call_target="tpu_custom_call" | custom-call | tf_op jit(solution)/shard_map/down_grad/pallas_call | solution.py:230
  258.9 3.0 convolution_convert_fusion.3
  263.2 2.5 pad_maximum_fusion.refs_14_
  270.7 17.5 %unmix.1 = (f32[512,1024]{1,0:T(8,128)}, bf16[512,1024]{1,0:T(8,128)(2,1)}, bf16[512,1024]{1,0:T(8,128)(2,1)}, f32[8,1024]{1,0:T(8,128)}) custom-call(bf16[512,2048]{1,0:T(8,128)(2,1)} %get-tuple-element.418.refs_0_.refs_1_, bf16[512,2048]{1,0:T(8,128)(2,1)} %get-tuple-element.415.refs_1_.refs_2_, ...), custom_call_target="tpu_custom_call" | custom-call | tf_op jit(solution)/shard_map/unmix/pallas_call | solution.py:230
  292.7 9.6 %weight_cols.2 = (bf16[128,4096]{1,0:T(8,128)(2,1)}, bf16[128,4096]{1,0:T(8,128)(2,1)}, bf16[256,2048]{1,0:T(8,128)(2,1)}, bf16[256,2048]{1,0:T(8,128)(2,1)}) custom-call(bf16[512,512]{1,0:T(8,128)(2,1)} %slice.254.refs_0_, bf16[512,2048]{1,0:T(8,128)(2,1)} %get-tuple-element.418.refs_0_.refs_1_, bf16[512,2048]{1,0:T(8,128)(2,1)} %get-tuple-element.415.refs_1_.refs_2_, ...), custom_call_target="tpu_custom_call" | custom-call | tf_op jit(solution)/shard_map/weight_cols/pallas_call | solution.py:230
  302.3 13.2 %attend_grad.2 = (bf16[512,1536]{1,0:T(8,128)(2,1)}, f32[1,1536]{1,0:T(1,128)}) custom-call(s32[2]{0:T(128)} %pad_add_fusion.refs_0_, bf16[512,3072]{1,0:T(8,128)(2,1)} %project.1.refs_1_, bf16[512,1024]{1,0:T(8,128)(2,1)} %get-tuple-element.435.refs_2_, bf16[128,4096]{1,0:T(8,128)(2,1)} %get-tuple-element.454.refs_3_, bf16[512,1024]{1,0:T(8,128)(2,1)} %copy-done.23), custom_call_target="tpu_custom_call" | custom-call | tf_op jit(solution)/shard_map/attend_grad/pallas_call | solution.py:230
  316.5 4.7 weight_rows.1
  321.2 12.9 %attend_grad.3 = (bf16[512,1536]{1,0:T(8,128)(2,1)}, f32[1,1536]{1,0:T(1,128)}) custom-call(s32[2]{0:T(128)} %pad_add_fusion.refs_0_, bf16[512,3072]{1,0:T(8,128)(2,1)} %project.1.refs_1_, bf16[512,1024]{1,0:T(8,128)(2,1)} %get-tuple-element.435.refs_2_, bf16[128,1024]{1,0:T(8,128)(2,1)} %get-tuple-element.456.refs_3_), custom_call_target="tpu_custom_call" | custom-call | tf_op jit(solution)/shard_map/attend_grad/pallas_call | solution.py:230
  336.0 2.3 maximum_select_fusion
  342.4 43.6 %collective-permute-done.57 = bf16[4,2,16,128]{3,2,0,1:T(8,128)(2,1)S(1)} collective-permute-done((bf16[4,2,16,128]{3,2,0,1:T(8,128)(2,1)S(1)}, bf16[4,2,16,128]{3,2,0,1:T(8,128)(2,1)S(1)}, u32[]{:S(2)}, u32[]{:S(2)}) %collective-permute-start.57) | collective-permute-done | bytes 32800 | tf_op jit(solution)/shard_map/ppermute | solution.py:778
  391.8 3.5 collective-permute-start.60
  401.9 7.7 %collective-permute-done.46 = bf16[128,1024]{1,0:T(8,128)(2,1)S(1)} collective-permute-done((bf16[128,1024]{1,0:T(8,128)(2,1)S(1)}, bf16[128,1024]{1,0:T(8,128)(2,1)S(1)}, u32[]{:S(2)}, u32[]{:S(2)}) %collective-permute-start.46) | collective-permute-done | bytes 262176 | tf_op jit(solution)/shard_map/ppermute | solution.py:778
  418.4 5.1 %collective-permute-start.65 = (bf16[32,1024]{1,0:T(8,128)(2,1)S(1)}, bf16[32,1024]{1,0:T(8,128)(2,1)S(1)}, u32[]{:S(2)}, u32[]{:S(2)}) collective-permute-start(bf16[32,1024]{1,0:T(8,128)(2,1)S(1)} %get-tuple-element.524), channel_id=1, source_target_pairs={{0,16},{2,18},{4,20},{6,22},{8,24},{10,26},{12,28},{14,30},{16,0},... | collective-permute-start | bytes 196616 | tf_op jit(solution)/shard_map/ppermute | solution.py:938
  423.6 4.2 collective-permute-start.64
  432.1 7.6 %weight_cols.3 = (bf16[128,3072]{1,0:T(8,128)(2,1)}, bf16[128,3072]{1,0:T(8,128)(2,1)}, bf16[256,1536]{1,0:T(8,128)(2,1)}, bf16[256,1536]{1,0:T(8,128)(2,1)}) custom-call(bf16[512,512]{1,0:T(8,128)(2,1)} %slice.323.refs_0_, bf16[512,1536]{1,0:T(8,128)(2,1)} %get-tuple-element.439.refs_3_.refs_1_.refs_0_, ...), custom_call_target="tpu_custom_call" | custom-call | tf_op jit(solution)/shard_map/weight_cols/pallas_call | solution.py:230
  442.3 10.1 %stream_grad.1 = bf16[512,1024]{1,0:T(8,128)(2,1)} custom-call(bf16[512,1536]{1,0:T(8,128)(2,1)} %get-tuple-element.439.refs_3_.refs_1_.refs_0_, bf16[512,1536]{1,0:T(8,128)(2,1)} %get-tuple-element.449.refs_2_.refs_1_, bf16[512,1536]{1,0:T(8,128)(2,1)} %copy-done.4, bf16[512,1536]{1,0:T(8,128)(2,1)} %collective-permute-done.26.refs_2_.refs_3_, ...), custom_call_target="tpu_custom_call" | custom-call | tf_op jit(solution)/shard_map/stream_grad/pallas_call | solution.py:230
  452.4 5.4 %collective-permute-done.48 = bf16[128,3072]{1,0:T(8,128)(2,1)S(1)} collective-permute-done((bf16[128,3072]{1,0:T(8,128)(2,1)}, bf16[128,3072]{1,0:T(8,128)(2,1)S(1)}, u32[]{:S(2)}, u32[]{:S(2)}) %collective-permute-start.48) | collective-permute-done | bytes 786464 | tf_op jit(solution)/shard_map/ppermute | solution.py:778
  460.3 5.4 %collective-permute-start.70 = (bf16[64,2048]{1,0:T(8,128)(2,1)S(1)}, bf16[64,2048]{1,0:T(8,128)(2,1)S(1)}, u32[]{:S(2)}, u32[]{:S(2)}) collective-permute-start(bf16[64,2048]{1,0:T(8,128)(2,1)S(1)} %get-tuple-element.512), channel_id=1, source_target_pairs={{0,16},{2,18},{4,20},{6,22},{8,24},{10,26},{12,28},{14,30},{16,0},... | collective-permute-start | bytes 786440 | tf_op jit(solution)/shard_map/ppermute | solution.py:938
  470.5 2.9 collective-permute-start.54
  473.5 15.3 %collective-permute-done.70 = bf16[64,2048]{1,0:T(8,128)(2,1)S(1)} collective-permute-done((bf16[64,2048]{1,0:T(8,128)(2,1)S(1)}, bf16[64,2048]{1,0:T(8,128)(2,1)S(1)}, u32[]{:S(2)}, u32[]{:S(2)}) %collective-permute-start.70) | collective-permute-done | bytes 262176 | tf_op jit(solution)/shard_map/ppermute | solution.py:938
  488.8 5.8 %collective-permute-done.69 = bf16[64,2048]{1,0:T(8,128)(2,1)S(1)} collective-permute-done((bf16[64,2048]{1,0:T(8,128)(2,1)S(1)}, bf16[64,2048]{1,0:T(8,128)(2,1)S(1)}, u32[]{:S(2)}, u32[]{:S(2)}) %collective-permute-start.69) | collective-permute-done | bytes 262176 | tf_op jit(solution)/shard_map/ppermute | solution.py:938
  497.9 4.2 collective-permute-done.53
  (398 shorter events, 126.6 us)
Async XLA Ops:
  7.2 210.7 %all-gather.2.cloned.1.call-start = ((), (), s32[]{:S(2)}) async-start(), calls=%async_computation.1 | async-start | bytes 8650752 | tf_op jit(solution)/shard_map/all_gather | solution.py:881
  10.9 24.5 %collective-permute-start.1 = (bf16[16,128]{1,0:T(8,128)(2,1)S(1)}, bf16[16,128]{1,0:T(8,128)(2,1)S(1)}, u32[]{:S(2)}, u32[]{:S(2)}) collective-permute-start(bf16[16,128]{1,0:T(8,128)(2,1)S(1)} %concatenate.67), channel_id=1, source_target_pairs={{0,8},{2,10},{4,12},{6,14},{8,16},{10,18},{12,20},{14,22},{16,24},... | collective-permute-start | bytes 12296 | tf_op jit(solution)/shard_map/ppermute | solution.py:782
  12.5 22.9 %collective-permute-start.2 = (bf16[16,128]{1,0:T(8,128)(2,1)S(1)}, bf16[16,128]{1,0:T(8,128)(2,1)S(1)}, u32[]{:S(2)}, u32[]{:S(2)}) collective-permute-start(bf16[16,128]{1,0:T(8,128)(2,1)S(1)} %concatenate.67), channel_id=1, source_target_pairs={{0,16},{2,18},{4,20},{6,22},{8,24},{10,26},{12,28},{14,30},{16,0},... | collective-permute-start | bytes 12296 | tf_op jit(solution)/shard_map/ppermute | solution.py:782
  14.4 16.5 %collective-permute-start.5 = (bf16[64,1536]{1,0:T(8,128)(2,1)S(1)}, bf16[64,1536]{1,0:T(8,128)(2,1)S(1)}, u32[]{:S(2)}, u32[]{:S(2)}) collective-permute-start(bf16[64,1536]{1,0:T(8,128)(2,1)S(1)} %reshape.232), channel_id=1, source_target_pairs={{0,16},{2,18},{4,20},{6,22},{8,24},{10,26},{12,28},{14,30},{16,0},... | collective-permute-start | bytes 589832 | tf_op jit(solution)/shard_map/ppermute | solution.py:782
  17.9 16.0 %collective-permute-start.6 = (bf16[64,1536]{1,0:T(8,128)(2,1)S(1)}, bf16[64,1536]{1,0:T(8,128)(2,1)S(1)}, u32[]{:S(2)}, u32[]{:S(2)}) collective-permute-start(bf16[64,1536]{1,0:T(8,128)(2,1)S(1)} %reshape.232), channel_id=1, source_target_pairs={{0,24},{2,26},{4,28},{6,30},{8,0},{10,2},{12,4},{14,6},{16,8},{18,... | collective-permute-start | bytes 589832 | tf_op jit(solution)/shard_map/ppermute | solution.py:782
  21.4 14.0 %collective-permute-start.3 = (bf16[16,128]{1,0:T(8,128)(2,1)S(1)}, bf16[16,128]{1,0:T(8,128)(2,1)S(1)}, u32[]{:S(2)}, u32[]{:S(2)}) collective-permute-start(bf16[16,128]{1,0:T(8,128)(2,1)S(1)} %concatenate.67), channel_id=1, source_target_pairs={{0,24},{2,26},{4,28},{6,30},{8,0},{10,2},{12,4},{14,6},{16,8},{18,... | collective-permute-start | bytes 12296 | tf_op jit(solution)/shard_map/ppermute | solution.py:782
  30.9 13.2 %collective-permute-start = (bf16[256,1024]{1,0:T(8,128)(2,1)}, bf16[256,1024]{1,0:T(8,128)(2,1)}, u32[]{:S(2)}, u32[]{:S(2)}) collective-permute-start(bf16[256,1024]{1,0:T(8,128)(2,1)} %get-tuple-element.252), channel_id=1, source_target_pairs={{0,1},{1,0},{2,3},{3,2},{4,5},{5,4},{6,7},{7,6},{8,9},{9,8},{10,11... | collective-permute-start | bytes 1572872 | tf_op jit(solution)/shard_map/ppermute | solution.py:778
  44.1 459.3 %reduce-scatter.2.cloned.1.call-start = ((), (), s32[]{:S(2)}) async-start(), calls=%async_computation.2 | async-start | bytes 8650752 | tf_op jit(solution)/shard_map/reduce_scatter | solution.py:966
  50.5 13.7 %collective-permute-start.14 = (bf16[32,1024]{1,0:T(8,128)(2,1)S(1)}, bf16[32,1024]{1,0:T(8,128)(2,1)S(1)}, u32[]{:S(2)}, u32[]{:S(2)}) collective-permute-start(bf16[32,1024]{1,0:T(8,128)(2,1)S(1)} %copy-done.41), channel_id=1, source_target_pairs={{0,8},{2,10},{4,12},{6,14},{8,16},{10,18},{12,20},{14,22},{16,24},... | collective-permute-start | bytes 196616 | tf_op jit(solution)/shard_map/ppermute | solution.py:782
  50.5 15.3 %collective-permute-start.15 = (bf16[32,1024]{1,0:T(8,128)(2,1)S(1)}, bf16[32,1024]{1,0:T(8,128)(2,1)S(1)}, u32[]{:S(2)}, u32[]{:S(2)}) collective-permute-start(bf16[32,1024]{1,0:T(8,128)(2,1)S(1)} %copy-done.41), channel_id=1, source_target_pairs={{0,16},{2,18},{4,20},{6,22},{8,24},{10,26},{12,28},{14,30},{16,0},... | collective-permute-start | bytes 196616 | tf_op jit(solution)/shard_map/ppermute | solution.py:782
  57.9 17.5 %collective-permute-start.16 = (bf16[32,1024]{1,0:T(8,128)(2,1)S(1)}, bf16[32,1024]{1,0:T(8,128)(2,1)S(1)}, u32[]{:S(2)}, u32[]{:S(2)}) collective-permute-start(bf16[32,1024]{1,0:T(8,128)(2,1)S(1)} %copy-done.41), channel_id=1, source_target_pairs={{0,24},{2,26},{4,28},{6,30},{8,0},{10,2},{12,4},{14,6},{16,8},{18,... | collective-permute-start | bytes 196616 | tf_op jit(solution)/shard_map/ppermute | solution.py:782
  59.9 35.9 %collective-permute-start.7 = (bf16[64,2048]{1,0:T(8,128)(2,1)}, bf16[64,2048]{1,0:T(8,128)(2,1)S(1)}, u32[]{:S(2)}, u32[]{:S(2)}) collective-permute-start(bf16[64,2048]{1,0:T(8,128)(2,1)} %param.19), channel_id=1, source_target_pairs={{0,8},{2,10},{4,12},{6,14},{8,16},{10,18},{12,20},{14,22},{16,24},... | collective-permute-start | bytes 786440 | tf_op jit(solution)/shard_map/ppermute | solution.py:782
  60.0 35.9 %collective-permute-start.8 = (bf16[64,2048]{1,0:T(8,128)(2,1)}, bf16[64,2048]{1,0:T(8,128)(2,1)S(1)}, u32[]{:S(2)}, u32[]{:S(2)}) collective-permute-start(bf16[64,2048]{1,0:T(8,128)(2,1)} %param.19), channel_id=1, source_target_pairs={{0,16},{2,18},{4,20},{6,22},{8,24},{10,26},{12,28},{14,30},{16,0},... | collective-permute-start | bytes 786440 | tf_op jit(solution)/shard_map/ppermute | solution.py:782
  64.1 13.8 %collective-permute-start.13 = (bf16[2,4,16,128]{3,2,1,0:T(8,128)(2,1)S(1)}, bf16[2,4,16,128]{3,2,1,0:T(8,128)(2,1)S(1)}, u32[]{:S(2)}, u32[]{:S(2)}) collective-permute-start(bf16[2,4,16,128]{3,2,1,0:T(8,128)(2,1)S(1)} %get-tuple-element.285), channel_id=1, source_target_pairs={{0,4},{2,6},{4,0},{6,2},{8,12},{10,14},{12,8},{14,10},{16,20},{18,... | collective-permute-start | bytes 98312 | tf_op jit(solution)/shard_map/ppermute | solution.py:778
  77.9 17.9 %collective-permute-start.9 = (bf16[64,2048]{1,0:T(8,128)(2,1)}, bf16[64,2048]{1,0:T(8,128)(2,1)S(1)}, u32[]{:S(2)}, u32[]{:S(2)}) collective-permute-start(bf16[64,2048]{1,0:T(8,128)(2,1)} %param.19), channel_id=1, source_target_pairs={{0,24},{2,26},{4,28},{6,30},{8,0},{10,2},{12,4},{14,6},{16,8},{18,... | collective-permute-start | bytes 786440 | tf_op jit(solution)/shard_map/ppermute | solution.py:782
  95.9 25.8 %collective-permute-start.22 = (bf16[64,1024]{1,0:T(8,128)(2,1)}, bf16[64,1024]{1,0:T(8,128)(2,1)}, u32[]{:S(2)}, u32[]{:S(2)}) collective-permute-start(bf16[64,1024]{1,0:T(8,128)(2,1)} %get-tuple-element.333), channel_id=1, source_target_pairs={{0,1},{1,0},{2,3},{3,2},{4,5},{5,4},{6,7},{7,6},{8,9},{9,8},{10,11... | collective-permute-start | bytes 393224 | tf_op jit(solution)/shard_map/ppermute | solution.py:778
  96.5 12.9 %collective-permute-start.26 = (bf16[512,1536]{1,0:T(8,128)(2,1)S(1)}, bf16[512,1536]{1,0:T(8,128)(2,1)}, u32[]{:S(2)}, u32[]{:S(2)}) collective-permute-start(bf16[512,1536]{1,0:T(8,128)(2,1)S(1)} %constant_dynamic-update-slice_fusion.8.refs_1_.refs_2_), channel_id=1, source_target_pairs={{0,2},{2,0},{4,6},{6,4},{8,10},{10,8},{12,14},{14,12},{16,18},{18,... | collective-permute-start | bytes 4718600 | tf_op jit(solution)/shard_map/ppermute | solution.py:778
  97.4 30.5 %collective-permute-start.24 = (bf16[128,2048]{1,0:T(8,128)(2,1)}, bf16[128,2048]{1,0:T(8,128)(2,1)}, u32[]{:S(2)}, u32[]{:S(2)}) collective-permute-start(bf16[128,2048]{1,0:T(8,128)(2,1)} %get-tuple-element.343), channel_id=1, source_target_pairs={{0,1},{1,0},{2,3},{3,2},{4,5},{5,4},{6,7},{7,6},{8,9},{9,8},{10,11... | collective-permute-start | bytes 1572872 | tf_op jit(solution)/shard_map/ppermute | solution.py:778
  100.5 27.4 %collective-permute-start.25 = (bf16[128,2048]{1,0:T(8,128)(2,1)}, bf16[128,2048]{1,0:T(8,128)(2,1)}, u32[]{:S(2)}, u32[]{:S(2)}) collective-permute-start(bf16[128,2048]{1,0:T(8,128)(2,1)} %constant_dynamic-update-slice_fusion.20), channel_id=1, source_target_pairs={{0,4},{2,6},{4,0},{6,2},{8,12},{10,14},{12,8},{14,10},{16,20},{18,... | collective-permute-start | bytes 1572872 | tf_op jit(solution)/shard_map/ppermute | solution.py:778
  109.4 18.5 %collective-permute-start.23 = (bf16[64,1024]{1,0:T(8,128)(2,1)}, bf16[64,1024]{1,0:T(8,128)(2,1)S(1)}, u32[]{:S(2)}, u32[]{:S(2)}) collective-permute-start(bf16[64,1024]{1,0:T(8,128)(2,1)} %copy-done.42), channel_id=1, source_target_pairs={{0,4},{2,6},{4,0},{6,2},{8,12},{10,14},{12,8},{14,10},{16,20},{18,... | collective-permute-start | bytes 393224 | tf_op jit(solution)/shard_map/ppermute | solution.py:778
  127.9 31.9 %collective-permute-start.32 = (bf16[128,2048]{1,0:T(8,128)(2,1)}, bf16[128,2048]{1,0:T(8,128)(2,1)S(1)}, u32[]{:S(2)}, u32[]{:S(2)}) collective-permute-start(bf16[128,2048]{1,0:T(8,128)(2,1)} %get-tuple-element.343), channel_id=1, source_target_pairs={{0,4},{2,6},{4,0},{6,2},{8,12},{10,14},{12,8},{14,10},{16,20},{18,... | collective-permute-start | bytes 1572872 | tf_op jit(solution)/shard_map/ppermute | solution.py:778
  130.3 29.5 %collective-permute-start.33 = (bf16[128,2048]{1,0:T(8,128)(2,1)}, bf16[128,2048]{1,0:T(8,128)(2,1)S(1)}, u32[]{:S(2)}, u32[]{:S(2)}) collective-permute-start(bf16[128,2048]{1,0:T(8,128)(2,1)} %constant_dynamic-update-slice_fusion.20), channel_id=1, source_target_pairs={{0,1},{1,0},{2,3},{3,2},{4,5},{5,4},{6,7},{7,6},{8,9},{9,8},{10,11... | collective-permute-start | bytes 1572872 | tf_op jit(solution)/shard_map/ppermute | solution.py:778
  130.4 17.0 %collective-permute-start.28 = (bf16[64,1024]{1,0:T(8,128)(2,1)}, bf16[64,1024]{1,0:T(8,128)(2,1)S(1)}, u32[]{:S(2)}, u32[]{:S(2)}) collective-permute-start(bf16[64,1024]{1,0:T(8,128)(2,1)} %get-tuple-element.333), channel_id=1, source_target_pairs={{0,4},{2,6},{4,0},{6,2},{8,12},{10,14},{12,8},{14,10},{16,20},{18,... | collective-permute-start | bytes 393224 | tf_op jit(solution)/shard_map/ppermute | solution.py:778
  132.4 27.4 %collective-permute-start.29 = (bf16[64,1024]{1,0:T(8,128)(2,1)}, bf16[64,1024]{1,0:T(8,128)(2,1)S(1)}, u32[]{:S(2)}, u32[]{:S(2)}) collective-permute-start(bf16[64,1024]{1,0:T(8,128)(2,1)} %collective-permute-done.22), channel_id=1, source_target_pairs={{0,4},{2,6},{4,0},{6,2},{8,12},{10,14},{12,8},{14,10},{16,20},{18,... | collective-permute-start | bytes 393224 | tf_op jit(solution)/shard_map/ppermute | solution.py:778
  134.3 25.4 %collective-permute-start.30 = (bf16[64,1024]{1,0:T(8,128)(2,1)S(1)}, bf16[64,1024]{1,0:T(8,128)(2,1)S(1)}, u32[]{:S(2)}, u32[]{:S(2)}) collective-permute-start(bf16[64,1024]{1,0:T(8,128)(2,1)S(1)} %copy-done.43), channel_id=1, source_target_pairs={{0,1},{1,0},{2,3},{3,2},{4,5},{5,4},{6,7},{7,6},{8,9},{9,8},{10,11... | collective-permute-start | bytes 393224 | tf_op jit(solution)/shard_map/ppermute | solution.py:778
  159.9 18.2 %collective-permute-start.34 = (bf16[512,1024]{1,0:T(8,128)(2,1)S(1)}, bf16[512,1024]{1,0:T(8,128)(2,1)S(1)}, u32[]{:S(2)}, u32[]{:S(2)}) collective-permute-start(bf16[512,1024]{1,0:T(8,128)(2,1)S(1)} %constant_dynamic-update-slice_fusion.28.refs_3_.refs_10_), channel_id=1, source_target_pairs={{0,2},{2,0},{4,6},{6,4},{8,10},{10,8},{12,14},{14,12},{16,18},{18,... | collective-permute-start | bytes 3145736 | tf_op jit(solution)/shard_map/ppermute | solution.py:778
  161.4 16.7 %collective-permute-start.35 = (bf16[128,2048]{1,0:T(8,128)(2,1)}, bf16[128,2048]{1,0:T(8,128)(2,1)S(1)}, u32[]{:S(2)}, u32[]{:S(2)}) collective-permute-start(bf16[128,2048]{1,0:T(8,128)(2,1)} %collective-permute-done.24), channel_id=1, source_target_pairs={{0,4},{2,6},{4,0},{6,2},{8,12},{10,14},{12,8},{14,10},{16,20},{18,... | collective-permute-start | bytes 1572872 | tf_op jit(solution)/shard_map/ppermute | solution.py:778
  163.3 14.8 %collective-permute-start.36 = (bf16[128,2048]{1,0:T(8,128)(2,1)}, bf16[128,2048]{1,0:T(8,128)(2,1)S(1)}, u32[]{:S(2)}, u32[]{:S(2)}) collective-permute-start(bf16[128,2048]{1,0:T(8,128)(2,1)} %collective-permute-done.25), channel_id=1, source_target_pairs={{0,1},{1,0},{2,3},{3,2},{4,5},{5,4},{6,7},{7,6},{8,9},{9,8},{10,11... | collective-permute-start | bytes 1572872 | tf_op jit(solution)/shard_map/ppermute | solution.py:778
  178.1 18.4 %collective-permute-start.37 = (bf16[512,2048]{1,0:T(8,128)(2,1)}, bf16[512,2048]{1,0:T(8,128)(2,1)}, u32[]{:S(2)}, u32[]{:S(2)}) collective-permute-start(bf16[512,2048]{1,0:T(8,128)(2,1)} %constant_dynamic-update-slice_fusion.22.refs_2_), channel_id=1, source_target_pairs={{0,2},{2,0},{4,6},{6,4},{8,10},{10,8},{12,14},{14,12},{16,18},{18,... | collective-permute-start | bytes 6291464 | tf_op jit(solution)/shard_map/ppermute | solution.py:778
  179.1 17.4 %collective-permute-start.38 = (bf16[512,2048]{1,0:T(8,128)(2,1)S(1)}, bf16[512,2048]{1,0:T(8,128)(2,1)}, u32[]{:S(2)}, u32[]{:S(2)}) collective-permute-start(bf16[512,2048]{1,0:T(8,128)(2,1)S(1)} %constant_dynamic-update-slice_fusion.38.refs_4_), channel_id=1, source_target_pairs={{0,2},{2,0},{4,6},{6,4},{8,10},{10,8},{12,14},{14,12},{16,18},{18,... | collective-permute-start | bytes 6291464 | tf_op jit(solution)/shard_map/ppermute | solution.py:778
  196.5 21.4 %collective-permute-start.39 = (bf16[256,1024]{1,0:T(8,128)(2,1)S(1)}, bf16[256,1024]{1,0:T(8,128)(2,1)S(1)}, u32[]{:S(2)}, u32[]{:S(2)}) collective-permute-start(bf16[256,1024]{1,0:T(8,128)(2,1)S(1)} %get-tuple-element.391), channel_id=1, source_target_pairs={{0,1},{1,0},{2,3},{3,2},{4,5},{5,4},{6,7},{7,6},{8,9},{9,8},{10,11... | collective-permute-start | bytes 1572872 | tf_op jit(solution)/shard_map/ppermute | solution.py:778
  265.7 24.8 %collective-permute-start.41 = (bf16[512,4096]{1,0:T(8,128)(2,1)}, bf16[512,4096]{1,0:T(8,128)(2,1)}, u32[]{:S(2)}, u32[]{:S(2)}) collective-permute-start(bf16[512,4096]{1,0:T(8,128)(2,1)} %pad_maximum_fusion.refs_14_), channel_id=1, source_target_pairs={{0,2},{2,0},{4,6},{6,4},{8,10},{10,8},{12,14},{14,12},{16,18},{18,... | collective-permute-start | bytes 12582920 | tf_op jit(solution)/shard_map/ppermute | solution.py:778
  269.5 66.6 %collective-permute-start.40 = (bf16[256,1024]{1,0:T(8,128)(2,1)}, bf16[256,1024]{1,0:T(8,128)(2,1)}, u32[]{:S(2)}, u32[]{:S(2)}) collective-permute-start(bf16[256,1024]{1,0:T(8,128)(2,1)} %get-tuple-element.405), channel_id=1, source_target_pairs={{0,1},{1,0},{2,3},{3,2},{4,5},{5,4},{6,7},{7,6},{8,9},{9,8},{10,11... | collective-permute-start | bytes 1572872 | tf_op jit(solution)/shard_map/ppermute | solution.py:778
  292.5 23.0 %collective-permute-start.42 = (bf16[512,1024]{1,0:T(8,128)(2,1)S(1)}, bf16[512,1024]{1,0:T(8,128)(2,1)S(1)}, u32[]{:S(2)}, u32[]{:S(2)}) collective-permute-start(bf16[512,1024]{1,0:T(8,128)(2,1)S(1)} %convolution_convert_fusion.5.refs_4_), channel_id=1, source_target_pairs={{0,2},{2,0},{4,6},{6,4},{8,10},{10,8},{12,14},{14,12},{16,18},{18,... | collective-permute-start | bytes 3145736 | tf_op jit(solution)/shard_map/ppermute | solution.py:778
  338.4 63.6 %collective-permute-start.44 = (bf16[128,4096]{1,0:T(8,128)(2,1)}, bf16[128,4096]{1,0:T(8,128)(2,1)S(1)}, u32[]{:S(2)}, u32[]{:S(2)}) collective-permute-start(bf16[128,4096]{1,0:T(8,128)(2,1)} %get-tuple-element.454.refs_3_), channel_id=1, source_target_pairs={{0,4},{2,6},{4,0},{6,2},{8,12},{10,14},{12,8},{14,10},{16,20},{18,... | collective-permute-start | bytes 3145736 | tf_op jit(solution)/shard_map/ppermute | solution.py:778
  338.6 63.3 %collective-permute-start.45 = (bf16[256,2048]{1,0:T(8,128)(2,1)}, bf16[256,2048]{1,0:T(8,128)(2,1)S(1)}, u32[]{:S(2)}, u32[]{:S(2)}) collective-permute-start(bf16[256,2048]{1,0:T(8,128)(2,1)} %get-tuple-element.455), channel_id=1, source_target_pairs={{0,1},{1,0},{2,3},{3,2},{4,5},{5,4},{6,7},{7,6},{8,9},{9,8},{10,11... | collective-permute-start | bytes 3145736 | tf_op jit(solution)/shard_map/ppermute | solution.py:778
  339.5 46.5 %collective-permute-start.57 = (bf16[4,2,16,128]{3,2,0,1:T(8,128)(2,1)S(1)}, bf16[4,2,16,128]{3,2,0,1:T(8,128)(2,1)S(1)}, u32[]{:S(2)}, u32[]{:S(2)}) collective-permute-start(bf16[4,2,16,128]{3,2,0,1:T(8,128)(2,1)S(1)} %fusion.14), channel_id=1, source_target_pairs={{0,4},{2,6},{4,0},{6,2},{8,12},{10,14},{12,8},{14,10},{16,20},{18,... | collective-permute-start | bytes 98312 | tf_op jit(solution)/shard_map/ppermute | solution.py:778
  395.8 34.5 %collective-permute-start.43 = (bf16[512,3072]{1,0:T(8,128)(2,1)S(1)}, bf16[512,3072]{1,0:T(8,128)(2,1)S(1)}, u32[]{:S(2)}, u32[]{:S(2)}) collective-permute-start(bf16[512,3072]{1,0:T(8,128)(2,1)S(1)} %pad_maximum_fusion.1), channel_id=1, source_target_pairs={{0,2},{2,0},{4,6},{6,4},{8,10},{10,8},{12,14},{14,12},{16,18},{18,... | collective-permute-start | bytes 9437192 | tf_op jit(solution)/shard_map/ppermute | solution.py:778
  411.6 18.7 %collective-permute-start.67 = (bf16[128,2048]{1,0:T(8,128)(2,1)S(1)}, bf16[128,2048]{1,0:T(8,128)(2,1)S(1)}, u32[]{:S(2)}, u32[]{:S(2)}) collective-permute-start(bf16[128,2048]{1,0:T(8,128)(2,1)S(1)} %add_convert_fusion.2.refs_4_), channel_id=1, source_target_pairs={{0,1},{1,0},{2,3},{3,2},{4,5},{5,4},{6,7},{7,6},{8,9},{9,8},{10,11... | collective-permute-start | bytes 1572872 | tf_op jit(solution)/shard_map/ppermute | solution.py:778
  412.3 18.0 %collective-permute-start.68 = (bf16[128,2048]{1,0:T(8,128)(2,1)S(1)}, bf16[128,2048]{1,0:T(8,128)(2,1)}, u32[]{:S(2)}, u32[]{:S(2)}) collective-permute-start(bf16[128,2048]{1,0:T(8,128)(2,1)S(1)} %add_convert_fusion.1), channel_id=1, source_target_pairs={{0,4},{2,6},{4,0},{6,2},{8,12},{10,14},{12,8},{14,10},{16,20},{18,... | collective-permute-start | bytes 1572872 | tf_op jit(solution)/shard_map/ppermute | solution.py:778
  439.7 18.1 %collective-permute-start.48 = (bf16[128,3072]{1,0:T(8,128)(2,1)}, bf16[128,3072]{1,0:T(8,128)(2,1)S(1)}, u32[]{:S(2)}, u32[]{:S(2)}) collective-permute-start(bf16[128,3072]{1,0:T(8,128)(2,1)} %get-tuple-element.462.refs_8_), channel_id=1, source_target_pairs={{0,4},{2,6},{4,0},{6,2},{8,12},{10,14},{12,8},{14,10},{16,20},{18,... | collective-permute-start | bytes 2359304 | tf_op jit(solution)/shard_map/ppermute | solution.py:778
  439.8 18.1 %collective-permute-start.49 = (bf16[256,1536]{1,0:T(8,128)(2,1)}, bf16[256,1536]{1,0:T(8,128)(2,1)S(1)}, u32[]{:S(2)}, u32[]{:S(2)}) collective-permute-start(bf16[256,1536]{1,0:T(8,128)(2,1)} %get-tuple-element.463), channel_id=1, source_target_pairs={{0,1},{1,0},{2,3},{3,2},{4,5},{5,4},{6,7},{7,6},{8,9},{9,8},{10,11... | collective-permute-start | bytes 2359304 | tf_op jit(solution)/shard_map/ppermute | solution.py:778
  460.3 28.5 %collective-permute-start.70 = (bf16[64,2048]{1,0:T(8,128)(2,1)S(1)}, bf16[64,2048]{1,0:T(8,128)(2,1)S(1)}, u32[]{:S(2)}, u32[]{:S(2)}) collective-permute-start(bf16[64,2048]{1,0:T(8,128)(2,1)S(1)} %get-tuple-element.512), channel_id=1, source_target_pairs={{0,16},{2,18},{4,20},{6,22},{8,24},{10,26},{12,28},{14,30},{16,0},... | collective-permute-start | bytes 786440 | tf_op jit(solution)/shard_map/ppermute | solution.py:938
  465.7 28.9 %collective-permute-start.69 = (bf16[64,2048]{1,0:T(8,128)(2,1)S(1)}, bf16[64,2048]{1,0:T(8,128)(2,1)S(1)}, u32[]{:S(2)}, u32[]{:S(2)}) collective-permute-start(bf16[64,2048]{1,0:T(8,128)(2,1)S(1)} %slice.431), channel_id=1, source_target_pairs={{0,24},{2,26},{4,28},{6,30},{8,0},{10,2},{12,4},{14,6},{16,8},{18,... | collective-permute-start | bytes 786440 | tf_op jit(solution)/shard_map/ppermute | solution.py:938
  467.3 28.2 %collective-permute-start.50 = (bf16[256,1024]{1,0:T(8,128)(2,1)S(1)}, bf16[256,1024]{1,0:T(8,128)(2,1)S(1)}, u32[]{:S(2)}, u32[]{:S(2)}) collective-permute-start(bf16[256,1024]{1,0:T(8,128)(2,1)S(1)} %get-tuple-element.505), channel_id=1, source_target_pairs={{0,1},{1,0},{2,3},{3,2},{4,5},{5,4},{6,7},{7,6},{8,9},{9,8},{10,11... | collective-permute-start | bytes 1572872 | tf_op jit(solution)/shard_map/ppermute | solution.py:778
  468.0 28.7 %collective-permute-start.55 = (bf16[64,1536]{1,0:T(8,128)(2,1)S(1)}, bf16[64,1536]{1,0:T(8,128)(2,1)S(1)}, u32[]{:S(2)}, u32[]{:S(2)}) collective-permute-start(bf16[64,1536]{1,0:T(8,128)(2,1)S(1)} %get-tuple-element.515), channel_id=1, source_target_pairs={{0,8},{2,10},{4,12},{6,14},{8,16},{10,18},{12,20},{14,22},{16,24},... | collective-permute-start | bytes 589832 | tf_op jit(solution)/shard_map/ppermute | solution.py:938
  470.5 27.4 %collective-permute-start.54 = (bf16[64,1536]{1,0:T(8,128)(2,1)S(1)}, bf16[64,1536]{1,0:T(8,128)(2,1)S(1)}, u32[]{:S(2)}, u32[]{:S(2)}) collective-permute-start(bf16[64,1536]{1,0:T(8,128)(2,1)S(1)} %get-tuple-element.514), channel_id=1, source_target_pairs={{0,16},{2,18},{4,20},{6,22},{8,24},{10,26},{12,28},{14,30},{16,0},... | collective-permute-start | bytes 589832 | tf_op jit(solution)/shard_map/ppermute | solution.py:938
  488.7 13.3 %collective-permute-start.53 = (bf16[64,1536]{1,0:T(8,128)(2,1)S(1)}, bf16[64,1536]{1,0:T(8,128)(2,1)S(1)}, u32[]{:S(2)}, u32[]{:S(2)}) collective-permute-start(bf16[64,1536]{1,0:T(8,128)(2,1)S(1)} %slice.432), channel_id=1, source_target_pairs={{0,24},{2,26},{4,28},{6,30},{8,0},{10,2},{12,4},{14,6},{16,8},{18,... | collective-permute-start | bytes 589832 | tf_op jit(solution)/shard_map/ppermute | solution.py:938
  (84 other events, 1035.3 us)
Sparse Core Ops, SparseCore 0:
  44.2 104.4 all-gather.1
  265.9 149.4 reduce-scatter.1

commit v2 on v1

--- a/solution.py
+++ b/solution.py
@@ -298,91 +298,80 @@
     )
 
 
-def up_body(place, a_ref, w00, w10, w01, w11, b_ref, h_ref, g_ref, acc, *, half):
-    j = pl.program_id(0)
-    k = w00.shape[0]
-
-    def go(w0, w1):
-        new = dot(a_ref[:, :k], w0[...]) + dot(a_ref[:, k:], w1[...])
-        v = acc[...]
-        cdf, density = gelu_terms(v)
-        h_ref[...] = (v * cdf).astype(BF)
-        g_ref[...] = (cdf + v * density).astype(BF)
-        acc[...] = new + b_ref[...]
-
-    @pl.when(j < half)
-    def _():
-        go(w00, w10)
-
-    @pl.when(j >= half)
-    def _():
-        go(w01, w11)
-
-
-def up_gelu(a, w, bias, place, block, deps=()):
+def up_body(a_ref, w_ref, b_ref, h_ref, g_ref, acc):
+    new = dot(a_ref[...], w_ref[...])
+    v = acc[...]
+    cdf, density = gelu_terms(v)
+    h_ref[...] = (v * cdf).astype(BF)
+    g_ref[...] = (cdf + v * density).astype(BF)
+    acc[...] = new + b_ref[...]
+
+
+def up_gelu(a, w, bias, block, deps=()):
     rows, width = a.shape
-    cols = w[0][0].shape[1]
-    half = cols // block
-    end = 2 * half - 1
-    out = jax.ShapeDtypeStruct((rows, 2 * cols), BF)
-
-    def where(j, place):
-        j = jnp.maximum(j - 1, 0)
-        return (0, (j + place[0] * half) % (2 * half))
-
-    spot = pl.BlockSpec((rows, block), where)
-    low = pl.BlockSpec((width // 2, block), lambda j, place: (0, jnp.minimum(j, half - 1)))
-    high = pl.BlockSpec((width // 2, block), lambda j, place: (0, jnp.clip(j - half, 0, half - 1)))
-    return kernel(
-        functools.partial(up_body, half=half),
+    cols = w.shape[1]
+    end = cols // block - 1
+    out = jax.ShapeDtypeStruct((rows, cols), BF)
+    spot = pl.BlockSpec((rows, block), lambda j: (0, jnp.maximum(j - 1, 0)))
+    return kernel(
+        up_body,
         "up_gelu",
-        (2 * half + 1,),
-        [pl.BlockSpec((rows, width), lambda j, place: (0, 0))]
-            + [low, low, high, high]
-            + [pl.BlockSpec((1, block), lambda j, place: (0, jnp.minimum(j, end)))],
+        (end + 2,),
+        [
+            whole_of(a),
+            pl.BlockSpec((width, block), lambda j: (0, jnp.minimum(j, end))),
+            pl.BlockSpec((1, block), lambda j: (0, jnp.minimum(j, end))),
+        ],
         [spot, spot],
         [out, out],
-        (place, a, w[0][0], w[1][0], w[0][1], w[1][1], bias,),
+        (a, w, bias),
         scratch=[pltpu.VMEM((rows, block), F32)],
-        prefetch=1,
-        deps=deps,
-    )
-
-
-def down_grad_body(place, a_ref, w_ref, g_ref, d_ref, s_ref):
+        deps=deps,
+    )
+
+
+def matmul_body(a_ref, w_ref, o_ref):
+    o_ref[...] = dot(a_ref[...], w_ref[...]).astype(o_ref.dtype)
+
+
+def matmul(a, w, block, dtype, deps=()):
+    return kernel(
+        matmul_body,
+        "matmul",
+        (w.shape[1] // block,),
+        [whole_of(a), pl.BlockSpec((w.shape[0], block), lambda j: (0, j))],
+        pl.BlockSpec((a.shape[0], block), lambda j: (0, j)),
+        jax.ShapeDtypeStruct((a.shape[0], w.shape[1]), dtype),
+        (a, w),
+        deps=deps,
+    )
+
+
+def down_grad_body(a_ref, w_ref, g_ref, d_ref, s_ref):
     d = dot(a_ref[...], w_ref[...], ((1,), (1,)))
     d = (d * g_ref[...].astype(F32)).astype(BF)
     d_ref[...] = d
     s_ref[...] = jnp.sum(d.astype(F32), axis=0, keepdims=True)
 
 
-def down_grad(a, w, g, place, block, part, deps=()):
+def down_grad(a, w, g, block, deps=()):
     rows, width = a.shape
-    cols = g.shape[1] // 2
-    steps = cols // block
-
-    def at(j, place):
-        return (j + (place[0] ^ part) * steps)
-
+    cols = g.shape[1]
     return kernel(
         down_grad_body,
         "down_grad",
-        (steps,),
+        (cols // block,),
         [
-                pl.BlockSpec((rows, width), lambda j, place: (0, 0)),
-                pl.BlockSpec((block, width), lambda j, place: (at(j, place), 0)),
-                pl.BlockSpec((rows, block), lambda j, place: (0, at(j, place))),
-            ],
+            whole_of(a),
+            pl.BlockSpec((block, width), lambda j: (j, 0)),
+            pl.BlockSpec((rows, block), lambda j: (0, j)),
+        ],
         [
-                pl.BlockSpec((rows, block), lambda j, place: (0, j)),
-                pl.BlockSpec((1, block), lambda j, place: (0, j)),
-            ],
-        [
-            jax.ShapeDtypeStruct((rows, cols), BF),
-            jax.ShapeDtypeStruct((1, cols), F32),
+            pl.BlockSpec((rows, block), lambda j: (0, j)),
+            pl.BlockSpec((1, block), lambda j: (0, j)),
         ],
-        (place, a, w, g,),
-        prefetch=1,
+        [jax.ShapeDtypeStruct((rows, cols), BF), jax.ShapeDtypeStruct((1, cols), F32)],
+        (a, w, g),
         deps=deps,
     )
 
@@ -499,7 +488,7 @@
         s_ref[...] += sums
 
 
-def mix_body(c0, c1, s_ref, w0, w1, pc, pi, v_ref, zh_ref, r_ref, m_ref, mr_ref, x_ref):
+def mix_body(c0, c1, s_ref, w0, w1, pc, v_ref, zh_ref, r_ref, m_ref, mr_ref, x_ref):
     h = w0.shape[0]
     ctx = dot(c0[...], pc[:h, :]) + dot(c1[...], pc[h:, :])
     ctx = ctx.astype(BF)
@@ -510,10 +499,10 @@
     r_ref[...] = jnp.broadcast_to(r, r_ref.shape)
     mixed = zhat * v_ref[0:1, :] + v_ref[2:3, :]
     m_ref[...] = mixed
-    mr_ref[...] = dot(mixed.astype(BF), pi[...]).astype(BF)
-
-
-def mix(c0, c1, stream, w0, w1, perm_ctx, perm_in, vecs, tile, deps=()):
+    mr_ref[...] = mixed.astype(BF)
+
+
+def mix(c0, c1, stream, w0, w1, perm_ctx, vecs, tile, deps=()):
     rows, width = stream.shape
     full = jax.ShapeDtypeStruct((rows, width), F32)
     low = jax.ShapeDtypeStruct((rows, width), BF)
@@ -523,16 +512,16 @@
         "mix",
         (rows // tile,),
         [tile_of(v, tile) for v in (c0, c1, stream)]
-        + [whole_of(v) for v in (w0, w1, perm_ctx, perm_in, vecs)],
+        + [whole_of(v) for v in (w0, w1, perm_ctx, vecs)],
         [tile_of(v, tile) for v in outs],
         outs,
-        (c0, c1, stream, w0, w1, perm_ctx, perm_in, vecs,),
-        deps=deps,
-    )
-
-
-def turn_body(h_ref, w_ref, m_ref, c_ref, l_ref, v_ref, o_ref, g_ref, gb_ref, s_ref):
-    branch = dot(h_ref[...], w_ref[...]) + v_ref[5:6, :]
+        (c0, c1, stream, w0, w1, perm_ctx, vecs,),
+        deps=deps,
+    )
+
+
+def turn_body(p_ref, t_ref, m_ref, c_ref, l_ref, v_ref, o_ref, g_ref, gb_ref, s_ref):
+    branch = p_ref[...] + t_ref[...].astype(F32) + v_ref[5:6, :]
     zhat, r = norm_of(m_ref[...] + branch)
     gain = v_ref[1:2, :]
     o_ref[...] = (zhat * gain + v_ref[4:5, :]).astype(BF)
@@ -544,34 +533,27 @@
     gather_sums(s_ref, seed * zhat, seed, low.astype(F32))
 
 
-def turn(h, w, mixed, cot, live, vecs, tile, deps=()):
+def turn(part, theirs, mixed, cot, live, vecs, tile, deps=()):
     rows, width = mixed.shape
     full = jax.ShapeDtypeStruct((rows, width), F32)
     low = jax.ShapeDtypeStruct((rows, width), BF)
     sums = jax.ShapeDtypeStruct((8, width), F32)
+    tiled = (part, theirs, mixed, cot, live)
     return kernel(
         turn_body,
         "turn",
         (rows // tile,),
-        [tile_of(h, tile), whole_of(w)]
-        + [tile_of(v, tile) for v in (mixed, cot, live)]
-        + [whole_of(vecs)],
+        [tile_of(v, tile) for v in tiled] + [whole_of(vecs)],
         [tile_of(v, tile) for v in (low, full, low)] + [whole_of(sums)],
         [low, full, low, sums],
-        (h, w, mixed, cot, live, vecs,),
-        deps=deps,
-    )
-
-
-def unmix_body(
-    d0, d1, w00, w10, w01, w11, pi, g2, zh, r_ref, wo0, wo1, pc, v_ref, g1_ref, ga_ref, gc_ref, s_ref
-):
+        (*tiled, vecs),
+        deps=deps,
+    )
+
+
+def unmix_body(p_ref, t_ref, g2, zh, r_ref, wo0, wo1, pc, v_ref, g1_ref, ga_ref, gc_ref, s_ref):
     nt = ((1,), (1,))
-    parts = [
-        dot(d0[...], u[...], nt) + dot(d1[...], v[...], nt) for u, v in ((w00, w01), (w10, w11))
-    ]
-    back = jnp.concatenate(parts, axis=1).astype(BF)
-    grad = g2[...] + dot(back, pi[...], nt)
+    grad = g2[...] + p_ref[...] + t_ref[...].astype(F32)
     zhat = zh[...]
     g1 = norm_grad(grad, zhat, r_ref[:, 0:1], v_ref[0:1, :])
     g1_ref[...] = g1
@@ -582,23 +564,21 @@
     gather_sums(s_ref, grad * zhat, grad, low.astype(F32))
 
 
-def unmix(d0, d1, w, perm_in, g2, zhat, r, wo0, wo1, perm_ctx, vecs, tile, deps=()):
+def unmix(part, theirs, g2, zhat, r, wo0, wo1, perm_ctx, vecs, tile, deps=()):
     rows, width = g2.shape
     full = jax.ShapeDtypeStruct((rows, width), F32)
     low = jax.ShapeDtypeStruct((rows, width), BF)
     sums = jax.ShapeDtypeStruct((8, width), F32)
-    ws = (w[0][0], w[1][0], w[0][1], w[1][1])
+    tiled = (part, theirs, g2, zhat, r)
+    fixed = (wo0, wo1, perm_ctx, vecs)
     return kernel(
         unmix_body,
         "unmix",
         (rows // tile,),
-        [tile_of(d0, tile), tile_of(d1, tile)]
-        + [whole_of(v) for v in ws + (perm_in,)]
-        + [tile_of(v, tile) for v in (g2, zhat, r)]
-        + [whole_of(v) for v in (wo0, wo1, perm_ctx, vecs)],
+        [tile_of(v, tile) for v in tiled] + [whole_of(v) for v in fixed],
         [tile_of(v, tile) for v in (full, low, low)] + [whole_of(sums)],
         [full, low, low, sums],
-        (d0, d1, *ws, perm_in, g2, zhat, r, wo0, wo1, perm_ctx, vecs,),
+        tiled + fixed,
         deps=deps,
     )
 
@@ -739,6 +719,22 @@
     )
 
 
+def tie_body(*refs):
+    pass
+
+
+def tie(values, deps=()):
+    spot = pl.BlockSpec(memory_space=pl.ANY)
+    return pl.pallas_call(
+        tie_body,
+        in_specs=[spot] * (len(values) + len(deps)),
+        out_specs=[spot] * len(values),
+        out_shape=[jax.ShapeDtypeStruct(v.shape, v.dtype) for v in values],
+        input_output_aliases={i: i for i in range(len(values))},
+        name="tie",
+    )(*values, *deps)
+
+
 class Order:
     def __init__(self):
         self.token = jnp.zeros((8, 128), F32)
@@ -859,7 +855,7 @@
         sm = sm.transpose(0, 1, 3, 2, 4, 5).reshape(dp, 2, 16, lanes)
         sm = jnp.einsum("nr,rxql->nxql", rel_at, sm, preferred_element_type=F32)
         vecs = sm[:, 0, 1:9, :dw].transpose(1, 0, 2).reshape(8, width)
-        bias_up = sm[:, :, 0].transpose(1, 0, 2).reshape(1, -1)
+        bias_up = sm[:, 0, 0].reshape(1, -1)
         bias = sm[:, :, 7:9, :bw].transpose(2, 1, 0, 3).reshape(2, 2, groups, 1, lanes)
         bias = jnp.concatenate([bias[0], jnp.zeros_like(bias[0]), bias[1]], axis=2)
         return vecs, bias_up, bias.reshape(1, -1)
@@ -867,18 +863,18 @@
     q1, q2, q3 = along_z(qs)
     theirs = send("x", other(stream))
     t1, t2, t3 = along_z(small)
-    q1, q2, q3 = at(q1, q2, q3)
+    q1, q2, q3, perm_in, perm_ctx = tie([q1, q2, q3, perm_in, perm_ctx], [theirs, t1, t2, t3])
     qa, qb = rows_cat(qs, q1), rows_cat(q2, q3)
     qax, qby = send("x", qa), send("y", qb)
     o1, o2, o3 = along_z(w_out)
-    t1, t2, t3 = at(t1, t2, t3)
     sm = jnp.stack([small, t1, t2, t3])
     tx = send("x", sm)
     theirs = at(theirs)
     own_seq = rows_cat(mine(stream), theirs)
     stream_rel = dot(own_seq, perm_in).astype(BF)
-    i1, i2, i3 = along_z(w_in)
-    wb = lax.all_gather(at(w_back), ("tensor", "dp"), axis=0, tiled=True)
+    in_shard, back_shard = tie([w_in, w_back], [q1, q2, q3])
+    wi = lax.all_gather(in_shard, "dp", axis=0, tiled=True)
+    wb = lax.all_gather(back_shard, "dp", axis=0, tiled=True)
     qax, qby = at(qax, qby)
     qay, qaxy, qbx, qbxy = send("y", qa), send("y", qax), send("x", qb), send("x", qby)
     tx = at(tx)
@@ -898,37 +894,32 @@
     oax, oby = send("x", oa), send("y", ob)
     tc = at(tc)
     vecs, bias_up, bias_proj = unpack(jnp.stack([sm, tc]))
-    i1, i2, i3 = at(i1, i2, i3)
-    ia, ib = rows_cat(w_in, i1), rows_cat(i2, i3)
-    iax, iby = send("x", ia), send("y", ib)
     q10, q11, bias_proj, vecs, bias_up = at(q10, q11, bias_proj, vecs, bias_up)
     wq = [[q00, q01], [q10, q11]]
     proj = at(project(at(stream_rel), wq, bias_proj, 3 * lanes))
-    oax, oby, iax, iby = at(oax, oby, iax, iby)
-    oay, oaxy, obx, obxy = send("y", oa), send("y", oax), send("x", ob), send("x", oby)
-    iay, ibx = send("y", ia), send("x", ib)
-    ctx0 = at(attend(info, at(proj), lanes, 0))
-    oay, oaxy, obx, obxy, iay, ibx = at(oay, oaxy, obx, obxy, iay, ibx)
-    wo0 = rows_cat(oa, oax, oay, oaxy, ob, oby, obx, obxy)
+    oax, oby, far = tie([oax, oby, other(cotangent)], [proj])
+    oa, ob = rows_cat(oa, oax), rows_cat(ob, oby)
+    oya, oxb = send("y", oa), send("x", ob)
+    ctx0 = attend(info, proj, lanes, 0, deps=[oa, ob])
+    oya, oxb = tie([oya, oxb], [ctx0])
+    wo0 = rows_cat(oa, oya, ob, oxb)
     wo1 = send("c", wo0)
-    iaxy, ibxy = send("y", iax), send("x", iby)
-    ctx1 = at(attend(info, at(proj), lanes, 1))
-    wo1, iaxy, ibxy = at(wo1, iaxy, ibxy)
-    i00, i01 = rows_cat(ia, iay, ib, iby), rows_cat(iax, iaxy, ibx, ibxy)
-    i10, i11 = send("c", i00), send("c", i01)
+    cot_theirs = send("x", far)
+    ctx1 = attend(info, proj, lanes, 1, deps=[wo0])
     tile = own // 2
-    zhat1, r1, mixed, mixed_rel, ctx_rel = mix(
-        at(ctx0), ctx1, own_seq, wo0, wo1, perm_ctx, perm_in, vecs, tile
-    )
-    i10, i11, mixed_rel = at(i10, i11, mixed_rel)
-    cot_theirs = send("x", other(cotangent))
-    wi = [[i00, i01], [i10, i11]]
     block = 2 * lanes
-    hidden, slope = up_gelu(at(mixed_rel), wi, bias_up, place, block)
-    hidden, cot_theirs, wb = at(hidden, cot_theirs, wb)
+    zhat1, r1, mixed, m_own, ctx_rel = mix(
+        ctx0, ctx1, own_seq, wo0, wo1, perm_ctx, vecs, tile, deps=[cot_theirs]
+    )
+    m_far = send("x", m_own)
+    h_own, g_own = up_gelu(m_own, wi, bias_up, block)
+    h_far, g_far = up_gelu(m_far, wi, bias_up, block, deps=[h_own])
+    p_far = matmul(h_far, wb, 2 * block, BF)
+    p_theirs = send("x", p_far)
+    p_own = matmul(h_own, wb, 2 * block, F32, deps=[p_far])
     cot = rows_cat(mine(cotangent), cot_theirs)
     live = jnp.broadcast_to(live[:, None], (rows, lanes))
-    result, grad_sum2, grad_branch, sums2 = turn(hidden, wb, mixed, cot, live, vecs, tile)
+    result, grad_sum2, gb_own, sums2 = turn(p_own, p_theirs, mixed, cot, live, vecs, tile)
 
     def whole(both, got):
         return jnp.where(x == 0, jnp.stack([both, got]), jnp.stack([got, both]))
@@ -961,26 +952,25 @@
         got = at(*got)
         return add(a, got[0]), add(b, got[1]), n
 
-    grad_branch, hidden = at(grad_branch, hidden)
-    back = dot(hidden, grad_branch, TN).astype(BF)
-    back_done = lax.psum_scatter(at(back), ("tensor", "dp"), scatter_dimension=0, tiled=True)
+    nt = ((1,), (1,))
+    gb_far = send("x", gb_own)
+    d_own, us0 = down_grad(gb_own, wb, g_own, block)
+    d_far, us1 = down_grad(gb_far, wb, g_far, block, deps=[d_own])
+    dm_far = dot(d_far, wi, nt).astype(BF)
+    dm_theirs = send("x", dm_far)
+    back = (dot(h_own, gb_own, TN) + dot(h_far, gb_far, TN)).astype(BF)
+    back_done = lax.psum_scatter(back, "dp", scatter_dimension=0, tiled=True)
+    dm_own = dot(d_own, wi, nt)
+    grad_sum1, grad_att, grad_ctx, sums1 = unmix(
+        dm_own, dm_theirs, grad_sum2, zhat1, r1, wo0, wo1, perm_ctx, vecs, own, deps=[back]
+    )
+    inner = (dot(m_own, d_own, TN) + dot(m_far, d_far, TN)).astype(BF)
+    in_done = lax.psum_scatter(inner, "dp", scatter_dimension=0, tiled=True)
     lo_theirs = send("x", result[own:])
-    di0, us0 = down_grad(at(grad_branch), wb, slope, place, block, 0)
-    di1, us1 = down_grad(at(grad_branch), wb, slope, place, block, 1)
-    di0, di1 = at(di0, di1)
-    m0, m1 = half_cols(mixed_rel)
-    i_core = jnp.concatenate([dot(m1, r, TN).astype(BF) for r in (di0, di1)], axis=1)
-    i_got = send("c", i_core)
-    grad_sum1, grad_att, grad_ctx, sums1 = unmix(
-        at(di0), di1, wi, perm_in, grad_sum2, zhat1, r1, wo0, wo1, perm_ctx, vecs, own, deps=[i_core]
-    )
-    grad_att, i_got = at(grad_att, i_got)
-    ik_a, is_a, ik_b, is_b = weight_cols(m0, di0, di1, i_got, deps=[grad_att])
-    ia_got, ib_got = send("y", is_a), send("x", is_b)
     c0, c1 = half_cols(ctx_rel)
     o_core = dot(c1, grad_att, TN).astype(BF)
     o_got = send("c", o_core)
-    dp0, ps0 = attend_grad(info, proj, at(grad_ctx), lanes, 0, deps=[is_a, o_core])
+    dp0, ps0 = attend_grad(info, proj, at(grad_ctx), lanes, 0, deps=[inner, o_core])
     dp0, o_got = at(dp0, o_got)
     ok_a, os_a, ok_b, os_b = weight_rows(c0, grad_att, o_got, deps=[dp0])
     oa_got, ob_got = send("y", os_a), send("x", os_b)
@@ -989,22 +979,19 @@
     s0, s1 = half_cols(stream_rel)
     q_core = jnp.concatenate([dot(s1, r, TN).astype(BF) for r in (dp0, dp1)], axis=1)
     q_got = send("c", q_core)
-    ia_got, ib_got, oa_got, ob_got = at(ia_got, ib_got, oa_got, ob_got)
-    i_join = join_cols(ik_a, ik_b, ia_got, ib_got)
     o_join = join_rows(ok_a, ok_b, oa_got, ob_got)
-    qk_a, qs_a, qk_b, qs_b = weight_cols(s0, dp0, dp1, at(q_got), deps=[i_join[3], o_join[3]])
+    qk_a, qs_a, qk_b, qs_b = weight_cols(s0, dp0, dp1, q_got)
     qa_got, qb_got = send("y", qs_a), send("x", qs_b)
     grad_stream = stream_grad(dp0, dp1, wq, perm_in, grad_sum1, own, deps=[qs_a])
     grad_stream, qa_got, qb_got = at(grad_stream, qa_got, qb_got)
     q_join = join_cols(qk_a, qk_b, qa_got, qb_got)
-    in_done = finish(*joined(*i_join, w_in.shape[0]))
     out_done = finish(*joined(*o_join, w_out.shape[0]))
     gs_theirs = send("x", grad_stream[own:])
     qkv_done = finish(*joined(*q_join, qs.shape[0]))
 
     proj_sum = jnp.concatenate([ps0, ps1], axis=1).reshape(2, groups, 3, lanes)
     bias_grad = [proj_sum[:, :, j].reshape(2, dp, bw).transpose(1, 0, 2) for j in (0, 2)]
-    up_sum = jnp.concatenate([us0, us1], axis=1)
+    up_sum = jnp.stack([us0 + us1, jnp.zeros_like(us0)])
 
     def widen(v):
         return jnp.pad(v, ((0, 0), (0, 0), (0, lanes - v.shape[2])))
@@ -1021,6 +1008,7 @@
         "nr,nxql->rxql", rel_at.astype(F32), tiny, precision=lax.Precision.HIGHEST
     ).reshape(2, 2, 4, 2, 16, lanes)
 
+    (tiny,) = tie([tiny], [qs_a])
     tiny = tiny[0] + send("c", tiny[1].astype(BF)).astype(F32)
     tiny = tiny[0] + send("y", tiny[1].astype(BF)).astype(F32)
     tiny = tiny[:, 0] + send("x", tiny[:, 1].astype(BF)).astype(F32)
@@ -1034,7 +1022,7 @@
         qkv_done().reshape(-1, groups, 3, lanes).transpose(0, 2, 1, 3).reshape(w_qkv.shape),
         t[7:9, :bw].T,
         out_done(),
-        in_done(),
+        in_done.astype(F32),
         t[0],
         back_done.astype(F32),
         t[1:3, :dw].T,

time: 519 us -> 464 us (0.89)
  starting transfers between devices: 87.7 us -> 56.8 us
  waiting for transfers between devices: 155 us -> 126 us
  matrix products: 20 us -> 37.1 us
  Pallas kernels: 164 us -> 152 us
    ppermute x12 -> x9, waiting for transfers between devices: 30.5 us -> 9.76 us  [finish(): got = [lax.ppermute(v, *routes[-1 - i]) for i, v in enumerate(parts)]]
    dot_general x7 -> x10, matrix products: 18.8 us -> 36.6 us  [dot(): return lax.dot_general(a, b, (dims, ((), ())), preferred_element_type=F32)]
    ppermute x48 -> x37, starting transfers between devices: 41.3 us -> 29.6 us  [send(): return lax.ppermute(at(value), *routes[way])]
    pallas_call x15 -> x17, Pallas kernels: 164 us -> 152 us  [kernel(): pl.pallas_call(without_deps, grid_spec=pltpu.PrefetchScalarGridSpec(num_s...]
    ppermute x12 -> x9, starting transfers between devices: 25.8 us -> 14.9 us  [finish(): got = [lax.ppermute(v, *routes[-1 - i]) for i, v in enumerate(parts)]]
    unnamed x154 -> x184, local copies, waits for them, and re-layouts: 16.5 us -> 24.9 us
    ppermute x12 -> x9, starting transfers between devices: 20.5 us -> 12.2 us  [along_z(): return [lax.ppermute(value, *routes[k]) for k in range(1, 4)]]
    ppermute x12 -> x9, waiting for transfers between devices: 19.6 us -> 12.6 us  [along_z(): return [lax.ppermute(value, *routes[k]) for k in range(1, 4)]]
  transfers between devices with their start and end apart: 74 -> 59, of which waited for: 26 -> 23; matrix products, arithmetic and copies ran while one was open for 12% -> 18% of each run, Pallas kernels for 26% -> 29%
where the time goes in v2:
time: 464 us; the launch traced here: 458 us
  Pallas kernels  152 us (33%)
  waiting for transfers between devices  126 us (27%)
  starting transfers between devices  56.8 us (12%)
  local copies, waits for them, and re-layouts  49 us (11%)
  matrix products  37.1 us (8%)
  other arithmetic  21.2 us (5%)
  between operations  15.9 us (3%)
    pallas_call x17, Pallas kernels, kernel(): pl.pallas_call(without_deps, grid_spec=pltpu.PrefetchScalarGridSpec(num_s...  152 us
    ppermute x37, waiting for transfers between devices, send(): return lax.ppermute(at(value), *routes[way])  103 us
    dot_general x10, matrix products, dot(): return lax.dot_general(a, b, (dims, ((), ())), preferred_element_type=F32)  36.6 us
    ppermute x37, starting transfers between devices, send(): return lax.ppermute(at(value), *routes[way])  29.6 us
    unnamed x184, local copies, waits for them, and re-layouts  24.9 us
    ppermute x9, starting transfers between devices, finish(): got = [lax.ppermute(v, *routes[-1 - i]) for i, v in enumerate(parts)]  14.9 us
    ppermute x9, waiting for transfers between devices, along_z(): return [lax.ppermute(value, *routes[k]) for k in range(1, 4)]  12.6 us
    ppermute x9, starting transfers between devices, along_z(): return [lax.ppermute(value, *routes[k]) for k in range(1, 4)]  12.2 us
  transfers between devices with their start and end apart: 59, of which 23 were waited for; matrix products, arithmetic and copies ran while one was open for 18% of the time, Pallas kernels for 29%

profile of v2, /device:TPU:8, one launch (start us, length us, event | category | flops | bytes accessed | tf_op | source)
XLA Modules:
  0.0 457.6 jit_solution(10139933203492210422)
XLA Ops:
  16.7 3.5 collective-permute-start.2
  24.5 6.2 %collective-permute-done.1.refs_6_ = bf16[16,128]{1,0:T(8,128)(2,1)S(1)} collective-permute-done((bf16[16,128]{1,0:T(8,128)(2,1)S(1)}, bf16[16,128]{1,0:T(8,128)(2,1)S(1)}, u32[]{:S(2)}, u32[]{:S(2)}) %collective-permute-start.1) | collective-permute-done | bytes 4128 | tf_op jit(solution)/shard_map/ppermute | solution.py:778
  32.5 4.8 %collective-permute-done.3.refs_8_ = bf16[16,128]{1,0:T(8,128)(2,1)S(1)} collective-permute-done((bf16[16,128]{1,0:T(8,128)(2,1)S(1)}, bf16[16,128]{1,0:T(8,128)(2,1)S(1)}, u32[]{:S(2)}, u32[]{:S(2)}) %collective-permute-start.3) | collective-permute-done | bytes 4128 | tf_op jit(solution)/shard_map/ppermute | solution.py:778
  40.2 2.4 dynamic-slice_bitcast_fusion
  52.8 3.5 convolution_convert_fusion.2.refs_0_
  66.3 7.0 %collective-permute-done.12 = bf16[2,4,16,128]{3,2,1,0:T(8,128)(2,1)S(1)} collective-permute-done((bf16[2,4,16,128]{3,2,1,0:T(8,128)(2,1)S(1)}, bf16[2,4,16,128]{3,2,1,0:T(8,128)(2,1)S(1)}, u32[]{:S(2)}, u32[]{:S(2)}) %collective-permute-start.12) | collective-permute-done | bytes 32800 | tf_op jit(solution)/shard_map/ppermute | solution.py:774
  76.3 10.9 %collective-permute-done.17 = bf16[128,1536]{1,0:T(8,128)(2,1)S(1)} collective-permute-done((bf16[128,1536]{1,0:T(8,128)(2,1)S(1)}, bf16[128,1536]{1,0:T(8,128)(2,1)S(1)}, u32[]{:S(2)}, u32[]{:S(2)}) %collective-permute-start.17) | collective-permute-done | bytes 393248 | tf_op jit(solution)/shard_map/ppermute | solution.py:774
  92.7 2.5 collective-permute-start.22
  95.9 10.3 %project.1.refs_3_.refs_1_ = bf16[512,3072]{1,0:T(8,128)(2,1)} custom-call(bf16[512,1024]{1,0:T(8,128)(2,1)} %convolution_convert_fusion.2.refs_0_, bf16[512,1536]{1,0:T(8,128)(2,1)} %constant_dynamic-update-slice_fusion.4.refs_1_.refs_2_, bf16[512,1536]{1,0:T(8,128)(2,1)} %collective-permute-done.16.refs_2_.refs_3_, bf16[512,1536]{1,0:T(8,128)(2,1)} %copy-done.4, ...), custom_call_target="tpu_custom_call" | custom-call | tf_op jit(solution)/shard_map/project/pallas_call | solution.py:230
  115.2 9.5 %attend.2.refs_2_.refs_0_ = bf16[512,512]{1,0:T(8,128)(2,1)} custom-call(s32[2]{0:T(128)} %pad_add_fusion.refs_0_, bf16[512,3072]{1,0:T(8,128)(2,1)} %project.1.refs_3_.refs_1_, bf16[128,1024]{1,0:T(8,128)(2,1)} %get-tuple-element.228.refs_2_, bf16[128,1024]{1,0:T(8,128)(2,1)} %constant_dynamic-update-slice_fusion.17.refs_3_), custom_call_target="tpu_custom_call" | custom-call | tf_op jit(solution)/shard_map/attend/pallas_call | solution.py:230
  129.5 9.4 %attend.3.refs_1_ = bf16[512,512]{1,0:T(8,128)(2,1)} custom-call(s32[2]{0:T(128)} %pad_add_fusion.refs_0_, bf16[512,3072]{1,0:T(8,128)(2,1)} %project.1.refs_3_.refs_1_, bf16[512,1024]{1,0:T(8,128)(2,1)} %copy-done.2), custom_call_target="tpu_custom_call" | custom-call | tf_op jit(solution)/shard_map/attend/pallas_call | solution.py:230
  138.9 3.7 collective-permute-done.26.refs_7_
  143.8 8.6 %mix.1 = (f32[512,1024]{1,0:T(8,128)}, f32[512,128]{1,0:T(8,128)}, f32[512,1024]{1,0:T(8,128)}, bf16[512,1024]{1,0:T(8,128)(2,1)}, bf16[512,1024]{1,0:T(8,128)(2,1)}) custom-call(bf16[512,512]{1,0:T(8,128)(2,1)} %attend.2.refs_2_.refs_0_, bf16[512,512]{1,0:T(8,128)(2,1)} %attend.3.refs_1_, bf16[512,1024]{1,0:T(8,128)(2,1)} %pad_maximum_fusion.1.refs_2_, ...), custom_call_target="tpu_custom_call" | custom-call | tf_op jit(solution)/shard_map/mix/pallas_call | solution.py:230
  152.7 10.7 %up_gelu.2 = (bf16[512,2048]{1,0:T(8,128)(2,1)}, bf16[512,2048]{1,0:T(8,128)(2,1)}) custom-call(bf16[512,1024]{1,0:T(8,128)(2,1)} %get-tuple-element.246.refs_0_, bf16[1024,2048]{1,0:T(8,128)(2,1)} %all-gather.3.cloned.1.call-done.refs_1_, f32[1,2048]{1,0:T(1,128)} %bitcast.158), custom_call_target="tpu_custom_call" | custom-call | tf_op jit(solution)/shard_map/up_gelu/pallas_call | solution.py:230
  163.4 14.1 %collective-permute-done.27.refs_0_ = bf16[512,1024]{1,0:T(8,128)(2,1)S(1)} collective-permute-done((bf16[512,1024]{1,0:T(8,128)(2,1)}, bf16[512,1024]{1,0:T(8,128)(2,1)S(1)}, u32[]{:S(2)}, u32[]{:S(2)}) %collective-permute-start.27) | collective-permute-done | bytes 1048608 | tf_op jit(solution)/shard_map/ppermute | solution.py:774
  178.4 10.6 %up_gelu.3 = (bf16[512,2048]{1,0:T(8,128)(2,1)}, bf16[512,2048]{1,0:T(8,128)(2,1)}) custom-call(bf16[512,1024]{1,0:T(8,128)(2,1)} %copy-done.35, bf16[1024,2048]{1,0:T(8,128)(2,1)} %all-gather.3.cloned.1.call-done.refs_1_, f32[1,2048]{1,0:T(1,128)} %bitcast.159, bf16[512,2048]{1,0:T(8,128)(2,1)} %get-tuple-element.243.refs_3_.refs_0_), custom_call_target="tpu_custom_call" | custom-call | tf_op jit(solution)/shard_map/up_gelu/pallas_call | solution.py:230
  189.1 5.7 %matmul.2.refs_2_ = bf16[512,1024]{1,0:T(8,128)(2,1)} custom-call(bf16[512,2048]{1,0:T(8,128)(2,1)} %get-tuple-element.247.refs_0_, bf16[2048,1024]{1,0:T(8,128)(2,1)} %all-gather.5.cloned.1.call-done.refs_1_), custom_call_target="tpu_custom_call" | custom-call | tf_op jit(solution)/shard_map/matmul/pallas_call | solution.py:230
  197.7 5.7 %matmul.3.refs_0_ = f32[512,1024]{1,0:T(8,128)} custom-call(bf16[512,2048]{1,0:T(8,128)(2,1)} %get-tuple-element.243.refs_3_.refs_0_, bf16[2048,1024]{1,0:T(8,128)(2,1)} %all-gather.5.cloned.1.call-done.refs_1_, bf16[512,1024]{1,0:T(8,128)(2,1)} %matmul.2.refs_2_), custom_call_target="tpu_custom_call" | custom-call | tf_op jit(solution)/shard_map/matmul/pallas_call | solution.py:230
  203.4 15.6 %collective-permute-done.28.refs_1_ = bf16[512,1024]{1,0:T(8,128)(2,1)S(1)} collective-permute-done((bf16[512,1024]{1,0:T(8,128)(2,1)}, bf16[512,1024]{1,0:T(8,128)(2,1)S(1)}, u32[]{:S(2)}, u32[]{:S(2)}) %collective-permute-start.28) | collective-permute-done | bytes 1048608 | tf_op jit(solution)/shard_map/ppermute | solution.py:774
  220.1 6.6 %turn.1 = (bf16[512,1024]{1,0:T(8,128)(2,1)}, f32[512,1024]{1,0:T(8,128)}, bf16[512,1024]{1,0:T(8,128)(2,1)}, f32[8,1024]{1,0:T(8,128)}) custom-call(f32[512,1024]{1,0:T(8,128)} %matmul.3.refs_0_, bf16[512,1024]{1,0:T(8,128)(2,1)} %copy-done.30, f32[512,1024]{1,0:T(8,128)} %get-tuple-element.250.refs_2_, bf16[512,1024]{1,0:T(8,128)(2,1)} %pad_maximum_fusion.2.refs_3_, ...), custom_call_target="tpu_custom_call" | custom-call | tf_op jit(solution)/shard_map/turn/pallas_call | solution.py:230
  227.3 8.7 %down_grad.2 = (bf16[512,2048]{1,0:T(8,128)(2,1)}, f32[1,2048]{1,0:T(1,128)}) custom-call(bf16[512,1024]{1,0:T(8,128)(2,1)} %get-tuple-element.254.refs_0_, bf16[2048,1024]{1,0:T(8,128)(2,1)} %all-gather.5.cloned.1.call-done.refs_1_, bf16[512,2048]{1,0:T(8,128)(2,1)} %get-tuple-element.256.refs_2_), custom_call_target="tpu_custom_call" | custom-call | tf_op jit(solution)/shard_map/down_grad/pallas_call | solution.py:230
  236.0 14.0 %collective-permute-done.29.refs_0_ = bf16[512,1024]{1,0:T(8,128)(2,1)S(1)} collective-permute-done((bf16[512,1024]{1,0:T(8,128)(2,1)}, bf16[512,1024]{1,0:T(8,128)(2,1)S(1)}, u32[]{:S(2)}, u32[]{:S(2)}) %collective-permute-start.29) | collective-permute-done | bytes 1048608 | tf_op jit(solution)/shard_map/ppermute | solution.py:774
  251.0 9.2 %down_grad.3 = (bf16[512,2048]{1,0:T(8,128)(2,1)}, f32[1,2048]{1,0:T(1,128)}) custom-call(bf16[512,1024]{1,0:T(8,128)(2,1)} %copy-done.27, bf16[2048,1024]{1,0:T(8,128)(2,1)} %all-gather.5.cloned.1.call-done.refs_1_, bf16[512,2048]{1,0:T(8,128)(2,1)} %get-tuple-element.255.refs_2_, bf16[512,2048]{1,0:T(8,128)(2,1)} %get-tuple-element.257.refs_3_), custom_call_target="tpu_custom_call" | custom-call | tf_op jit(solution)/shard_map/down_grad/pallas_call | solution.py:230
  260.2 4.2 fusion.43
  264.4 4.7 %add_convert_fusion.refs_3_ = bf16[1024,2048]{1,0:T(8,128)(2,1)} fusion(f32[1024,2048]{1,0:T(8,128)S(1)} %fusion.43, bf16[512,1024]{1,0:T(8,128)(2,1)S(1)} %copy-done.25, bf16[512,2048]{1,0:T(8,128)(2,1)S(1)} %copy-done.17), kind=kOutput, calls=%fused_computation | convolution fusion | flops 2151677952 | bytes 15728640 | tf_op jit(solution)/shard_map/dot_general | solution.py:257
  275.7 7.0 %fusion.41.refs_0_ = f32[512,1024]{1,0:T(8,128)} fusion(bf16[512,2048]{1,0:T(8,128)(2,1)} %get-tuple-element.257.refs_3_, bf16[1024,2048]{1,0:T(8,128)(2,1)} %all-gather.3.cloned.1.call-done.refs_1_), kind=kOutput, calls=%fused_computation.181 | convolution fusion | flops 2147483648 | bytes 8388608 | tf_op jit(solution)/shard_map/dot_general | solution.py:257
  282.7 3.3 convolution_convert_fusion.4
  287.4 2.4 fusion.42
  289.8 4.6 %add_convert_fusion.1.refs_9_ = bf16[2048,1024]{1,0:T(8,128)(2,1)} fusion(f32[2048,1024]{1,0:T(8,128)S(1)} %fusion.42, bf16[512,2048]{1,0:T(8,128)(2,1)S(1)} %copy-done.3, bf16[512,1024]{1,0:T(8,128)(2,1)S(1)} %copy-done.26), kind=kOutput, calls=%fused_computation.1 | convolution fusion | flops 2151677952 | bytes 15728640 | tf_op jit(solution)/shard_map/dot_general | solution.py:257
  294.5 13.7 %collective-permute-done.31.refs_1_ = bf16[512,1024]{1,0:T(8,128)(2,1)S(1)} collective-permute-done((bf16[512,1024]{1,0:T(8,128)(2,1)}, bf16[512,1024]{1,0:T(8,128)(2,1)S(1)}, u32[]{:S(2)}, u32[]{:S(2)}) %collective-permute-start.31) | collective-permute-done | bytes 1048608 | tf_op jit(solution)/shard_map/ppermute | solution.py:774
  309.1 9.1 %unmix.1 = (f32[512,1024]{1,0:T(8,128)}, bf16[512,1024]{1,0:T(8,128)(2,1)}, bf16[512,1024]{1,0:T(8,128)(2,1)}, f32[8,1024]{1,0:T(8,128)}) custom-call(f32[512,1024]{1,0:T(8,128)} %fusion.41.refs_0_, bf16[512,1024]{1,0:T(8,128)(2,1)} %copy-done.37, f32[512,1024]{1,0:T(8,128)} %get-tuple-element.263.refs_2_, f32[512,1024]{1,0:T(8,128)} %get-tuple-element.264.refs_3_, ...), custom_call_target="tpu_custom_call" | custom-call | tf_op jit(solution)/shard_map/unmix/pallas_call | solution.py:230
  322.4 12.7 %attend_grad.2 = (bf16[512,1536]{1,0:T(8,128)(2,1)}, f32[1,1536]{1,0:T(1,128)}) custom-call(s32[2]{0:T(128)} %pad_add_fusion.refs_0_, bf16[512,3072]{1,0:T(8,128)(2,1)} %project.1.refs_3_.refs_1_, bf16[512,1024]{1,0:T(8,128)(2,1)} %get-tuple-element.271.refs_2_, bf16[1024,2048]{1,0:T(8,128)(2,1)} %add_convert_fusion.refs_3_, bf16[512,1024]{1,0:T(8,128)(2,1)} %copy-done.29), custom_call_target="tpu_custom_call" | custom-call | tf_op jit(solution)/shard_map/attend_grad/pallas_call | solution.py:230
  335.1 2.4 convolution_convert_fusion.1
  337.6 4.7 %weight_rows.1 = (bf16[128,1024]{1,0:T(8,128)(2,1)}, bf16[128,1024]{1,0:T(8,128)(2,1)}, bf16[128,1024]{1,0:T(8,128)(2,1)}, bf16[128,1024]{1,0:T(8,128)(2,1)}) custom-call(bf16[512,512]{1,0:T(8,128)(2,1)} %slice.206.refs_0_, bf16[512,1024]{1,0:T(8,128)(2,1)} %get-tuple-element.268.refs_1_, bf16[512,1024]{1,0:T(8,128)(2,1)} %collective-permute-done.32.refs_2_, ...), custom_call_target="tpu_custom_call" | custom-call | tf_op jit(solution)/shard_map/weight_rows/pallas_call | solution.py:230
  342.3 12.8 %attend_grad.3 = (bf16[512,1536]{1,0:T(8,128)(2,1)}, f32[1,1536]{1,0:T(1,128)}) custom-call(s32[2]{0:T(128)} %pad_add_fusion.refs_0_, bf16[512,3072]{1,0:T(8,128)(2,1)} %project.1.refs_3_.refs_1_, bf16[512,1024]{1,0:T(8,128)(2,1)} %get-tuple-element.271.refs_2_, bf16[128,1024]{1,0:T(8,128)(2,1)} %get-tuple-element.303.refs_3_), custom_call_target="tpu_custom_call" | custom-call | tf_op jit(solution)/shard_map/attend_grad/pallas_call | solution.py:230
  355.1 2.5 convolution_convert_fusion
  360.0 2.2 collective-permute-start.48
  362.4 6.5 %collective-permute-done.48 = bf16[128,1024]{1,0:T(8,128)(2,1)S(1)} collective-permute-done((bf16[128,1024]{1,0:T(8,128)(2,1)}, bf16[128,1024]{1,0:T(8,128)(2,1)S(1)}, u32[]{:S(2)}, u32[]{:S(2)}) %collective-permute-start.48) | collective-permute-done | bytes 262176 | tf_op jit(solution)/shard_map/ppermute | solution.py:774
  377.5 7.5 %weight_cols.1 = (bf16[128,3072]{1,0:T(8,128)(2,1)}, bf16[128,3072]{1,0:T(8,128)(2,1)}, bf16[256,1536]{1,0:T(8,128)(2,1)}, bf16[256,1536]{1,0:T(8,128)(2,1)}) custom-call(bf16[512,512]{1,0:T(8,128)(2,1)} %slice.262.refs_0_, bf16[512,1536]{1,0:T(8,128)(2,1)} %get-tuple-element.275.refs_3_.refs_1_.refs_0_, ...), custom_call_target="tpu_custom_call" | custom-call | tf_op jit(solution)/shard_map/weight_cols/pallas_call | solution.py:230
  391.5 2.6 collective-permute-start.53
  398.5 3.1 collective-permute-start.47
  403.5 3.4 collective-permute-start.46
  407.6 10.2 %stream_grad.1 = bf16[512,1024]{1,0:T(8,128)(2,1)} custom-call(bf16[512,1536]{1,0:T(8,128)(2,1)} %get-tuple-element.275.refs_3_.refs_1_.refs_0_, bf16[512,1536]{1,0:T(8,128)(2,1)} %get-tuple-element.285.refs_2_.refs_1_, bf16[512,1536]{1,0:T(8,128)(2,1)} %constant_dynamic-update-slice_fusion.4.refs_1_.refs_2_, ...), custom_call_target="tpu_custom_call" | custom-call | tf_op jit(solution)/shard_map/stream_grad/pallas_call | solution.py:230
  422.5 8.7 %collective-permute-done.37 = bf16[128,1536]{1,0:T(8,128)(2,1)S(1)} collective-permute-done((bf16[128,1536]{1,0:T(8,128)(2,1)S(1)}, bf16[128,1536]{1,0:T(8,128)(2,1)S(1)}, u32[]{:S(2)}, u32[]{:S(2)}) %collective-permute-start.37) | collective-permute-done | bytes 393248 | tf_op jit(solution)/shard_map/ppermute | solution.py:774
  431.4 2.2 collective-permute-start.41
  441.7 3.3 collective-permute-done.41
  445.0 2.1 collective-permute-done.40
  447.1 2.4 collective-permute-done.39
  (400 shorter events, 120.3 us)
Async XLA Ops:
  7.2 145.5 %all-gather.3.cloned.1.call-start = ((), (), s32[]{:S(2)}) async-start(), calls=%async_computation.2 | async-start | bytes 4456448 | tf_op jit(solution)/shard_map/all_gather | solution.py:876
  12.1 25.2 %collective-permute-start.4 = (bf16[64,1536]{1,0:T(8,128)(2,1)S(1)}, bf16[64,1536]{1,0:T(8,128)(2,1)S(1)}, u32[]{:S(2)}, u32[]{:S(2)}) collective-permute-start(bf16[64,1536]{1,0:T(8,128)(2,1)S(1)} %reshape.227), channel_id=1, source_target_pairs={{0,8},{2,10},{4,12},{6,14},{8,16},{10,18},{12,20},{14,22},{16,24},... | collective-permute-start | bytes 589832 | tf_op jit(solution)/shard_map/ppermute | solution.py:778
  13.7 23.6 %collective-permute-start.5 = (bf16[64,1536]{1,0:T(8,128)(2,1)S(1)}, bf16[64,1536]{1,0:T(8,128)(2,1)S(1)}, u32[]{:S(2)}, u32[]{:S(2)}) collective-permute-start(bf16[64,1536]{1,0:T(8,128)(2,1)S(1)} %reshape.227), channel_id=1, source_target_pairs={{0,16},{2,18},{4,20},{6,22},{8,24},{10,26},{12,28},{14,30},{16,0},... | collective-permute-start | bytes 589832 | tf_op jit(solution)/shard_map/ppermute | solution.py:778
  15.9 14.9 %collective-permute-start.1 = (bf16[16,128]{1,0:T(8,128)(2,1)S(1)}, bf16[16,128]{1,0:T(8,128)(2,1)S(1)}, u32[]{:S(2)}, u32[]{:S(2)}) collective-permute-start(bf16[16,128]{1,0:T(8,128)(2,1)S(1)} %concatenate.56), channel_id=1, source_target_pairs={{0,8},{2,10},{4,12},{6,14},{8,16},{10,18},{12,20},{14,22},{16,24},... | collective-permute-start | bytes 12296 | tf_op jit(solution)/shard_map/ppermute | solution.py:778
  16.7 14.0 %collective-permute-start.2 = (bf16[16,128]{1,0:T(8,128)(2,1)S(1)}, bf16[16,128]{1,0:T(8,128)(2,1)S(1)}, u32[]{:S(2)}, u32[]{:S(2)}) collective-permute-start(bf16[16,128]{1,0:T(8,128)(2,1)S(1)} %concatenate.56), channel_id=1, source_target_pairs={{0,16},{2,18},{4,20},{6,22},{8,24},{10,26},{12,28},{14,30},{16,0},... | collective-permute-start | bytes 12296 | tf_op jit(solution)/shard_map/ppermute | solution.py:778
  20.2 17.1 %collective-permute-start = (bf16[256,1024]{1,0:T(8,128)(2,1)S(1)}, bf16[256,1024]{1,0:T(8,128)(2,1)S(1)}, u32[]{:S(2)}, u32[]{:S(2)}) collective-permute-start(bf16[256,1024]{1,0:T(8,128)(2,1)S(1)} %get-tuple-element.160), channel_id=1, source_target_pairs={{0,1},{1,0},{2,3},{3,2},{4,5},{5,4},{6,7},{7,6},{8,9},{9,8},{10,11... | collective-permute-start | bytes 1572872 | tf_op jit(solution)/shard_map/ppermute | solution.py:774
  38.9 150.1 %all-gather.5.cloned.1.call-start = ((), (), s32[]{:S(2)}) async-start(), calls=%async_computation.3 | async-start | bytes 4456448 | tf_op jit(solution)/shard_map/all_gather | solution.py:877
  46.1 390.1 %reduce-scatter.3.cloned.1.call-start = ((), (), s32[]{:S(2)}) async-start(), calls=%async_computation.4 | async-start | bytes 4456448 | tf_op jit(solution)/shard_map/reduce_scatter | solution.py:968
  46.2 10.1 %collective-permute-start.7 = (bf16[128,1536]{1,0:T(8,128)(2,1)}, bf16[128,1536]{1,0:T(8,128)(2,1)S(1)}, u32[]{:S(2)}, u32[]{:S(2)}) collective-permute-start(bf16[128,1536]{1,0:T(8,128)(2,1)} %get-tuple-element.178), channel_id=1, source_target_pairs={{0,1},{1,0},{2,3},{3,2},{4,5},{5,4},{6,7},{7,6},{8,9},{9,8},{10,11... | collective-permute-start | bytes 1179656 | tf_op jit(solution)/shard_map/ppermute | solution.py:774
  47.7 11.8 %collective-permute-start.8 = (bf16[128,1536]{1,0:T(8,128)(2,1)S(1)}, bf16[128,1536]{1,0:T(8,128)(2,1)S(1)}, u32[]{:S(2)}, u32[]{:S(2)}) collective-permute-start(bf16[128,1536]{1,0:T(8,128)(2,1)S(1)} %constant_dynamic-update-slice_fusion), channel_id=1, source_target_pairs={{0,4},{2,6},{4,0},{6,2},{8,12},{10,14},{12,8},{14,10},{16,20},{18,... | collective-permute-start | bytes 1179656 | tf_op jit(solution)/shard_map/ppermute | solution.py:774
  49.3 12.4 %collective-permute-start.13 = (bf16[32,1024]{1,0:T(8,128)(2,1)}, bf16[32,1024]{1,0:T(8,128)(2,1)S(1)}, u32[]{:S(2)}, u32[]{:S(2)}) collective-permute-start(bf16[32,1024]{1,0:T(8,128)(2,1)} %param.18), channel_id=1, source_target_pairs={{0,8},{2,10},{4,12},{6,14},{8,16},{10,18},{12,20},{14,22},{16,24},... | collective-permute-start | bytes 196616 | tf_op jit(solution)/shard_map/ppermute | solution.py:778
  51.1 11.2 %collective-permute-start.14 = (bf16[32,1024]{1,0:T(8,128)(2,1)}, bf16[32,1024]{1,0:T(8,128)(2,1)S(1)}, u32[]{:S(2)}, u32[]{:S(2)}) collective-permute-start(bf16[32,1024]{1,0:T(8,128)(2,1)} %param.18), channel_id=1, source_target_pairs={{0,16},{2,18},{4,20},{6,22},{8,24},{10,26},{12,28},{14,30},{16,0},... | collective-permute-start | bytes 196616 | tf_op jit(solution)/shard_map/ppermute | solution.py:778
  52.2 8.8 %collective-permute-start.11 = (bf16[4,16,128]{2,1,0:T(8,128)(2,1)S(1)}, bf16[4,16,128]{2,1,0:T(8,128)(2,1)S(1)}, u32[]{:S(2)}, u32[]{:S(2)}) collective-permute-start(bf16[4,16,128]{2,1,0:T(8,128)(2,1)S(1)} %get-tuple-element.183), channel_id=1, source_target_pairs={{0,1},{1,0},{2,3},{3,2},{4,5},{5,4},{6,7},{7,6},{8,9},{9,8},{10,11... | collective-permute-start | bytes 49160 | tf_op jit(solution)/shard_map/ppermute | solution.py:774
  59.6 13.8 %collective-permute-start.9 = (bf16[128,1536]{1,0:T(8,128)(2,1)}, bf16[128,1536]{1,0:T(8,128)(2,1)S(1)}, u32[]{:S(2)}, u32[]{:S(2)}) collective-permute-start(bf16[128,1536]{1,0:T(8,128)(2,1)} %get-tuple-element.178), channel_id=1, source_target_pairs={{0,4},{2,6},{4,0},{6,2},{8,12},{10,14},{12,8},{14,10},{16,20},{18,... | collective-permute-start | bytes 1179656 | tf_op jit(solution)/shard_map/ppermute | solution.py:774
  61.1 12.3 %collective-permute-start.10 = (bf16[128,1536]{1,0:T(8,128)(2,1)S(1)}, bf16[128,1536]{1,0:T(8,128)(2,1)S(1)}, u32[]{:S(2)}, u32[]{:S(2)}) collective-permute-start(bf16[128,1536]{1,0:T(8,128)(2,1)S(1)} %constant_dynamic-update-slice_fusion), channel_id=1, source_target_pairs={{0,1},{1,0},{2,3},{3,2},{4,5},{5,4},{6,7},{7,6},{8,9},{9,8},{10,11... | collective-permute-start | bytes 1179656 | tf_op jit(solution)/shard_map/ppermute | solution.py:774
  61.7 11.6 %collective-permute-start.12 = (bf16[2,4,16,128]{3,2,1,0:T(8,128)(2,1)S(1)}, bf16[2,4,16,128]{3,2,1,0:T(8,128)(2,1)S(1)}, u32[]{:S(2)}, u32[]{:S(2)}) collective-permute-start(bf16[2,4,16,128]{3,2,1,0:T(8,128)(2,1)S(1)} %get-tuple-element.189), channel_id=1, source_target_pairs={{0,4},{2,6},{4,0},{6,2},{8,12},{10,14},{12,8},{14,10},{16,20},{18,... | collective-permute-start | bytes 98312 | tf_op jit(solution)/shard_map/ppermute | solution.py:774
  63.8 23.3 %collective-permute-start.17 = (bf16[128,1536]{1,0:T(8,128)(2,1)S(1)}, bf16[128,1536]{1,0:T(8,128)(2,1)S(1)}, u32[]{:S(2)}, u32[]{:S(2)}) collective-permute-start(bf16[128,1536]{1,0:T(8,128)(2,1)S(1)} %collective-permute-done.7), channel_id=1, source_target_pairs={{0,4},{2,6},{4,0},{6,2},{8,12},{10,14},{12,8},{14,10},{16,20},{18,... | collective-permute-start | bytes 1179656 | tf_op jit(solution)/shard_map/ppermute | solution.py:774
  64.3 22.8 %collective-permute-start.18 = (bf16[128,1536]{1,0:T(8,128)(2,1)S(1)}, bf16[128,1536]{1,0:T(8,128)(2,1)S(1)}, u32[]{:S(2)}, u32[]{:S(2)}) collective-permute-start(bf16[128,1536]{1,0:T(8,128)(2,1)S(1)} %collective-permute-done.8), channel_id=1, source_target_pairs={{0,1},{1,0},{2,3},{3,2},{4,5},{5,4},{6,7},{7,6},{8,9},{9,8},{10,11... | collective-permute-start | bytes 1179656 | tf_op jit(solution)/shard_map/ppermute | solution.py:774
  76.3 19.6 %collective-permute-start.16 = (bf16[512,1536]{1,0:T(8,128)(2,1)}, bf16[512,1536]{1,0:T(8,128)(2,1)}, u32[]{:S(2)}, u32[]{:S(2)}) collective-permute-start(bf16[512,1536]{1,0:T(8,128)(2,1)} %constant_dynamic-update-slice_fusion.4.refs_1_.refs_2_), channel_id=1, source_target_pairs={{0,2},{2,0},{4,6},{6,4},{8,10},{10,8},{12,14},{14,12},{16,18},{18,... | collective-permute-start | bytes 4718600 | tf_op jit(solution)/shard_map/ppermute | solution.py:774
  92.7 13.5 %collective-permute-start.21 = (bf16[64,1024]{1,0:T(8,128)(2,1)S(1)}, bf16[64,1024]{1,0:T(8,128)(2,1)S(1)}, u32[]{:S(2)}, u32[]{:S(2)}) collective-permute-start(bf16[64,1024]{1,0:T(8,128)(2,1)S(1)} %copy-done.53), channel_id=1, source_target_pairs={{0,1},{1,0},{2,3},{3,2},{4,5},{5,4},{6,7},{7,6},{8,9},{9,8},{10,11... | collective-permute-start | bytes 393224 | tf_op jit(solution)/shard_map/ppermute | solution.py:774
  92.7 13.6 %collective-permute-start.22 = (bf16[64,1024]{1,0:T(8,128)(2,1)S(1)}, bf16[64,1024]{1,0:T(8,128)(2,1)S(1)}, u32[]{:S(2)}, u32[]{:S(2)}) collective-permute-start(bf16[64,1024]{1,0:T(8,128)(2,1)S(1)} %pad_maximum_fusion.3), channel_id=1, source_target_pairs={{0,4},{2,6},{4,0},{6,2},{8,12},{10,14},{12,8},{14,10},{16,20},{18,... | collective-permute-start | bytes 393224 | tf_op jit(solution)/shard_map/ppermute | solution.py:774
  108.5 16.3 %collective-permute-start.23 = (bf16[128,1024]{1,0:T(8,128)(2,1)}, bf16[128,1024]{1,0:T(8,128)(2,1)S(1)}, u32[]{:S(2)}, u32[]{:S(2)}) collective-permute-start(bf16[128,1024]{1,0:T(8,128)(2,1)} %get-tuple-element.228.refs_2_), channel_id=1, source_target_pairs={{0,4},{2,6},{4,0},{6,2},{8,12},{10,14},{12,8},{14,10},{16,20},{18,... | collective-permute-start | bytes 786440 | tf_op jit(solution)/shard_map/ppermute | solution.py:774
  110.1 14.7 %collective-permute-start.24 = (bf16[128,1024]{1,0:T(8,128)(2,1)}, bf16[128,1024]{1,0:T(8,128)(2,1)S(1)}, u32[]{:S(2)}, u32[]{:S(2)}) collective-permute-start(bf16[128,1024]{1,0:T(8,128)(2,1)} %constant_dynamic-update-slice_fusion.17.refs_3_), channel_id=1, source_target_pairs={{0,1},{1,0},{2,3},{3,2},{4,5},{5,4},{6,7},{7,6},{8,9},{9,8},{10,11... | collective-permute-start | bytes 786440 | tf_op jit(solution)/shard_map/ppermute | solution.py:774
  128.2 14.4 %collective-permute-start.25 = (bf16[512,1024]{1,0:T(8,128)(2,1)S(1)}, bf16[512,1024]{1,0:T(8,128)(2,1)S(1)}, u32[]{:S(2)}, u32[]{:S(2)}) collective-permute-start(bf16[512,1024]{1,0:T(8,128)(2,1)S(1)} %constant_dynamic-update-slice_fusion.20.refs_2_.refs_3_.refs_5_), channel_id=1, source_target_pairs={{0,2},{2,0},{4,6},{6,4},{8,10},{10,8},{12,14},{14,12},{16,18},{18,... | collective-permute-start | bytes 3145736 | tf_op jit(solution)/shard_map/ppermute | solution.py:774
  128.3 14.3 %collective-permute-start.26 = (bf16[256,1024]{1,0:T(8,128)(2,1)S(1)}, bf16[256,1024]{1,0:T(8,128)(2,1)S(1)}, u32[]{:S(2)}, u32[]{:S(2)}) collective-permute-start(bf16[256,1024]{1,0:T(8,128)(2,1)S(1)} %copy-done.16), channel_id=1, source_target_pairs={{0,1},{1,0},{2,3},{3,2},{4,5},{5,4},{6,7},{7,6},{8,9},{9,8},{10,11... | collective-permute-start | bytes 1572872 | tf_op jit(solution)/shard_map/ppermute | solution.py:774
  152.4 25.1 %collective-permute-start.27 = (bf16[512,1024]{1,0:T(8,128)(2,1)}, bf16[512,1024]{1,0:T(8,128)(2,1)S(1)}, u32[]{:S(2)}, u32[]{:S(2)}) collective-permute-start(bf16[512,1024]{1,0:T(8,128)(2,1)} %get-tuple-element.246.refs_0_), channel_id=1, source_target_pairs={{0,1},{1,0},{2,3},{3,2},{4,5},{5,4},{6,7},{7,6},{8,9},{9,8},{10,11... | collective-permute-start | bytes 3145736 | tf_op jit(solution)/shard_map/ppermute | solution.py:774
  194.8 24.2 %collective-permute-start.28 = (bf16[512,1024]{1,0:T(8,128)(2,1)}, bf16[512,1024]{1,0:T(8,128)(2,1)S(1)}, u32[]{:S(2)}, u32[]{:S(2)}) collective-permute-start(bf16[512,1024]{1,0:T(8,128)(2,1)} %matmul.2.refs_2_), channel_id=1, source_target_pairs={{0,1},{1,0},{2,3},{3,2},{4,5},{5,4},{6,7},{7,6},{8,9},{9,8},{10,11... | collective-permute-start | bytes 3145736 | tf_op jit(solution)/shard_map/ppermute | solution.py:774
  226.7 23.3 %collective-permute-start.29 = (bf16[512,1024]{1,0:T(8,128)(2,1)}, bf16[512,1024]{1,0:T(8,128)(2,1)S(1)}, u32[]{:S(2)}, u32[]{:S(2)}) collective-permute-start(bf16[512,1024]{1,0:T(8,128)(2,1)} %get-tuple-element.254.refs_0_), channel_id=1, source_target_pairs={{0,1},{1,0},{2,3},{3,2},{4,5},{5,4},{6,7},{7,6},{8,9},{9,8},{10,11... | collective-permute-start | bytes 3145736 | tf_op jit(solution)/shard_map/ppermute | solution.py:774
  269.1 168.8 %reduce-scatter.5.cloned.1.call-start = ((), (), s32[]{:S(2)}) async-start(), calls=%async_computation.5 | async-start | bytes 4456448 | tf_op jit(solution)/shard_map/reduce_scatter | solution.py:962
  273.9 46.6 %collective-permute-start.30 = (bf16[256,1024]{1,0:T(8,128)(2,1)}, bf16[256,1024]{1,0:T(8,128)(2,1)S(1)}, u32[]{:S(2)}, u32[]{:S(2)}) collective-permute-start(bf16[256,1024]{1,0:T(8,128)(2,1)} %get-tuple-element.261), channel_id=1, source_target_pairs={{0,1},{1,0},{2,3},{3,2},{4,5},{5,4},{6,7},{7,6},{8,9},{9,8},{10,11... | collective-permute-start | bytes 1572872 | tf_op jit(solution)/shard_map/ppermute | solution.py:774
  286.1 22.1 %collective-permute-start.31 = (bf16[512,1024]{1,0:T(8,128)(2,1)}, bf16[512,1024]{1,0:T(8,128)(2,1)S(1)}, u32[]{:S(2)}, u32[]{:S(2)}) collective-permute-start(bf16[512,1024]{1,0:T(8,128)(2,1)} %convolution_convert_fusion.4), channel_id=1, source_target_pairs={{0,1},{1,0},{2,3},{3,2},{4,5},{5,4},{6,7},{7,6},{8,9},{9,8},{10,11... | collective-permute-start | bytes 3145736 | tf_op jit(solution)/shard_map/ppermute | solution.py:774
  320.3 14.9 %collective-permute-start.32 = (bf16[512,1024]{1,0:T(8,128)(2,1)S(1)}, bf16[512,1024]{1,0:T(8,128)(2,1)}, u32[]{:S(2)}, u32[]{:S(2)}) collective-permute-start(bf16[512,1024]{1,0:T(8,128)(2,1)S(1)} %convolution_convert_fusion.3.refs_4_), channel_id=1, source_target_pairs={{0,2},{2,0},{4,6},{6,4},{8,10},{10,8},{12,14},{14,12},{16,18},{18,... | collective-permute-start | bytes 3145736 | tf_op jit(solution)/shard_map/ppermute | solution.py:774
  358.1 19.4 %collective-permute-start.33 = (bf16[512,3072]{1,0:T(8,128)(2,1)S(1)}, bf16[512,3072]{1,0:T(8,128)(2,1)}, u32[]{:S(2)}, u32[]{:S(2)}) collective-permute-start(bf16[512,3072]{1,0:T(8,128)(2,1)S(1)} %pad_maximum_fusion), channel_id=1, source_target_pairs={{0,2},{2,0},{4,6},{6,4},{8,10},{10,8},{12,14},{14,12},{16,18},{18,... | collective-permute-start | bytes 9437192 | tf_op jit(solution)/shard_map/ppermute | solution.py:774
  360.0 8.9 %collective-permute-start.48 = (bf16[128,1024]{1,0:T(8,128)(2,1)}, bf16[128,1024]{1,0:T(8,128)(2,1)S(1)}, u32[]{:S(2)}, u32[]{:S(2)}) collective-permute-start(bf16[128,1024]{1,0:T(8,128)(2,1)} %get-tuple-element.303.refs_3_), channel_id=1, source_target_pairs={{0,4},{2,6},{4,0},{6,2},{8,12},{10,14},{12,8},{14,10},{16,20},{18,... | collective-permute-start | bytes 786440 | tf_op jit(solution)/shard_map/ppermute | solution.py:774
  389.7 8.8 %collective-permute-start.54 = (bf16[32,1024]{1,0:T(8,128)(2,1)S(1)}, bf16[32,1024]{1,0:T(8,128)(2,1)S(1)}, u32[]{:S(2)}, u32[]{:S(2)}) collective-permute-start(bf16[32,1024]{1,0:T(8,128)(2,1)S(1)} %get-tuple-element.335), channel_id=1, source_target_pairs={{0,8},{2,10},{4,12},{6,14},{8,16},{10,18},{12,20},{14,22},{16,24},... | collective-permute-start | bytes 196616 | tf_op jit(solution)/shard_map/ppermute | solution.py:929
  391.5 12.1 %collective-permute-start.53 = (bf16[32,1024]{1,0:T(8,128)(2,1)S(1)}, bf16[32,1024]{1,0:T(8,128)(2,1)S(1)}, u32[]{:S(2)}, u32[]{:S(2)}) collective-permute-start(bf16[32,1024]{1,0:T(8,128)(2,1)S(1)} %get-tuple-element.334), channel_id=1, source_target_pairs={{0,16},{2,18},{4,20},{6,22},{8,24},{10,26},{12,28},{14,30},{16,0},... | collective-permute-start | bytes 196616 | tf_op jit(solution)/shard_map/ppermute | solution.py:929
  394.8 12.1 %collective-permute-start.52 = (bf16[32,1024]{1,0:T(8,128)(2,1)S(1)}, bf16[32,1024]{1,0:T(8,128)(2,1)S(1)}, u32[]{:S(2)}, u32[]{:S(2)}) collective-permute-start(bf16[32,1024]{1,0:T(8,128)(2,1)S(1)} %slice.360), channel_id=1, source_target_pairs={{0,24},{2,26},{4,28},{6,30},{8,0},{10,2},{12,4},{14,6},{16,8},{18,... | collective-permute-start | bytes 196616 | tf_op jit(solution)/shard_map/ppermute | solution.py:929
  394.9 24.1 %collective-permute-start.34 = (bf16[128,3072]{1,0:T(8,128)(2,1)S(1)}, bf16[128,3072]{1,0:T(8,128)(2,1)S(1)}, u32[]{:S(2)}, u32[]{:S(2)}) collective-permute-start(bf16[128,3072]{1,0:T(8,128)(2,1)S(1)} %copy-done.11), channel_id=1, source_target_pairs={{0,4},{2,6},{4,0},{6,2},{8,12},{10,14},{12,8},{14,10},{16,20},{18,... | collective-permute-start | bytes 2359304 | tf_op jit(solution)/shard_map/ppermute | solution.py:774
  397.9 21.1 %collective-permute-start.35 = (bf16[256,1536]{1,0:T(8,128)(2,1)S(1)}, bf16[256,1536]{1,0:T(8,128)(2,1)S(1)}, u32[]{:S(2)}, u32[]{:S(2)}) collective-permute-start(bf16[256,1536]{1,0:T(8,128)(2,1)S(1)} %copy-done.72), channel_id=1, source_target_pairs={{0,1},{1,0},{2,3},{3,2},{4,5},{5,4},{6,7},{7,6},{8,9},{9,8},{10,11... | collective-permute-start | bytes 2359304 | tf_op jit(solution)/shard_map/ppermute | solution.py:774
  398.5 19.3 %collective-permute-start.47 = (bf16[1,16,128]{2,1,0:T(8,128)(2,1)S(1)}, bf16[1,16,128]{2,1,0:T(8,128)(2,1)S(1)}, u32[]{:S(2)}, u32[]{:S(2)}) collective-permute-start(bf16[1,16,128]{2,1,0:T(8,128)(2,1)S(1)} %get-tuple-element.349), channel_id=1, source_target_pairs={{0,8},{2,10},{4,12},{6,14},{8,16},{10,18},{12,20},{14,22},{16,24},... | collective-permute-start | bytes 12296 | tf_op jit(solution)/shard_map/ppermute | solution.py:929
  403.5 14.3 %collective-permute-start.46 = (bf16[1,16,128]{2,1,0:T(8,128)(2,1)S(1)}, bf16[1,16,128]{2,1,0:T(8,128)(2,1)S(1)}, u32[]{:S(2)}, u32[]{:S(2)}) collective-permute-start(bf16[1,16,128]{2,1,0:T(8,128)(2,1)S(1)} %get-tuple-element.350), channel_id=1, source_target_pairs={{0,16},{2,18},{4,20},{6,22},{8,24},{10,26},{12,28},{14,30},{16,0},... | collective-permute-start | bytes 12296 | tf_op jit(solution)/shard_map/ppermute | solution.py:929
  406.9 10.9 %collective-permute-start.45 = (bf16[1,16,128]{2,1,0:T(8,128)(2,1)S(1)}, bf16[1,16,128]{2,1,0:T(8,128)(2,1)S(1)}, u32[]{:S(2)}, u32[]{:S(2)}) collective-permute-start(bf16[1,16,128]{2,1,0:T(8,128)(2,1)S(1)} %get-tuple-element.348), channel_id=1, source_target_pairs={{0,24},{2,26},{4,28},{6,30},{8,0},{10,2},{12,4},{14,6},{16,8},{18,... | collective-permute-start | bytes 12296 | tf_op jit(solution)/shard_map/ppermute | solution.py:929
  419.1 12.1 %collective-permute-start.37 = (bf16[128,1536]{1,0:T(8,128)(2,1)S(1)}, bf16[128,1536]{1,0:T(8,128)(2,1)S(1)}, u32[]{:S(2)}, u32[]{:S(2)}) collective-permute-start(bf16[128,1536]{1,0:T(8,128)(2,1)S(1)} %add_convert_fusion.4), channel_id=1, source_target_pairs={{0,1},{1,0},{2,3},{3,2},{4,5},{5,4},{6,7},{7,6},{8,9},{9,8},{10,11... | collective-permute-start | bytes 1179656 | tf_op jit(solution)/shard_map/ppermute | solution.py:774
  420.7 10.5 %collective-permute-start.38 = (bf16[128,1536]{1,0:T(8,128)(2,1)S(1)}, bf16[128,1536]{1,0:T(8,128)(2,1)S(1)}, u32[]{:S(2)}, u32[]{:S(2)}) collective-permute-start(bf16[128,1536]{1,0:T(8,128)(2,1)S(1)} %add_convert_fusion.3), channel_id=1, source_target_pairs={{0,4},{2,6},{4,0},{6,2},{8,12},{10,14},{12,8},{14,10},{16,20},{18,... | collective-permute-start | bytes 1179656 | tf_op jit(solution)/shard_map/ppermute | solution.py:774
  421.9 18.6 %collective-permute-start.36 = (bf16[256,1024]{1,0:T(8,128)(2,1)S(1)}, bf16[256,1024]{1,0:T(8,128)(2,1)S(1)}, u32[]{:S(2)}, u32[]{:S(2)}) collective-permute-start(bf16[256,1024]{1,0:T(8,128)(2,1)S(1)} %get-tuple-element.321), channel_id=1, source_target_pairs={{0,1},{1,0},{2,3},{3,2},{4,5},{5,4},{6,7},{7,6},{8,9},{9,8},{10,11... | collective-permute-start | bytes 1572872 | tf_op jit(solution)/shard_map/ppermute | solution.py:774
  431.4 13.6 %collective-permute-start.41 = (bf16[64,1536]{1,0:T(8,128)(2,1)S(1)}, bf16[64,1536]{1,0:T(8,128)(2,1)S(1)}, u32[]{:S(2)}, u32[]{:S(2)}) collective-permute-start(bf16[64,1536]{1,0:T(8,128)(2,1)S(1)} %get-tuple-element.329), channel_id=1, source_target_pairs={{0,8},{2,10},{4,12},{6,14},{8,16},{10,18},{12,20},{14,22},{16,24},... | collective-permute-start | bytes 589832 | tf_op jit(solution)/shard_map/ppermute | solution.py:929
  433.6 13.5 %collective-permute-start.40 = (bf16[64,1536]{1,0:T(8,128)(2,1)S(1)}, bf16[64,1536]{1,0:T(8,128)(2,1)S(1)}, u32[]{:S(2)}, u32[]{:S(2)}) collective-permute-start(bf16[64,1536]{1,0:T(8,128)(2,1)S(1)} %get-tuple-element.328), channel_id=1, source_target_pairs={{0,16},{2,18},{4,20},{6,22},{8,24},{10,26},{12,28},{14,30},{16,0},... | collective-permute-start | bytes 589832 | tf_op jit(solution)/shard_map/ppermute | solution.py:929
  435.6 13.9 %collective-permute-start.39 = (bf16[64,1536]{1,0:T(8,128)(2,1)S(1)}, bf16[64,1536]{1,0:T(8,128)(2,1)S(1)}, u32[]{:S(2)}, u32[]{:S(2)}) collective-permute-start(bf16[64,1536]{1,0:T(8,128)(2,1)S(1)} %slice.359), channel_id=1, source_target_pairs={{0,24},{2,26},{4,28},{6,30},{8,0},{10,2},{12,4},{14,6},{16,8},{18,... | collective-permute-start | bytes 589832 | tf_op jit(solution)/shard_map/ppermute | solution.py:929
  (87 other events, 524.4 us)
Sparse Core Ops, SparseCore 0:
  39.0 59.8 all-gather.2
  101.1 52.5 all-gather.4
  269.2 71.1 reduce-scatter.2
  344.6 80.6 reduce-scatter.4

commit v3 on v2

--- a/solution.py
+++ b/solution.py
@@ -909,7 +909,7 @@
     tile = own // 2
     block = 2 * lanes
     zhat1, r1, mixed, m_own, ctx_rel = mix(
-        ctx0, ctx1, own_seq, wo0, wo1, perm_ctx, vecs, tile, deps=[cot_theirs]
+        ctx0, ctx1, own_seq, wo0, wo1, perm_ctx, vecs, own, deps=[cot_theirs]
     )
     m_far = send("x", m_own)
     h_own, g_own = up_gelu(m_own, wi, bias_up, block)

time: 464 us -> 464 us (level)
  transfers between devices with their start and end apart: 59 -> 59, of which waited for: 23 -> 23; matrix products, arithmetic and copies ran while one was open for 18% -> 18% of each run, Pallas kernels for 29% -> 28%
where the time goes in v3:
time: 464 us; the launch traced here: 457 us
  Pallas kernels  152 us (33%)
  waiting for transfers between devices  127 us (27%)
  starting transfers between devices  55.2 us (12%)
  local copies, waits for them, and re-layouts  49 us (11%)
  matrix products  37.1 us (8%)
  other arithmetic  21.2 us (5%)
  between operations  15.9 us (3%)
    pallas_call x17, Pallas kernels, kernel(): pl.pallas_call(without_deps, grid_spec=pltpu.PrefetchScalarGridSpec(num_s...  152 us
    ppermute x37, waiting for transfers between devices, send(): return lax.ppermute(at(value), *routes[way])  104 us
    dot_general x10, matrix products, dot(): return lax.dot_general(a, b, (dims, ((), ())), preferred_element_type=F32)  36.6 us
    ppermute x37, starting transfers between devices, send(): return lax.ppermute(at(value), *routes[way])  28.8 us
    unnamed x184, local copies, waits for them, and re-layouts  24.9 us
    ppermute x9, starting transfers between devices, finish(): got = [lax.ppermute(v, *routes[-1 - i]) for i, v in enumerate(parts)]  14.2 us
    ppermute x9, waiting for transfers between devices, along_z(): return [lax.ppermute(value, *routes[k]) for k in range(1, 4)]  12.6 us
    ppermute x9, starting transfers between devices, along_z(): return [lax.ppermute(value, *routes[k]) for k in range(1, 4)]  12 us
  transfers between devices with their start and end apart: 59, of which 23 were waited for; matrix products, arithmetic and copies ran while one was open for 18% of the time, Pallas kernels for 28%

profile of v3, /device:TPU:8, one launch (start us, length us, event | category | flops | bytes accessed | tf_op | source)
XLA Modules:
  0.0 456.7 jit_solution(5250001080422447628)
XLA Ops:
  16.7 3.5 collective-permute-start.2
  24.5 6.2 %collective-permute-done.1.refs_6_ = bf16[16,128]{1,0:T(8,128)(2,1)S(1)} collective-permute-done((bf16[16,128]{1,0:T(8,128)(2,1)S(1)}, bf16[16,128]{1,0:T(8,128)(2,1)S(1)}, u32[]{:S(2)}, u32[]{:S(2)}) %collective-permute-start.1) | collective-permute-done | bytes 4128 | tf_op jit(solution)/shard_map/ppermute | solution.py:778
  32.5 4.8 %collective-permute-done.3.refs_8_ = bf16[16,128]{1,0:T(8,128)(2,1)S(1)} collective-permute-done((bf16[16,128]{1,0:T(8,128)(2,1)S(1)}, bf16[16,128]{1,0:T(8,128)(2,1)S(1)}, u32[]{:S(2)}, u32[]{:S(2)}) %collective-permute-start.3) | collective-permute-done | bytes 4128 | tf_op jit(solution)/shard_map/ppermute | solution.py:778
  40.2 2.4 dynamic-slice_bitcast_fusion
  52.8 3.5 convolution_convert_fusion.2.refs_0_
  66.4 6.9 %collective-permute-done.12 = bf16[2,4,16,128]{3,2,1,0:T(8,128)(2,1)S(1)} collective-permute-done((bf16[2,4,16,128]{3,2,1,0:T(8,128)(2,1)S(1)}, bf16[2,4,16,128]{3,2,1,0:T(8,128)(2,1)S(1)}, u32[]{:S(2)}, u32[]{:S(2)}) %collective-permute-start.12) | collective-permute-done | bytes 32800 | tf_op jit(solution)/shard_map/ppermute | solution.py:774
  76.3 10.9 %collective-permute-done.17 = bf16[128,1536]{1,0:T(8,128)(2,1)S(1)} collective-permute-done((bf16[128,1536]{1,0:T(8,128)(2,1)S(1)}, bf16[128,1536]{1,0:T(8,128)(2,1)S(1)}, u32[]{:S(2)}, u32[]{:S(2)}) %collective-permute-start.17) | collective-permute-done | bytes 393248 | tf_op jit(solution)/shard_map/ppermute | solution.py:774
  92.7 2.5 collective-permute-start.22
  95.9 10.6 %project.1.refs_3_.refs_1_ = bf16[512,3072]{1,0:T(8,128)(2,1)} custom-call(bf16[512,1024]{1,0:T(8,128)(2,1)} %convolution_convert_fusion.2.refs_0_, bf16[512,1536]{1,0:T(8,128)(2,1)} %constant_dynamic-update-slice_fusion.4.refs_1_.refs_2_, bf16[512,1536]{1,0:T(8,128)(2,1)} %collective-permute-done.16.refs_2_.refs_3_, bf16[512,1536]{1,0:T(8,128)(2,1)} %copy-done.4, ...), custom_call_target="tpu_custom_call" | custom-call | tf_op jit(solution)/shard_map/project/pallas_call | solution.py:230
  115.4 9.5 %attend.2.refs_2_.refs_0_ = bf16[512,512]{1,0:T(8,128)(2,1)} custom-call(s32[2]{0:T(128)} %pad_add_fusion.refs_0_, bf16[512,3072]{1,0:T(8,128)(2,1)} %project.1.refs_3_.refs_1_, bf16[128,1024]{1,0:T(8,128)(2,1)} %get-tuple-element.228.refs_2_, bf16[128,1024]{1,0:T(8,128)(2,1)} %constant_dynamic-update-slice_fusion.17.refs_3_), custom_call_target="tpu_custom_call" | custom-call | tf_op jit(solution)/shard_map/attend/pallas_call | solution.py:230
  129.7 9.4 %attend.3.refs_1_ = bf16[512,512]{1,0:T(8,128)(2,1)} custom-call(s32[2]{0:T(128)} %pad_add_fusion.refs_0_, bf16[512,3072]{1,0:T(8,128)(2,1)} %project.1.refs_3_.refs_1_, bf16[512,1024]{1,0:T(8,128)(2,1)} %copy-done.2), custom_call_target="tpu_custom_call" | custom-call | tf_op jit(solution)/shard_map/attend/pallas_call | solution.py:230
  139.1 3.7 collective-permute-done.26.refs_7_
  144.0 7.9 %mix.1 = (f32[512,1024]{1,0:T(8,128)}, f32[512,128]{1,0:T(8,128)}, f32[512,1024]{1,0:T(8,128)}, bf16[512,1024]{1,0:T(8,128)(2,1)}, bf16[512,1024]{1,0:T(8,128)(2,1)}) custom-call(bf16[512,512]{1,0:T(8,128)(2,1)} %attend.2.refs_2_.refs_0_, bf16[512,512]{1,0:T(8,128)(2,1)} %attend.3.refs_1_, bf16[512,1024]{1,0:T(8,128)(2,1)} %pad_maximum_fusion.1.refs_2_, ...), custom_call_target="tpu_custom_call" | custom-call | tf_op jit(solution)/shard_map/mix/pallas_call | solution.py:230
  152.3 10.7 %up_gelu.2 = (bf16[512,2048]{1,0:T(8,128)(2,1)}, bf16[512,2048]{1,0:T(8,128)(2,1)}) custom-call(bf16[512,1024]{1,0:T(8,128)(2,1)} %get-tuple-element.246.refs_0_, bf16[1024,2048]{1,0:T(8,128)(2,1)} %all-gather.3.cloned.1.call-done.refs_1_, f32[1,2048]{1,0:T(1,128)} %bitcast.158), custom_call_target="tpu_custom_call" | custom-call | tf_op jit(solution)/shard_map/up_gelu/pallas_call | solution.py:230
  163.0 14.0 %collective-permute-done.27.refs_0_ = bf16[512,1024]{1,0:T(8,128)(2,1)S(1)} collective-permute-done((bf16[512,1024]{1,0:T(8,128)(2,1)}, bf16[512,1024]{1,0:T(8,128)(2,1)S(1)}, u32[]{:S(2)}, u32[]{:S(2)}) %collective-permute-start.27) | collective-permute-done | bytes 1048608 | tf_op jit(solution)/shard_map/ppermute | solution.py:774
  177.9 10.6 %up_gelu.3 = (bf16[512,2048]{1,0:T(8,128)(2,1)}, bf16[512,2048]{1,0:T(8,128)(2,1)}) custom-call(bf16[512,1024]{1,0:T(8,128)(2,1)} %copy-done.35, bf16[1024,2048]{1,0:T(8,128)(2,1)} %all-gather.3.cloned.1.call-done.refs_1_, f32[1,2048]{1,0:T(1,128)} %bitcast.159, bf16[512,2048]{1,0:T(8,128)(2,1)} %get-tuple-element.243.refs_3_.refs_0_), custom_call_target="tpu_custom_call" | custom-call | tf_op jit(solution)/shard_map/up_gelu/pallas_call | solution.py:230
  188.6 5.7 %matmul.2.refs_2_ = bf16[512,1024]{1,0:T(8,128)(2,1)} custom-call(bf16[512,2048]{1,0:T(8,128)(2,1)} %get-tuple-element.247.refs_0_, bf16[2048,1024]{1,0:T(8,128)(2,1)} %all-gather.5.cloned.1.call-done.refs_1_), custom_call_target="tpu_custom_call" | custom-call | tf_op jit(solution)/shard_map/matmul/pallas_call | solution.py:230
  197.2 5.7 %matmul.3.refs_0_ = f32[512,1024]{1,0:T(8,128)} custom-call(bf16[512,2048]{1,0:T(8,128)(2,1)} %get-tuple-element.243.refs_3_.refs_0_, bf16[2048,1024]{1,0:T(8,128)(2,1)} %all-gather.5.cloned.1.call-done.refs_1_, bf16[512,1024]{1,0:T(8,128)(2,1)} %matmul.2.refs_2_), custom_call_target="tpu_custom_call" | custom-call | tf_op jit(solution)/shard_map/matmul/pallas_call | solution.py:230
  203.0 15.5 %collective-permute-done.28.refs_1_ = bf16[512,1024]{1,0:T(8,128)(2,1)S(1)} collective-permute-done((bf16[512,1024]{1,0:T(8,128)(2,1)}, bf16[512,1024]{1,0:T(8,128)(2,1)S(1)}, u32[]{:S(2)}, u32[]{:S(2)}) %collective-permute-start.28) | collective-permute-done | bytes 1048608 | tf_op jit(solution)/shard_map/ppermute | solution.py:774
  219.5 6.6 %turn.1 = (bf16[512,1024]{1,0:T(8,128)(2,1)}, f32[512,1024]{1,0:T(8,128)}, bf16[512,1024]{1,0:T(8,128)(2,1)}, f32[8,1024]{1,0:T(8,128)}) custom-call(f32[512,1024]{1,0:T(8,128)} %matmul.3.refs_0_, bf16[512,1024]{1,0:T(8,128)(2,1)} %copy-done.30, f32[512,1024]{1,0:T(8,128)} %get-tuple-element.250.refs_2_, bf16[512,1024]{1,0:T(8,128)(2,1)} %pad_maximum_fusion.2.refs_3_, ...), custom_call_target="tpu_custom_call" | custom-call | tf_op jit(solution)/shard_map/turn/pallas_call | solution.py:230
  226.9 8.7 %down_grad.2 = (bf16[512,2048]{1,0:T(8,128)(2,1)}, f32[1,2048]{1,0:T(1,128)}) custom-call(bf16[512,1024]{1,0:T(8,128)(2,1)} %get-tuple-element.254.refs_0_, bf16[2048,1024]{1,0:T(8,128)(2,1)} %all-gather.5.cloned.1.call-done.refs_1_, bf16[512,2048]{1,0:T(8,128)(2,1)} %get-tuple-element.256.refs_2_), custom_call_target="tpu_custom_call" | custom-call | tf_op jit(solution)/shard_map/down_grad/pallas_call | solution.py:230
  235.6 13.8 %collective-permute-done.29.refs_0_ = bf16[512,1024]{1,0:T(8,128)(2,1)S(1)} collective-permute-done((bf16[512,1024]{1,0:T(8,128)(2,1)}, bf16[512,1024]{1,0:T(8,128)(2,1)S(1)}, u32[]{:S(2)}, u32[]{:S(2)}) %collective-permute-start.29) | collective-permute-done | bytes 1048608 | tf_op jit(solution)/shard_map/ppermute | solution.py:774
  250.3 9.2 %down_grad.3 = (bf16[512,2048]{1,0:T(8,128)(2,1)}, f32[1,2048]{1,0:T(1,128)}) custom-call(bf16[512,1024]{1,0:T(8,128)(2,1)} %copy-done.27, bf16[2048,1024]{1,0:T(8,128)(2,1)} %all-gather.5.cloned.1.call-done.refs_1_, bf16[512,2048]{1,0:T(8,128)(2,1)} %get-tuple-element.255.refs_2_, bf16[512,2048]{1,0:T(8,128)(2,1)} %get-tuple-element.257.refs_3_), custom_call_target="tpu_custom_call" | custom-call | tf_op jit(solution)/shard_map/down_grad/pallas_call | solution.py:230
  259.6 4.2 fusion.43
  263.8 4.7 %add_convert_fusion.refs_3_ = bf16[1024,2048]{1,0:T(8,128)(2,1)} fusion(f32[1024,2048]{1,0:T(8,128)S(1)} %fusion.43, bf16[512,1024]{1,0:T(8,128)(2,1)S(1)} %copy-done.25, bf16[512,2048]{1,0:T(8,128)(2,1)S(1)} %copy-done.17), kind=kOutput, calls=%fused_computation | convolution fusion | flops 2151677952 | bytes 15728640 | tf_op jit(solution)/shard_map/dot_general | solution.py:257
  275.4 7.0 %fusion.41.refs_0_ = f32[512,1024]{1,0:T(8,128)} fusion(bf16[512,2048]{1,0:T(8,128)(2,1)} %get-tuple-element.257.refs_3_, bf16[1024,2048]{1,0:T(8,128)(2,1)} %all-gather.3.cloned.1.call-done.refs_1_), kind=kOutput, calls=%fused_computation.181 | convolution fusion | flops 2147483648 | bytes 8388608 | tf_op jit(solution)/shard_map/dot_general | solution.py:257
  282.4 3.3 convolution_convert_fusion.4
  286.8 2.4 fusion.42
  289.3 4.6 %add_convert_fusion.1.refs_9_ = bf16[2048,1024]{1,0:T(8,128)(2,1)} fusion(f32[2048,1024]{1,0:T(8,128)S(1)} %fusion.42, bf16[512,2048]{1,0:T(8,128)(2,1)S(1)} %copy-done.3, bf16[512,1024]{1,0:T(8,128)(2,1)S(1)} %copy-done.26), kind=kOutput, calls=%fused_computation.1 | convolution fusion | flops 2151677952 | bytes 15728640 | tf_op jit(solution)/shard_map/dot_general | solution.py:257
  293.9 14.0 %collective-permute-done.31.refs_1_ = bf16[512,1024]{1,0:T(8,128)(2,1)S(1)} collective-permute-done((bf16[512,1024]{1,0:T(8,128)(2,1)}, bf16[512,1024]{1,0:T(8,128)(2,1)S(1)}, u32[]{:S(2)}, u32[]{:S(2)}) %collective-permute-start.31) | collective-permute-done | bytes 1048608 | tf_op jit(solution)/shard_map/ppermute | solution.py:774
  308.8 9.2 %unmix.1 = (f32[512,1024]{1,0:T(8,128)}, bf16[512,1024]{1,0:T(8,128)(2,1)}, bf16[512,1024]{1,0:T(8,128)(2,1)}, f32[8,1024]{1,0:T(8,128)}) custom-call(f32[512,1024]{1,0:T(8,128)} %fusion.41.refs_0_, bf16[512,1024]{1,0:T(8,128)(2,1)} %copy-done.37, f32[512,1024]{1,0:T(8,128)} %get-tuple-element.263.refs_2_, f32[512,1024]{1,0:T(8,128)} %get-tuple-element.264.refs_3_, ...), custom_call_target="tpu_custom_call" | custom-call | tf_op jit(solution)/shard_map/unmix/pallas_call | solution.py:230
  322.1 12.7 %attend_grad.2 = (bf16[512,1536]{1,0:T(8,128)(2,1)}, f32[1,1536]{1,0:T(1,128)}) custom-call(s32[2]{0:T(128)} %pad_add_fusion.refs_0_, bf16[512,3072]{1,0:T(8,128)(2,1)} %project.1.refs_3_.refs_1_, bf16[512,1024]{1,0:T(8,128)(2,1)} %get-tuple-element.271.refs_2_, bf16[1024,2048]{1,0:T(8,128)(2,1)} %add_convert_fusion.refs_3_, bf16[512,1024]{1,0:T(8,128)(2,1)} %copy-done.29), custom_call_target="tpu_custom_call" | custom-call | tf_op jit(solution)/shard_map/attend_grad/pallas_call | solution.py:230
  334.9 2.4 convolution_convert_fusion.1
  337.3 4.7 %weight_rows.1 = (bf16[128,1024]{1,0:T(8,128)(2,1)}, bf16[128,1024]{1,0:T(8,128)(2,1)}, bf16[128,1024]{1,0:T(8,128)(2,1)}, bf16[128,1024]{1,0:T(8,128)(2,1)}) custom-call(bf16[512,512]{1,0:T(8,128)(2,1)} %slice.206.refs_0_, bf16[512,1024]{1,0:T(8,128)(2,1)} %get-tuple-element.268.refs_1_, bf16[512,1024]{1,0:T(8,128)(2,1)} %collective-permute-done.32.refs_2_, ...), custom_call_target="tpu_custom_call" | custom-call | tf_op jit(solution)/shard_map/weight_rows/pallas_call | solution.py:230
  342.0 12.8 %attend_grad.3 = (bf16[512,1536]{1,0:T(8,128)(2,1)}, f32[1,1536]{1,0:T(1,128)}) custom-call(s32[2]{0:T(128)} %pad_add_fusion.refs_0_, bf16[512,3072]{1,0:T(8,128)(2,1)} %project.1.refs_3_.refs_1_, bf16[512,1024]{1,0:T(8,128)(2,1)} %get-tuple-element.271.refs_2_, bf16[128,1024]{1,0:T(8,128)(2,1)} %get-tuple-element.303.refs_3_), custom_call_target="tpu_custom_call" | custom-call | tf_op jit(solution)/shard_map/attend_grad/pallas_call | solution.py:230
  354.8 2.5 convolution_convert_fusion
  361.8 6.4 %collective-permute-done.48 = bf16[128,1024]{1,0:T(8,128)(2,1)S(1)} collective-permute-done((bf16[128,1024]{1,0:T(8,128)(2,1)}, bf16[128,1024]{1,0:T(8,128)(2,1)S(1)}, u32[]{:S(2)}, u32[]{:S(2)}) %collective-permute-start.48) | collective-permute-done | bytes 262176 | tf_op jit(solution)/shard_map/ppermute | solution.py:774
  376.9 7.4 %weight_cols.1 = (bf16[128,3072]{1,0:T(8,128)(2,1)}, bf16[128,3072]{1,0:T(8,128)(2,1)}, bf16[256,1536]{1,0:T(8,128)(2,1)}, bf16[256,1536]{1,0:T(8,128)(2,1)}) custom-call(bf16[512,512]{1,0:T(8,128)(2,1)} %slice.262.refs_0_, bf16[512,1536]{1,0:T(8,128)(2,1)} %get-tuple-element.275.refs_3_.refs_1_.refs_0_, ...), custom_call_target="tpu_custom_call" | custom-call | tf_op jit(solution)/shard_map/weight_cols/pallas_call | solution.py:230
  391.0 4.2 collective-permute-start.53
  396.7 2.3 collective-permute-done.44
  399.6 3.1 collective-permute-done.53
  402.7 3.4 collective-permute-start.46
  406.8 10.1 %stream_grad.1 = bf16[512,1024]{1,0:T(8,128)(2,1)} custom-call(bf16[512,1536]{1,0:T(8,128)(2,1)} %get-tuple-element.275.refs_3_.refs_1_.refs_0_, bf16[512,1536]{1,0:T(8,128)(2,1)} %get-tuple-element.285.refs_2_.refs_1_, bf16[512,1536]{1,0:T(8,128)(2,1)} %constant_dynamic-update-slice_fusion.4.refs_1_.refs_2_, ...), custom_call_target="tpu_custom_call" | custom-call | tf_op jit(solution)/shard_map/stream_grad/pallas_call | solution.py:230
  422.0 8.4 %collective-permute-done.37 = bf16[128,1536]{1,0:T(8,128)(2,1)S(1)} collective-permute-done((bf16[128,1536]{1,0:T(8,128)(2,1)S(1)}, bf16[128,1536]{1,0:T(8,128)(2,1)S(1)}, u32[]{:S(2)}, u32[]{:S(2)}) %collective-permute-start.37) | collective-permute-done | bytes 393248 | tf_op jit(solution)/shard_map/ppermute | solution.py:774
  430.6 2.2 collective-permute-start.41
  441.3 2.9 collective-permute-done.41
  444.2 2.1 collective-permute-done.40
  446.3 2.3 collective-permute-done.39
  (400 shorter events, 119.1 us)
Async XLA Ops:
  7.2 145.1 %all-gather.3.cloned.1.call-start = ((), (), s32[]{:S(2)}) async-start(), calls=%async_computation.2 | async-start | bytes 4456448 | tf_op jit(solution)/shard_map/all_gather | solution.py:876
  12.1 25.2 %collective-permute-start.4 = (bf16[64,1536]{1,0:T(8,128)(2,1)S(1)}, bf16[64,1536]{1,0:T(8,128)(2,1)S(1)}, u32[]{:S(2)}, u32[]{:S(2)}) collective-permute-start(bf16[64,1536]{1,0:T(8,128)(2,1)S(1)} %reshape.227), channel_id=1, source_target_pairs={{0,8},{2,10},{4,12},{6,14},{8,16},{10,18},{12,20},{14,22},{16,24},... | collective-permute-start | bytes 589832 | tf_op jit(solution)/shard_map/ppermute | solution.py:778
  13.7 23.6 %collective-permute-start.5 = (bf16[64,1536]{1,0:T(8,128)(2,1)S(1)}, bf16[64,1536]{1,0:T(8,128)(2,1)S(1)}, u32[]{:S(2)}, u32[]{:S(2)}) collective-permute-start(bf16[64,1536]{1,0:T(8,128)(2,1)S(1)} %reshape.227), channel_id=1, source_target_pairs={{0,16},{2,18},{4,20},{6,22},{8,24},{10,26},{12,28},{14,30},{16,0},... | collective-permute-start | bytes 589832 | tf_op jit(solution)/shard_map/ppermute | solution.py:778
  15.9 14.9 %collective-permute-start.1 = (bf16[16,128]{1,0:T(8,128)(2,1)S(1)}, bf16[16,128]{1,0:T(8,128)(2,1)S(1)}, u32[]{:S(2)}, u32[]{:S(2)}) collective-permute-start(bf16[16,128]{1,0:T(8,128)(2,1)S(1)} %concatenate.56), channel_id=1, source_target_pairs={{0,8},{2,10},{4,12},{6,14},{8,16},{10,18},{12,20},{14,22},{16,24},... | collective-permute-start | bytes 12296 | tf_op jit(solution)/shard_map/ppermute | solution.py:778
  16.7 14.0 %collective-permute-start.2 = (bf16[16,128]{1,0:T(8,128)(2,1)S(1)}, bf16[16,128]{1,0:T(8,128)(2,1)S(1)}, u32[]{:S(2)}, u32[]{:S(2)}) collective-permute-start(bf16[16,128]{1,0:T(8,128)(2,1)S(1)} %concatenate.56), channel_id=1, source_target_pairs={{0,16},{2,18},{4,20},{6,22},{8,24},{10,26},{12,28},{14,30},{16,0},... | collective-permute-start | bytes 12296 | tf_op jit(solution)/shard_map/ppermute | solution.py:778
  20.2 17.1 %collective-permute-start = (bf16[256,1024]{1,0:T(8,128)(2,1)S(1)}, bf16[256,1024]{1,0:T(8,128)(2,1)S(1)}, u32[]{:S(2)}, u32[]{:S(2)}) collective-permute-start(bf16[256,1024]{1,0:T(8,128)(2,1)S(1)} %get-tuple-element.160), channel_id=1, source_target_pairs={{0,1},{1,0},{2,3},{3,2},{4,5},{5,4},{6,7},{7,6},{8,9},{9,8},{10,11... | collective-permute-start | bytes 1572872 | tf_op jit(solution)/shard_map/ppermute | solution.py:774
  38.9 149.6 %all-gather.5.cloned.1.call-start = ((), (), s32[]{:S(2)}) async-start(), calls=%async_computation.3 | async-start | bytes 4456448 | tf_op jit(solution)/shard_map/all_gather | solution.py:877
  46.1 389.3 %reduce-scatter.3.cloned.1.call-start = ((), (), s32[]{:S(2)}) async-start(), calls=%async_computation.4 | async-start | bytes 4456448 | tf_op jit(solution)/shard_map/reduce_scatter | solution.py:968
  46.2 10.1 %collective-permute-start.7 = (bf16[128,1536]{1,0:T(8,128)(2,1)}, bf16[128,1536]{1,0:T(8,128)(2,1)S(1)}, u32[]{:S(2)}, u32[]{:S(2)}) collective-permute-start(bf16[128,1536]{1,0:T(8,128)(2,1)} %get-tuple-element.178), channel_id=1, source_target_pairs={{0,1},{1,0},{2,3},{3,2},{4,5},{5,4},{6,7},{7,6},{8,9},{9,8},{10,11... | collective-permute-start | bytes 1179656 | tf_op jit(solution)/shard_map/ppermute | solution.py:774
  47.7 11.8 %collective-permute-start.8 = (bf16[128,1536]{1,0:T(8,128)(2,1)S(1)}, bf16[128,1536]{1,0:T(8,128)(2,1)S(1)}, u32[]{:S(2)}, u32[]{:S(2)}) collective-permute-start(bf16[128,1536]{1,0:T(8,128)(2,1)S(1)} %constant_dynamic-update-slice_fusion), channel_id=1, source_target_pairs={{0,4},{2,6},{4,0},{6,2},{8,12},{10,14},{12,8},{14,10},{16,20},{18,... | collective-permute-start | bytes 1179656 | tf_op jit(solution)/shard_map/ppermute | solution.py:774
  49.3 12.4 %collective-permute-start.13 = (bf16[32,1024]{1,0:T(8,128)(2,1)}, bf16[32,1024]{1,0:T(8,128)(2,1)S(1)}, u32[]{:S(2)}, u32[]{:S(2)}) collective-permute-start(bf16[32,1024]{1,0:T(8,128)(2,1)} %param.18), channel_id=1, source_target_pairs={{0,8},{2,10},{4,12},{6,14},{8,16},{10,18},{12,20},{14,22},{16,24},... | collective-permute-start | bytes 196616 | tf_op jit(solution)/shard_map/ppermute | solution.py:778
  51.1 11.2 %collective-permute-start.14 = (bf16[32,1024]{1,0:T(8,128)(2,1)}, bf16[32,1024]{1,0:T(8,128)(2,1)S(1)}, u32[]{:S(2)}, u32[]{:S(2)}) collective-permute-start(bf16[32,1024]{1,0:T(8,128)(2,1)} %param.18), channel_id=1, source_target_pairs={{0,16},{2,18},{4,20},{6,22},{8,24},{10,26},{12,28},{14,30},{16,0},... | collective-permute-start | bytes 196616 | tf_op jit(solution)/shard_map/ppermute | solution.py:778
  52.2 8.8 %collective-permute-start.11 = (bf16[4,16,128]{2,1,0:T(8,128)(2,1)S(1)}, bf16[4,16,128]{2,1,0:T(8,128)(2,1)S(1)}, u32[]{:S(2)}, u32[]{:S(2)}) collective-permute-start(bf16[4,16,128]{2,1,0:T(8,128)(2,1)S(1)} %get-tuple-element.183), channel_id=1, source_target_pairs={{0,1},{1,0},{2,3},{3,2},{4,5},{5,4},{6,7},{7,6},{8,9},{9,8},{10,11... | collective-permute-start | bytes 49160 | tf_op jit(solution)/shard_map/ppermute | solution.py:774
  59.6 13.8 %collective-permute-start.9 = (bf16[128,1536]{1,0:T(8,128)(2,1)}, bf16[128,1536]{1,0:T(8,128)(2,1)S(1)}, u32[]{:S(2)}, u32[]{:S(2)}) collective-permute-start(bf16[128,1536]{1,0:T(8,128)(2,1)} %get-tuple-element.178), channel_id=1, source_target_pairs={{0,4},{2,6},{4,0},{6,2},{8,12},{10,14},{12,8},{14,10},{16,20},{18,... | collective-permute-start | bytes 1179656 | tf_op jit(solution)/shard_map/ppermute | solution.py:774
  61.1 12.2 %collective-permute-start.10 = (bf16[128,1536]{1,0:T(8,128)(2,1)S(1)}, bf16[128,1536]{1,0:T(8,128)(2,1)S(1)}, u32[]{:S(2)}, u32[]{:S(2)}) collective-permute-start(bf16[128,1536]{1,0:T(8,128)(2,1)S(1)} %constant_dynamic-update-slice_fusion), channel_id=1, source_target_pairs={{0,1},{1,0},{2,3},{3,2},{4,5},{5,4},{6,7},{7,6},{8,9},{9,8},{10,11... | collective-permute-start | bytes 1179656 | tf_op jit(solution)/shard_map/ppermute | solution.py:774
  61.7 11.6 %collective-permute-start.12 = (bf16[2,4,16,128]{3,2,1,0:T(8,128)(2,1)S(1)}, bf16[2,4,16,128]{3,2,1,0:T(8,128)(2,1)S(1)}, u32[]{:S(2)}, u32[]{:S(2)}) collective-permute-start(bf16[2,4,16,128]{3,2,1,0:T(8,128)(2,1)S(1)} %get-tuple-element.189), channel_id=1, source_target_pairs={{0,4},{2,6},{4,0},{6,2},{8,12},{10,14},{12,8},{14,10},{16,20},{18,... | collective-permute-start | bytes 98312 | tf_op jit(solution)/shard_map/ppermute | solution.py:774
  63.8 23.3 %collective-permute-start.17 = (bf16[128,1536]{1,0:T(8,128)(2,1)S(1)}, bf16[128,1536]{1,0:T(8,128)(2,1)S(1)}, u32[]{:S(2)}, u32[]{:S(2)}) collective-permute-start(bf16[128,1536]{1,0:T(8,128)(2,1)S(1)} %collective-permute-done.7), channel_id=1, source_target_pairs={{0,4},{2,6},{4,0},{6,2},{8,12},{10,14},{12,8},{14,10},{16,20},{18,... | collective-permute-start | bytes 1179656 | tf_op jit(solution)/shard_map/ppermute | solution.py:774
  64.3 22.9 %collective-permute-start.18 = (bf16[128,1536]{1,0:T(8,128)(2,1)S(1)}, bf16[128,1536]{1,0:T(8,128)(2,1)S(1)}, u32[]{:S(2)}, u32[]{:S(2)}) collective-permute-start(bf16[128,1536]{1,0:T(8,128)(2,1)S(1)} %collective-permute-done.8), channel_id=1, source_target_pairs={{0,1},{1,0},{2,3},{3,2},{4,5},{5,4},{6,7},{7,6},{8,9},{9,8},{10,11... | collective-permute-start | bytes 1179656 | tf_op jit(solution)/shard_map/ppermute | solution.py:774
  76.3 19.6 %collective-permute-start.16 = (bf16[512,1536]{1,0:T(8,128)(2,1)}, bf16[512,1536]{1,0:T(8,128)(2,1)}, u32[]{:S(2)}, u32[]{:S(2)}) collective-permute-start(bf16[512,1536]{1,0:T(8,128)(2,1)} %constant_dynamic-update-slice_fusion.4.refs_1_.refs_2_), channel_id=1, source_target_pairs={{0,2},{2,0},{4,6},{6,4},{8,10},{10,8},{12,14},{14,12},{16,18},{18,... | collective-permute-start | bytes 4718600 | tf_op jit(solution)/shard_map/ppermute | solution.py:774
  92.7 13.8 %collective-permute-start.21 = (bf16[64,1024]{1,0:T(8,128)(2,1)S(1)}, bf16[64,1024]{1,0:T(8,128)(2,1)S(1)}, u32[]{:S(2)}, u32[]{:S(2)}) collective-permute-start(bf16[64,1024]{1,0:T(8,128)(2,1)S(1)} %copy-done.53), channel_id=1, source_target_pairs={{0,1},{1,0},{2,3},{3,2},{4,5},{5,4},{6,7},{7,6},{8,9},{9,8},{10,11... | collective-permute-start | bytes 393224 | tf_op jit(solution)/shard_map/ppermute | solution.py:774
  92.7 13.8 %collective-permute-start.22 = (bf16[64,1024]{1,0:T(8,128)(2,1)S(1)}, bf16[64,1024]{1,0:T(8,128)(2,1)S(1)}, u32[]{:S(2)}, u32[]{:S(2)}) collective-permute-start(bf16[64,1024]{1,0:T(8,128)(2,1)S(1)} %pad_maximum_fusion.3), channel_id=1, source_target_pairs={{0,4},{2,6},{4,0},{6,2},{8,12},{10,14},{12,8},{14,10},{16,20},{18,... | collective-permute-start | bytes 393224 | tf_op jit(solution)/shard_map/ppermute | solution.py:774
  108.7 16.2 %collective-permute-start.23 = (bf16[128,1024]{1,0:T(8,128)(2,1)}, bf16[128,1024]{1,0:T(8,128)(2,1)S(1)}, u32[]{:S(2)}, u32[]{:S(2)}) collective-permute-start(bf16[128,1024]{1,0:T(8,128)(2,1)} %get-tuple-element.228.refs_2_), channel_id=1, source_target_pairs={{0,4},{2,6},{4,0},{6,2},{8,12},{10,14},{12,8},{14,10},{16,20},{18,... | collective-permute-start | bytes 786440 | tf_op jit(solution)/shard_map/ppermute | solution.py:774
  110.3 14.7 %collective-permute-start.24 = (bf16[128,1024]{1,0:T(8,128)(2,1)}, bf16[128,1024]{1,0:T(8,128)(2,1)S(1)}, u32[]{:S(2)}, u32[]{:S(2)}) collective-permute-start(bf16[128,1024]{1,0:T(8,128)(2,1)} %constant_dynamic-update-slice_fusion.17.refs_3_), channel_id=1, source_target_pairs={{0,1},{1,0},{2,3},{3,2},{4,5},{5,4},{6,7},{7,6},{8,9},{9,8},{10,11... | collective-permute-start | bytes 786440 | tf_op jit(solution)/shard_map/ppermute | solution.py:774
  128.4 14.4 %collective-permute-start.25 = (bf16[512,1024]{1,0:T(8,128)(2,1)S(1)}, bf16[512,1024]{1,0:T(8,128)(2,1)S(1)}, u32[]{:S(2)}, u32[]{:S(2)}) collective-permute-start(bf16[512,1024]{1,0:T(8,128)(2,1)S(1)} %constant_dynamic-update-slice_fusion.20.refs_2_.refs_3_.refs_5_), channel_id=1, source_target_pairs={{0,2},{2,0},{4,6},{6,4},{8,10},{10,8},{12,14},{14,12},{16,18},{18,... | collective-permute-start | bytes 3145736 | tf_op jit(solution)/shard_map/ppermute | solution.py:774
  128.5 14.3 %collective-permute-start.26 = (bf16[256,1024]{1,0:T(8,128)(2,1)S(1)}, bf16[256,1024]{1,0:T(8,128)(2,1)S(1)}, u32[]{:S(2)}, u32[]{:S(2)}) collective-permute-start(bf16[256,1024]{1,0:T(8,128)(2,1)S(1)} %copy-done.16), channel_id=1, source_target_pairs={{0,1},{1,0},{2,3},{3,2},{4,5},{5,4},{6,7},{7,6},{8,9},{9,8},{10,11... | collective-permute-start | bytes 1572872 | tf_op jit(solution)/shard_map/ppermute | solution.py:774
  151.9 25.1 %collective-permute-start.27 = (bf16[512,1024]{1,0:T(8,128)(2,1)}, bf16[512,1024]{1,0:T(8,128)(2,1)S(1)}, u32[]{:S(2)}, u32[]{:S(2)}) collective-permute-start(bf16[512,1024]{1,0:T(8,128)(2,1)} %get-tuple-element.246.refs_0_), channel_id=1, source_target_pairs={{0,1},{1,0},{2,3},{3,2},{4,5},{5,4},{6,7},{7,6},{8,9},{9,8},{10,11... | collective-permute-start | bytes 3145736 | tf_op jit(solution)/shard_map/ppermute | solution.py:774
  194.2 24.2 %collective-permute-start.28 = (bf16[512,1024]{1,0:T(8,128)(2,1)}, bf16[512,1024]{1,0:T(8,128)(2,1)S(1)}, u32[]{:S(2)}, u32[]{:S(2)}) collective-permute-start(bf16[512,1024]{1,0:T(8,128)(2,1)} %matmul.2.refs_2_), channel_id=1, source_target_pairs={{0,1},{1,0},{2,3},{3,2},{4,5},{5,4},{6,7},{7,6},{8,9},{9,8},{10,11... | collective-permute-start | bytes 3145736 | tf_op jit(solution)/shard_map/ppermute | solution.py:774
  226.1 23.3 %collective-permute-start.29 = (bf16[512,1024]{1,0:T(8,128)(2,1)}, bf16[512,1024]{1,0:T(8,128)(2,1)S(1)}, u32[]{:S(2)}, u32[]{:S(2)}) collective-permute-start(bf16[512,1024]{1,0:T(8,128)(2,1)} %get-tuple-element.254.refs_0_), channel_id=1, source_target_pairs={{0,1},{1,0},{2,3},{3,2},{4,5},{5,4},{6,7},{7,6},{8,9},{9,8},{10,11... | collective-permute-start | bytes 3145736 | tf_op jit(solution)/shard_map/ppermute | solution.py:774
  268.5 168.6 %reduce-scatter.5.cloned.1.call-start = ((), (), s32[]{:S(2)}) async-start(), calls=%async_computation.5 | async-start | bytes 4456448 | tf_op jit(solution)/shard_map/reduce_scatter | solution.py:962
  273.3 46.8 %collective-permute-start.30 = (bf16[256,1024]{1,0:T(8,128)(2,1)}, bf16[256,1024]{1,0:T(8,128)(2,1)S(1)}, u32[]{:S(2)}, u32[]{:S(2)}) collective-permute-start(bf16[256,1024]{1,0:T(8,128)(2,1)} %get-tuple-element.261), channel_id=1, source_target_pairs={{0,1},{1,0},{2,3},{3,2},{4,5},{5,4},{6,7},{7,6},{8,9},{9,8},{10,11... | collective-permute-start | bytes 1572872 | tf_op jit(solution)/shard_map/ppermute | solution.py:774
  285.8 22.1 %collective-permute-start.31 = (bf16[512,1024]{1,0:T(8,128)(2,1)}, bf16[512,1024]{1,0:T(8,128)(2,1)S(1)}, u32[]{:S(2)}, u32[]{:S(2)}) collective-permute-start(bf16[512,1024]{1,0:T(8,128)(2,1)} %convolution_convert_fusion.4), channel_id=1, source_target_pairs={{0,1},{1,0},{2,3},{3,2},{4,5},{5,4},{6,7},{7,6},{8,9},{9,8},{10,11... | collective-permute-start | bytes 3145736 | tf_op jit(solution)/shard_map/ppermute | solution.py:774
  320.0 14.9 %collective-permute-start.32 = (bf16[512,1024]{1,0:T(8,128)(2,1)S(1)}, bf16[512,1024]{1,0:T(8,128)(2,1)}, u32[]{:S(2)}, u32[]{:S(2)}) collective-permute-start(bf16[512,1024]{1,0:T(8,128)(2,1)S(1)} %convolution_convert_fusion.3.refs_4_), channel_id=1, source_target_pairs={{0,2},{2,0},{4,6},{6,4},{8,10},{10,8},{12,14},{14,12},{16,18},{18,... | collective-permute-start | bytes 3145736 | tf_op jit(solution)/shard_map/ppermute | solution.py:774
  357.7 19.1 %collective-permute-start.33 = (bf16[512,3072]{1,0:T(8,128)(2,1)S(1)}, bf16[512,3072]{1,0:T(8,128)(2,1)}, u32[]{:S(2)}, u32[]{:S(2)}) collective-permute-start(bf16[512,3072]{1,0:T(8,128)(2,1)S(1)} %pad_maximum_fusion), channel_id=1, source_target_pairs={{0,2},{2,0},{4,6},{6,4},{8,10},{10,8},{12,14},{14,12},{16,18},{18,... | collective-permute-start | bytes 9437192 | tf_op jit(solution)/shard_map/ppermute | solution.py:774
  361.4 8.7 %collective-permute-start.50 = (bf16[128,1024]{1,0:T(8,128)(2,1)}, bf16[128,1024]{1,0:T(8,128)(2,1)S(1)}, u32[]{:S(2)}, u32[]{:S(2)}) collective-permute-start(bf16[128,1024]{1,0:T(8,128)(2,1)} %get-tuple-element.305), channel_id=1, source_target_pairs={{0,1},{1,0},{2,3},{3,2},{4,5},{5,4},{6,7},{7,6},{8,9},{9,8},{10,11... | collective-permute-start | bytes 786440 | tf_op jit(solution)/shard_map/ppermute | solution.py:774
  389.0 10.0 %collective-permute-start.54 = (bf16[32,1024]{1,0:T(8,128)(2,1)S(1)}, bf16[32,1024]{1,0:T(8,128)(2,1)S(1)}, u32[]{:S(2)}, u32[]{:S(2)}) collective-permute-start(bf16[32,1024]{1,0:T(8,128)(2,1)S(1)} %get-tuple-element.335), channel_id=1, source_target_pairs={{0,8},{2,10},{4,12},{6,14},{8,16},{10,18},{12,20},{14,22},{16,24},... | collective-permute-start | bytes 196616 | tf_op jit(solution)/shard_map/ppermute | solution.py:929
  391.0 11.8 %collective-permute-start.53 = (bf16[32,1024]{1,0:T(8,128)(2,1)S(1)}, bf16[32,1024]{1,0:T(8,128)(2,1)S(1)}, u32[]{:S(2)}, u32[]{:S(2)}) collective-permute-start(bf16[32,1024]{1,0:T(8,128)(2,1)S(1)} %get-tuple-element.334), channel_id=1, source_target_pairs={{0,16},{2,18},{4,20},{6,22},{8,24},{10,26},{12,28},{14,30},{16,0},... | collective-permute-start | bytes 196616 | tf_op jit(solution)/shard_map/ppermute | solution.py:929
  395.4 10.8 %collective-permute-start.52 = (bf16[32,1024]{1,0:T(8,128)(2,1)S(1)}, bf16[32,1024]{1,0:T(8,128)(2,1)S(1)}, u32[]{:S(2)}, u32[]{:S(2)}) collective-permute-start(bf16[32,1024]{1,0:T(8,128)(2,1)S(1)} %slice.360), channel_id=1, source_target_pairs={{0,24},{2,26},{4,28},{6,30},{8,0},{10,2},{12,4},{14,6},{16,8},{18,... | collective-permute-start | bytes 196616 | tf_op jit(solution)/shard_map/ppermute | solution.py:929
  395.4 22.7 %collective-permute-start.34 = (bf16[128,3072]{1,0:T(8,128)(2,1)S(1)}, bf16[128,3072]{1,0:T(8,128)(2,1)S(1)}, u32[]{:S(2)}, u32[]{:S(2)}) collective-permute-start(bf16[128,3072]{1,0:T(8,128)(2,1)S(1)} %copy-done.11), channel_id=1, source_target_pairs={{0,4},{2,6},{4,0},{6,2},{8,12},{10,14},{12,8},{14,10},{16,20},{18,... | collective-permute-start | bytes 2359304 | tf_op jit(solution)/shard_map/ppermute | solution.py:774
  399.0 19.2 %collective-permute-start.35 = (bf16[256,1536]{1,0:T(8,128)(2,1)S(1)}, bf16[256,1536]{1,0:T(8,128)(2,1)S(1)}, u32[]{:S(2)}, u32[]{:S(2)}) collective-permute-start(bf16[256,1536]{1,0:T(8,128)(2,1)S(1)} %copy-done.72), channel_id=1, source_target_pairs={{0,1},{1,0},{2,3},{3,2},{4,5},{5,4},{6,7},{7,6},{8,9},{9,8},{10,11... | collective-permute-start | bytes 2359304 | tf_op jit(solution)/shard_map/ppermute | solution.py:774
  399.0 17.9 %collective-permute-start.47 = (bf16[1,16,128]{2,1,0:T(8,128)(2,1)S(1)}, bf16[1,16,128]{2,1,0:T(8,128)(2,1)S(1)}, u32[]{:S(2)}, u32[]{:S(2)}) collective-permute-start(bf16[1,16,128]{2,1,0:T(8,128)(2,1)S(1)} %get-tuple-element.349), channel_id=1, source_target_pairs={{0,8},{2,10},{4,12},{6,14},{8,16},{10,18},{12,20},{14,22},{16,24},... | collective-permute-start | bytes 12296 | tf_op jit(solution)/shard_map/ppermute | solution.py:929
  402.7 14.2 %collective-permute-start.46 = (bf16[1,16,128]{2,1,0:T(8,128)(2,1)S(1)}, bf16[1,16,128]{2,1,0:T(8,128)(2,1)S(1)}, u32[]{:S(2)}, u32[]{:S(2)}) collective-permute-start(bf16[1,16,128]{2,1,0:T(8,128)(2,1)S(1)} %get-tuple-element.350), channel_id=1, source_target_pairs={{0,16},{2,18},{4,20},{6,22},{8,24},{10,26},{12,28},{14,30},{16,0},... | collective-permute-start | bytes 12296 | tf_op jit(solution)/shard_map/ppermute | solution.py:929
  406.1 10.9 %collective-permute-start.45 = (bf16[1,16,128]{2,1,0:T(8,128)(2,1)S(1)}, bf16[1,16,128]{2,1,0:T(8,128)(2,1)S(1)}, u32[]{:S(2)}, u32[]{:S(2)}) collective-permute-start(bf16[1,16,128]{2,1,0:T(8,128)(2,1)S(1)} %get-tuple-element.348), channel_id=1, source_target_pairs={{0,24},{2,26},{4,28},{6,30},{8,0},{10,2},{12,4},{14,6},{16,8},{18,... | collective-permute-start | bytes 12296 | tf_op jit(solution)/shard_map/ppermute | solution.py:929
  418.3 12.1 %collective-permute-start.37 = (bf16[128,1536]{1,0:T(8,128)(2,1)S(1)}, bf16[128,1536]{1,0:T(8,128)(2,1)S(1)}, u32[]{:S(2)}, u32[]{:S(2)}) collective-permute-start(bf16[128,1536]{1,0:T(8,128)(2,1)S(1)} %add_convert_fusion.4), channel_id=1, source_target_pairs={{0,1},{1,0},{2,3},{3,2},{4,5},{5,4},{6,7},{7,6},{8,9},{9,8},{10,11... | collective-permute-start | bytes 1179656 | tf_op jit(solution)/shard_map/ppermute | solution.py:774
  420.1 10.3 %collective-permute-start.38 = (bf16[128,1536]{1,0:T(8,128)(2,1)S(1)}, bf16[128,1536]{1,0:T(8,128)(2,1)S(1)}, u32[]{:S(2)}, u32[]{:S(2)}) collective-permute-start(bf16[128,1536]{1,0:T(8,128)(2,1)S(1)} %add_convert_fusion.3), channel_id=1, source_target_pairs={{0,4},{2,6},{4,0},{6,2},{8,12},{10,14},{12,8},{14,10},{16,20},{18,... | collective-permute-start | bytes 1179656 | tf_op jit(solution)/shard_map/ppermute | solution.py:774
  421.2 18.9 %collective-permute-start.36 = (bf16[256,1024]{1,0:T(8,128)(2,1)S(1)}, bf16[256,1024]{1,0:T(8,128)(2,1)S(1)}, u32[]{:S(2)}, u32[]{:S(2)}) collective-permute-start(bf16[256,1024]{1,0:T(8,128)(2,1)S(1)} %get-tuple-element.321), channel_id=1, source_target_pairs={{0,1},{1,0},{2,3},{3,2},{4,5},{5,4},{6,7},{7,6},{8,9},{9,8},{10,11... | collective-permute-start | bytes 1572872 | tf_op jit(solution)/shard_map/ppermute | solution.py:774
  430.6 13.6 %collective-permute-start.41 = (bf16[64,1536]{1,0:T(8,128)(2,1)S(1)}, bf16[64,1536]{1,0:T(8,128)(2,1)S(1)}, u32[]{:S(2)}, u32[]{:S(2)}) collective-permute-start(bf16[64,1536]{1,0:T(8,128)(2,1)S(1)} %get-tuple-element.329), channel_id=1, source_target_pairs={{0,8},{2,10},{4,12},{6,14},{8,16},{10,18},{12,20},{14,22},{16,24},... | collective-permute-start | bytes 589832 | tf_op jit(solution)/shard_map/ppermute | solution.py:929
  432.8 13.5 %collective-permute-start.40 = (bf16[64,1536]{1,0:T(8,128)(2,1)S(1)}, bf16[64,1536]{1,0:T(8,128)(2,1)S(1)}, u32[]{:S(2)}, u32[]{:S(2)}) collective-permute-start(bf16[64,1536]{1,0:T(8,128)(2,1)S(1)} %get-tuple-element.328), channel_id=1, source_target_pairs={{0,16},{2,18},{4,20},{6,22},{8,24},{10,26},{12,28},{14,30},{16,0},... | collective-permute-start | bytes 589832 | tf_op jit(solution)/shard_map/ppermute | solution.py:929
  434.8 13.7 %collective-permute-start.39 = (bf16[64,1536]{1,0:T(8,128)(2,1)S(1)}, bf16[64,1536]{1,0:T(8,128)(2,1)S(1)}, u32[]{:S(2)}, u32[]{:S(2)}) collective-permute-start(bf16[64,1536]{1,0:T(8,128)(2,1)S(1)} %slice.359), channel_id=1, source_target_pairs={{0,24},{2,26},{4,28},{6,30},{8,0},{10,2},{12,4},{14,6},{16,8},{18,... | collective-permute-start | bytes 589832 | tf_op jit(solution)/shard_map/ppermute | solution.py:929
  (87 other events, 530.9 us)
Sparse Core Ops, SparseCore 0:
  39.0 59.8 all-gather.2
  101.1 52.6 all-gather.4
  268.6 71.3 reduce-scatter.2
  344.2 81.2 reduce-scatter.4
